TPU v7x, 128 devices: a whole 4x4x4 slice. The times are simulated.
128 devices in a mesh: dp: 4 (over y), ep: 32 (over x, z, core).
Axes of the slice: x: 4, y: 4, z: 4, core: 2. Of those that a mesh axis runs over, the one named last changes fastest.
Arguments:
- query_plain: bfloat16 [4, 512, 8192], P(None, 'dp', 'ep'), may hold values from -6 to 6
- query_rotary: bfloat16 [4, 512, 4096], P(None, 'dp', 'ep'), may hold values from -6 to 6
- key_up: bfloat16 [64, 128, 512], P('ep'), may hold values from -0.5 to 0.5
- value_up: bfloat16 [64, 512, 128], P('ep'), may hold values from -0.25 to 0.25
- output_weight: bfloat16 [8192, 3584], P('ep'), may hold values from -0.0625 to 0.0625
- cache_latent: bfloat16 [512, 64, 512], P(('dp', 'ep')), may hold values from -6 to 6
- cache_rotary: bfloat16 [512, 64, 64], P(('dp', 'ep')), may hold values from -18 to 18
- lengths: int32 [512], P(('dp', 'ep')), may hold values from 2 to 64, as said below
- new_latent: bfloat16 [4, 512, 512], P(None, ('dp', 'ep')), may hold values from -6 to 6
- new_rotary: bfloat16 [4, 512, 64], P(None, ('dp', 'ep')), may hold values from -6 to 6
- residual: bfloat16 [4, 512, 3584], P(None, ('dp', 'ep')), may hold values from -1.5 to 1.5
- norm_gain: float32 [3584], replicated, may hold values from 0.5 to 1.5
- expert_ids: int32 [4, 512, 8], P(None, ('dp', 'ep')), may hold values from 0 to 127, all different within a row; in each aligned block of 4 rows (0 to 3, 4 to 7, ..., all dimensions but the last counted through in order) at most 2 rows name the same one
- gate_weights: float32 [4, 512, 8], P(None, ('dp', 'ep')), may hold values from 0.05 to 0.5
- expert_gate: bfloat16 [128, 3584, 1024], P(('dp', 'ep')), may hold values from -0.09375 to 0.09375
- expert_up: bfloat16 [128, 3584, 1024], P(('dp', 'ep')), may hold values from -0.09375 to 0.09375
- expert_down: bfloat16 [128, 1024, 3584], P(('dp', 'ep')), may hold values from -0.1875 to 0.1875
Outputs:
- layer_out: bfloat16 [4, 512, 3584], P(None, ('dp', 'ep'))
Inputs may be any that keep to these rules, and one draw needn't show every extreme that they name: `expert_ids`: in each aligned block of 4 rows of one step no expert is named by more than 2 rows, a bound that some block reaches. `lengths`: some row has exactly 64 live positions.
All inputs are finite; a program needn't handle non-finite values.
Results may differ from a plain program's by a relative error of at most 0.025.
Values may be sent and summed in bfloat16 or wider, within the bound.
No kernel may reach another device: no remote copies, remote signals or barrier semaphores. Data moves between devices by JAX's collectives and lax.ppermute only.
A program may use at most 128 MiB of HBM per device.

v0:
```python
import jax
import jax.numpy as jnp
from jax import lax
from jax.sharding import PartitionSpec as P

D = 3584
HEADS = 64
LAT = 512
ROPE = 64
NOPE = 128
VHEAD = 128
MOST = 2
STEPS = 4
EXPERTS = 128
LMAX = 64


def feed_forward(received, expert_gate, expert_up, expert_down):
    gate = jnp.einsum(
        "...emd,edh->...emh", received, expert_gate, preferred_element_type=jnp.float32
    )
    upward = jnp.einsum(
        "...emd,edh->...emh", received, expert_up, preferred_element_type=jnp.float32
    )
    hidden = (jax.nn.silu(gate) * upward).astype(jnp.bfloat16)
    result = jnp.einsum(
        "...emh,ehd->...emd", hidden, expert_down, preferred_element_type=jnp.float32
    )
    return result.astype(jnp.bfloat16)


def per_device(
    query_plain,
    query_rotary,
    key_up,
    value_up,
    output_weight,
    cache_latent,
    cache_rotary,
    lengths,
    new_latent,
    new_rotary,
    residual,
    norm_gain,
    expert_ids,
    gate_weights,
    expert_gate,
    expert_up,
    expert_down,
):
    head_local = key_up.shape[0]
    group_rows = query_plain.shape[1]
    local_rows = cache_latent.shape[0]
    local_experts = expert_gate.shape[0]
    data_groups = lax.axis_size("dp")
    expert_ranks = lax.axis_size("ep")
    devices = data_groups * expert_ranks
    slot_count = EXPERTS * MOST
    scale = 1.0 / (NOPE + ROPE) ** 0.5
    fresh_latent = jnp.swapaxes(new_latent, 0, 1)
    fresh_rotary = jnp.swapaxes(new_rotary, 0, 1)
    visible = jnp.arange(LMAX, dtype=jnp.int32)[None, :] < lengths[:, None]
    sections = jnp.arange(STEPS, dtype=jnp.int32)
    catalog = jnp.arange(EXPERTS, dtype=jnp.int32)
    slot_index = jnp.arange(slot_count, dtype=jnp.int32)
    results = []
    for current in range(STEPS):
        plain = query_plain[current].reshape(group_rows, head_local, NOPE)
        absorbed = jnp.einsum(
            "rhn,hnl->rhl", plain, key_up, preferred_element_type=jnp.float32
        ).astype(jnp.bfloat16)
        absorbed, rotary = (
            lax.all_to_all(
                absorbed.reshape(group_rows, head_local * LAT),
                "ep",
                split_axis=0,
                concat_axis=1,
                tiled=True,
            ),
            lax.all_to_all(query_rotary[current], "ep", split_axis=0, concat_axis=1, tiled=True),
        )
        absorbed = absorbed.reshape(local_rows, HEADS, LAT)
        rotary = rotary.reshape(local_rows, HEADS, ROPE)
        cached = jnp.einsum(
            "rhl,rpl->rhp", absorbed, cache_latent, preferred_element_type=jnp.float32
        )
        cached = (
            cached
            + jnp.einsum("rhe,rep->rhp", rotary, cache_rotary, preferred_element_type=jnp.float32)
        ) * scale
        fresh = jnp.einsum(
            "rhl,rjl->rhj", absorbed, fresh_latent, preferred_element_type=jnp.float32
        )
        fresh = (
            fresh
            + jnp.einsum("rhe,rje->rhj", rotary, fresh_rotary, preferred_element_type=jnp.float32)
        ) * scale
        cached = jnp.where(visible[:, None, :], cached, -jnp.inf)
        fresh = jnp.where((sections <= current)[None, None, :], fresh, -jnp.inf)
        peak = jnp.maximum(jnp.max(cached, axis=-1), jnp.max(fresh, axis=-1))[..., None]
        cached_exp = jnp.exp(cached - peak)
        fresh_exp = jnp.exp(fresh - peak)
        total = jnp.sum(cached_exp, axis=-1, keepdims=True) + jnp.sum(
            fresh_exp, axis=-1, keepdims=True
        )
        cached_prob = (cached_exp / total).astype(jnp.bfloat16)
        fresh_prob = (fresh_exp / total).astype(jnp.bfloat16)
        mixed = jnp.einsum(
            "rhp,rpl->rhl", cached_prob, cache_latent, preferred_element_type=jnp.float32
        )
        mixed = mixed + jnp.einsum(
            "rhj,rjl->rhl", fresh_prob, fresh_latent, preferred_element_type=jnp.float32
        )
        mixed = mixed.astype(jnp.bfloat16).reshape(local_rows, HEADS * LAT)
        mixed = lax.all_to_all(mixed, "ep", split_axis=1, concat_axis=0, tiled=True)
        values = jnp.einsum(
            "rhl,hlv->rhv",
            mixed.reshape(group_rows, head_local, LAT),
            value_up,
            preferred_element_type=jnp.float32,
        )
        values = values.astype(jnp.bfloat16).reshape(group_rows, head_local * VHEAD)

        def project(start, count, values=values):
            return jnp.dot(values, output_weight, preferred_element_type=jnp.float32)

        attention = lax.psum_scatter(
            project(jnp.int32(0), local_rows * lax.axis_size("ep")).astype(jnp.bfloat16),
            "ep",
            scatter_dimension=0,
            tiled=True,
        ).astype(jnp.float32)
        hidden = residual[current].astype(jnp.float32) + attention
        normed = (
            hidden
            * lax.rsqrt(jnp.mean(hidden * hidden, axis=-1, keepdims=True) + 1e-06)
            * norm_gain
        ).astype(jnp.bfloat16)
        chosen = expert_ids[current]
        hits = (chosen[:, :, None] == catalog[None, None, :]).astype(jnp.int32)
        row_hits = jnp.sum(hits, axis=1)
        before = jnp.cumsum(row_hits, axis=0) - row_hits
        rank = jnp.sum(hits * before[:, None, :], axis=-1)
        target = chosen * MOST + rank
        placed = jnp.any(target[:, :, None] == slot_index[None, None, :], axis=1).astype(
            jnp.bfloat16
        )
        outbound = lax.dot_general(
            placed, normed, (((0,), (0,)), ((), ())), preferred_element_type=jnp.float32
        )
        outbound = outbound.astype(jnp.bfloat16).reshape(devices, local_experts, MOST, D)
        finished = feed_forward(
            lax.all_to_all(outbound, ("dp", "ep"), split_axis=0, concat_axis=0, tiled=True),
            expert_gate,
            expert_up,
            expert_down,
        )
        returned = lax.all_to_all(finished, ("dp", "ep"), split_axis=0, concat_axis=0, tiled=True)
        picked = returned.reshape(slot_count, D)[target]
        routed = jnp.sum(gate_weights[current][:, :, None] * picked.astype(jnp.float32), axis=1)
        results.append((hidden + routed).astype(jnp.bfloat16))
    return jnp.stack(results)


def solution(mesh):
    return jax.shard_map(
        per_device,
        mesh=mesh,
        in_specs=(
            P(None, "dp", "ep"),
            P(None, "dp", "ep"),
            P("ep", None, None),
            P("ep", None, None),
            P("ep", None),
            P(("dp", "ep"), None, None),
            P(("dp", "ep"), None, None),
            P(("dp", "ep")),
            P(None, ("dp", "ep"), None),
            P(None, ("dp", "ep"), None),
            P(None, ("dp", "ep"), None),
            P(),
            P(None, ("dp", "ep"), None),
            P(None, ("dp", "ep"), None),
            P(("dp", "ep"), None, None),
            P(("dp", "ep"), None, None),
            P(("dp", "ep"), None, None),
        ),
        out_specs=P(None, ("dp", "ep"), None),
        check_vma=False,
    )
```

profile of v0, /device:TPU:0, one launch (start us, length us, event | category | flops | bytes accessed | tf_op | source)
XLA Modules:
  0.0 567.6 jit_solution(15051974086535044349)
XLA Ops:
  8.1 8.2 %all-to-all-start.11 = ((bf16[32,4,128]{2,1,0:T(4,128)(2,1)}), bf16[32,4,128]{2,1,0:T(4,128)(2,1)S(1)}, u32[]{:S(2)}, u32[]{:S(2)}) async-start(bf16[32,4,128]{2,1,0:T(4,128)(2,1)} %bitcast.70), calls=%async_computation.11 | async-start | bytes 65536 | tf_op jit(solution)/shard_map/all_to_all | solution.py:80
  23.8 6.3 %all-to-all-start.16 = ((bf16[32,4,128]{2,1,0:T(4,128)(2,1)}), bf16[32,4,128]{2,1,0:T(4,128)(2,1)S(1)}, u32[]{:S(2)}, u32[]{:S(2)}) async-start(bf16[32,4,128]{2,1,0:T(4,128)(2,1)} %bitcast.99), calls=%async_computation.16 | async-start | bytes 65536 | tf_op jit(solution)/shard_map/all_to_all | solution.py:80
  42.9 7.1 %all-to-all-done.6 = bf16[32,4,128]{2,1,0:T(4,128)(2,1)S(1)} async-done(((bf16[32,4,128]{2,1,0:T(4,128)(2,1)}), bf16[32,4,128]{2,1,0:T(4,128)(2,1)S(1)}, u32[]{:S(2)}, u32[]{:S(2)}) %all-to-all-start.6) | async-done | bytes 32800 | tf_op jit(solution)/shard_map/all_to_all | solution.py:80
  54.9 6.5 %all-to-all-done.1 = bf16[32,4,128]{2,1,0:T(4,128)(2,1)S(1)} async-done(((bf16[32,4,128]{2,1,0:T(4,128)(2,1)}), bf16[32,4,128]{2,1,0:T(4,128)(2,1)S(1)}, u32[]{:S(2)}, u32[]{:S(2)}) %all-to-all-start.1) | async-done | bytes 32800 | tf_op jit(solution)/shard_map/all_to_all | solution.py:80
  67.1 7.1 %all-to-all-done.10 = bf16[32,4,1024]{2,1,0:T(4,128)(2,1)S(1)} async-done(((bf16[32,4,1024]{2,1,0:T(4,128)(2,1)}), bf16[32,4,1024]{2,1,0:T(4,128)(2,1)S(1)}, u32[]{:S(2)}, u32[]{:S(2)}) %all-to-all-start.10) | async-done | bytes 262176 | tf_op jit(solution)/shard_map/all_to_all | solution.py:73
  80.7 6.4 %all-to-all-done.15 = bf16[32,4,1024]{2,1,0:T(4,128)(2,1)S(1)} async-done(((bf16[32,4,1024]{2,1,0:T(4,128)(2,1)}), bf16[32,4,1024]{2,1,0:T(4,128)(2,1)S(1)}, u32[]{:S(2)}, u32[]{:S(2)}) %all-to-all-start.15) | async-done | bytes 262176 | tf_op jit(solution)/shard_map/all_to_all | solution.py:73
  159.8 7.1 %all-to-all-done.2 = bf16[4,32,1024]{2,0,1:T(4,128)(2,1)S(1)} async-done(((bf16[4,32,1024]{2,0,1:T(4,128)(2,1)}), bf16[4,32,1024]{2,0,1:T(4,128)(2,1)S(1)}, u32[]{:S(2)}, u32[]{:S(2)}) %all-to-all-start.2) | async-done | bytes 262176 | tf_op jit(solution)/shard_map/all_to_all | solution.py:115
  171.9 106.1 %all-reduce.7.cloned.1.call-done = (bf16[128,3584]{1,0:T(8,128)(2,1)}, bf16[128,3584]{1,0:T(8,128)(2,1)}, bf16[128,3584]{1,0:T(8,128)(2,1)}, bf16[128,3584]{1,0:T(8,128)(2,1)}) async-done(((bf16[128,3584]{1,0:T(8,128)(2,1)}, bf16[128,3584]{1,0:T(8,128)(2,1)}, bf16[128,3584]{1,0:T(8,128)(2,1)}, bf16[128,3584]{1,0:T(8,128)(2,1)}), (bf16[128,3584]{1,0:T(8,128)(2,1)}, bf16[128,3584]{1,0:T(8,128)(2,1)}, ...) | async-done | bytes 3670032
  282.3 8.6 %all-to-all-start.18 = ((bf16[128,1,2,3584]{3,2,1,0:T(2,128)(2,1)}), bf16[128,1,2,3584]{3,2,1,0:T(2,128)(2,1)}, u32[]{:S(2)}, u32[]{:S(2)}) async-start(bf16[128,1,2,3584]{3,2,1,0:T(2,128)(2,1)} %bitcast.106), calls=%async_computation.18 | async-start | bytes 3670016 | tf_op jit(solution)/shard_map/all_to_all | solution.py:153
  294.2 24.0 %all-to-all-done.18 = bf16[128,1,2,3584]{3,2,1,0:T(2,128)(2,1)} async-done(((bf16[128,1,2,3584]{3,2,1,0:T(2,128)(2,1)}), bf16[128,1,2,3584]{3,2,1,0:T(2,128)(2,1)}, u32[]{:S(2)}, u32[]{:S(2)}) %all-to-all-start.18) | async-done | bytes 1835040 | tf_op jit(solution)/shard_map/all_to_all | solution.py:153
  327.3 24.0 %all-to-all-done.13 = bf16[128,1,2,3584]{3,2,1,0:T(2,128)(2,1)} async-done(((bf16[128,1,2,3584]{3,2,1,0:T(2,128)(2,1)}), bf16[128,1,2,3584]{3,2,1,0:T(2,128)(2,1)}, u32[]{:S(2)}, u32[]{:S(2)}) %all-to-all-start.13) | async-done | bytes 1835040 | tf_op jit(solution)/shard_map/all_to_all | solution.py:153
  360.2 24.0 %all-to-all-done.8 = bf16[128,1,2,3584]{3,2,1,0:T(2,128)(2,1)} async-done(((bf16[128,1,2,3584]{3,2,1,0:T(2,128)(2,1)}), bf16[128,1,2,3584]{3,2,1,0:T(2,128)(2,1)}, u32[]{:S(2)}, u32[]{:S(2)}) %all-to-all-start.8) | async-done | bytes 1835040 | tf_op jit(solution)/shard_map/all_to_all | solution.py:153
  389.3 5.8 %fusion.79 = f32[128,1,2,1024]{3,0,2,1:T(8,128)S(1)} fusion(bf16[1,3584,1024]{2,1,0:T(8,128)(2,1)} %param.31, bf16[128,1,2,3584]{3,2,1,0:T(2,128)(2,1)} %all-to-all-done.18), kind=kOutput, calls=%fused_computation.63 | convolution fusion | flops 1879048192 | bytes 10223616 | tf_op jit(solution)/shard_map/...emd,edh->...emh/dot_general | solution.py:19
  395.2 6.0 %fusion.159 = bf16[128,2,1024]{2,0,1:T(8,128)(2,1)S(1)} fusion(bf16[1,3584,1024]{2,1,0:T(8,128)(2,1)} %param.32, bf16[128,1,2,3584]{3,2,1,0:T(2,128)(2,1)} %all-to-all-done.18, f32[128,1,2,1024]{3,0,2,1:T(8,128)S(1)} %fusion.79), kind=kOutput, calls=%fused_computation.79 | convolution fusion | flops 1880621056 | bytes 10747904 | tf_op jit(solution)/shard_map/...emd,edh->...emh/dot_general | solution.py:22
  406.5 10.5 %all-to-all-done.3 = bf16[128,1,2,3584]{3,2,1,0:T(2,128)(2,1)S(1)} async-done(((bf16[128,1,2,3584]{3,2,1,0:T(2,128)(2,1)}), bf16[128,1,2,3584]{3,2,1,0:T(2,128)(2,1)S(1)}, u32[]{:S(2)}, u32[]{:S(2)}) %all-to-all-start.3) | async-done | bytes 1835040 | tf_op jit(solution)/shard_map/all_to_all | solution.py:153
  428.9 6.0 %fusion.154 = bf16[128,2,1024]{2,0,1:T(8,128)(2,1)S(1)} fusion(bf16[1,3584,1024]{2,1,0:T(8,128)(2,1)} %param.32, bf16[128,1,2,3584]{3,2,1,0:T(2,128)(2,1)} %all-to-all-done.13, f32[128,1,2,1024]{3,0,2,1:T(8,128)S(1)} %fusion.74), kind=kOutput, calls=%fused_computation.78 | convolution fusion | flops 1880621056 | bytes 10747904 | tf_op jit(solution)/shard_map/...emd,edh->...emh/dot_general | solution.py:22
  440.2 10.5 %all-to-all-done.19 = bf16[128,1,2,3584]{3,2,1,0:T(2,128)(2,1)S(1)} async-done(((bf16[128,1,2,3584]{3,2,1,0:T(2,128)(2,1)}), bf16[128,1,2,3584]{3,2,1,0:T(2,128)(2,1)S(1)}, u32[]{:S(2)}, u32[]{:S(2)}) %all-to-all-start.19) | async-done | bytes 1835040 | tf_op jit(solution)/shard_map/all_to_all | solution.py:158
  450.7 5.9 %all-to-all-start.14 = ((bf16[128,1,2,3584]{3,2,1,0:T(2,128)(2,1)}), bf16[128,1,2,3584]{3,2,1,0:T(2,128)(2,1)}, u32[]{:S(2)}, u32[]{:S(2)}) async-start(bf16[128,1,2,3584]{3,2,1,0:T(2,128)(2,1)} %copy.240), calls=%async_computation.14 | async-start | bytes 3670016 | tf_op jit(solution)/shard_map/all_to_all | solution.py:158
  462.5 6.0 %fusion.149 = bf16[128,2,1024]{2,0,1:T(8,128)(2,1)S(1)} fusion(bf16[1,3584,1024]{2,1,0:T(8,128)(2,1)} %param.32, bf16[128,1,2,3584]{3,2,1,0:T(2,128)(2,1)} %all-to-all-done.8, f32[128,1,2,1024]{3,0,2,1:T(8,128)S(1)} %fusion.69), kind=kOutput, calls=%fused_computation.77 | convolution fusion | flops 1880621056 | bytes 10747904 | tf_op jit(solution)/shard_map/...emd,edh->...emh/dot_general | solution.py:22
  473.8 10.1 %all-to-all-done.14 = bf16[128,1,2,3584]{3,2,1,0:T(2,128)(2,1)} async-done(((bf16[128,1,2,3584]{3,2,1,0:T(2,128)(2,1)}), bf16[128,1,2,3584]{3,2,1,0:T(2,128)(2,1)}, u32[]{:S(2)}, u32[]{:S(2)}) %all-to-all-start.14) | async-done | bytes 1835040 | tf_op jit(solution)/shard_map/all_to_all | solution.py:158
  483.9 6.0 %all-to-all-start.9 = ((bf16[128,1,2,3584]{3,2,1,0:T(2,128)(2,1)}), bf16[128,1,2,3584]{3,2,1,0:T(2,128)(2,1)}, u32[]{:S(2)}, u32[]{:S(2)}) async-start(bf16[128,1,2,3584]{3,2,1,0:T(2,128)(2,1)} %copy.223), calls=%async_computation.9 | async-start | bytes 3670016 | tf_op jit(solution)/shard_map/all_to_all | solution.py:158
  506.5 10.7 %all-to-all-done.9 = bf16[128,1,2,3584]{3,2,1,0:T(2,128)(2,1)} async-done(((bf16[128,1,2,3584]{3,2,1,0:T(2,128)(2,1)}), bf16[128,1,2,3584]{3,2,1,0:T(2,128)(2,1)}, u32[]{:S(2)}, u32[]{:S(2)}) %all-to-all-start.9) | async-done | bytes 1835040 | tf_op jit(solution)/shard_map/all_to_all | solution.py:158
  517.2 6.0 %all-to-all-start.4 = ((bf16[128,1,2,3584]{3,2,1,0:T(2,128)(2,1)}), bf16[128,1,2,3584]{3,2,1,0:T(2,128)(2,1)}, u32[]{:S(2)}, u32[]{:S(2)}) async-start(bf16[128,1,2,3584]{3,2,1,0:T(2,128)(2,1)} %copy.206), calls=%async_computation.4 | async-start | bytes 3670016 | tf_op jit(solution)/shard_map/all_to_all | solution.py:158
  538.2 12.3 %all-to-all-done.4 = bf16[128,1,2,3584]{3,2,1,0:T(2,128)(2,1)} async-done(((bf16[128,1,2,3584]{3,2,1,0:T(2,128)(2,1)}), bf16[128,1,2,3584]{3,2,1,0:T(2,128)(2,1)}, u32[]{:S(2)}, u32[]{:S(2)}) %all-to-all-start.4) | async-done | bytes 1835040 | tf_op jit(solution)/shard_map/all_to_all | solution.py:158
  (282 shorter events, 220.6 us)
Async XLA Ops:
  6.5 140.3 %copy-start = (bf16[256,3584]{1,0:T(8,128)(2,1)S(1)}, bf16[256,3584]{1,0:T(8,128)(2,1)}, u32[]{:S(2)}) copy-start(bf16[256,3584]{1,0:T(8,128)(2,1)} %param.21) | copy-start | bytes 5505028
  8.1 15.7 %all-to-all-start.11 = ((bf16[32,4,128]{2,1,0:T(4,128)(2,1)}), bf16[32,4,128]{2,1,0:T(4,128)(2,1)S(1)}, u32[]{:S(2)}, u32[]{:S(2)}) async-start(bf16[32,4,128]{2,1,0:T(4,128)(2,1)} %bitcast.70), calls=%async_computation.11 | async-start | bytes 65536 | tf_op jit(solution)/shard_map/all_to_all | solution.py:80
  23.8 13.8 %all-to-all-start.16 = ((bf16[32,4,128]{2,1,0:T(4,128)(2,1)}), bf16[32,4,128]{2,1,0:T(4,128)(2,1)S(1)}, u32[]{:S(2)}, u32[]{:S(2)}) async-start(bf16[32,4,128]{2,1,0:T(4,128)(2,1)} %bitcast.99), calls=%async_computation.16 | async-start | bytes 65536 | tf_op jit(solution)/shard_map/all_to_all | solution.py:80
  37.6 12.4 %all-to-all-start.6 = ((bf16[32,4,128]{2,1,0:T(4,128)(2,1)}), bf16[32,4,128]{2,1,0:T(4,128)(2,1)S(1)}, u32[]{:S(2)}, u32[]{:S(2)}) async-start(bf16[32,4,128]{2,1,0:T(4,128)(2,1)} %bitcast.41), calls=%async_computation.6 | async-start | bytes 65536 | tf_op jit(solution)/shard_map/all_to_all | solution.py:80
  50.0 11.4 %all-to-all-start.1 = ((bf16[32,4,128]{2,1,0:T(4,128)(2,1)}), bf16[32,4,128]{2,1,0:T(4,128)(2,1)S(1)}, u32[]{:S(2)}, u32[]{:S(2)}) async-start(bf16[32,4,128]{2,1,0:T(4,128)(2,1)} %bitcast.4), calls=%async_computation.1 | async-start | bytes 65536 | tf_op jit(solution)/shard_map/all_to_all | solution.py:80
  61.4 12.8 %all-to-all-start.10 = ((bf16[32,4,1024]{2,1,0:T(4,128)(2,1)}), bf16[32,4,1024]{2,1,0:T(4,128)(2,1)S(1)}, u32[]{:S(2)}, u32[]{:S(2)}) async-start(bf16[32,4,1024]{2,1,0:T(4,128)(2,1)} %all_to_all.190), calls=%async_computation.10 | async-start | bytes 524288 | tf_op jit(solution)/shard_map/all_to_all | solution.py:73
  74.2 12.8 %all-to-all-start.15 = ((bf16[32,4,1024]{2,1,0:T(4,128)(2,1)}), bf16[32,4,1024]{2,1,0:T(4,128)(2,1)S(1)}, u32[]{:S(2)}, u32[]{:S(2)}) async-start(bf16[32,4,1024]{2,1,0:T(4,128)(2,1)} %all_to_all.201), calls=%async_computation.15 | async-start | bytes 524288 | tf_op jit(solution)/shard_map/all_to_all | solution.py:73
  87.0 13.5 %all-to-all-start.5 = ((bf16[32,4,1024]{2,1,0:T(4,128)(2,1)}), bf16[32,4,1024]{2,1,0:T(4,128)(2,1)}, u32[]{:S(2)}, u32[]{:S(2)}) async-start(bf16[32,4,1024]{2,1,0:T(4,128)(2,1)} %all_to_all.179), calls=%async_computation.5 | async-start | bytes 524288 | tf_op jit(solution)/shard_map/all_to_all | solution.py:73
  100.5 13.5 %all-to-all-start = ((bf16[32,4,1024]{2,1,0:T(4,128)(2,1)}), bf16[32,4,1024]{2,1,0:T(4,128)(2,1)}, u32[]{:S(2)}, u32[]{:S(2)}) async-start(bf16[32,4,1024]{2,1,0:T(4,128)(2,1)} %all_to_all.168), calls=%async_computation | async-start | bytes 524288 | tf_op jit(solution)/shard_map/all_to_all | solution.py:73
  114.1 13.5 %all-to-all-start.12 = ((bf16[4,32,1024]{2,0,1:T(4,128)(2,1)}), bf16[4,32,1024]{2,0,1:T(4,128)(2,1)}, u32[]{:S(2)}, u32[]{:S(2)}) async-start(bf16[4,32,1024]{2,0,1:T(4,128)(2,1)} %copy.235), calls=%async_computation.12 | async-start | bytes 524288 | tf_op jit(solution)/shard_map/all_to_all | solution.py:115
  127.6 13.7 %all-to-all-start.17 = ((bf16[4,32,1024]{2,0,1:T(4,128)(2,1)}), bf16[4,32,1024]{2,0,1:T(4,128)(2,1)}, u32[]{:S(2)}, u32[]{:S(2)}) async-start(bf16[4,32,1024]{2,0,1:T(4,128)(2,1)} %copy.252), calls=%async_computation.17 | async-start | bytes 524288 | tf_op jit(solution)/shard_map/all_to_all | solution.py:115
  141.3 12.8 %all-to-all-start.7 = ((bf16[4,32,1024]{2,0,1:T(4,128)(2,1)}), bf16[4,32,1024]{2,0,1:T(4,128)(2,1)S(1)}, u32[]{:S(2)}, u32[]{:S(2)}) async-start(bf16[4,32,1024]{2,0,1:T(4,128)(2,1)} %copy.218), calls=%async_computation.7 | async-start | bytes 524288 | tf_op jit(solution)/shard_map/all_to_all | solution.py:115
  154.1 12.8 %all-to-all-start.2 = ((bf16[4,32,1024]{2,0,1:T(4,128)(2,1)}), bf16[4,32,1024]{2,0,1:T(4,128)(2,1)S(1)}, u32[]{:S(2)}, u32[]{:S(2)}) async-start(bf16[4,32,1024]{2,0,1:T(4,128)(2,1)} %copy.201), calls=%async_computation.2 | async-start | bytes 524288 | tf_op jit(solution)/shard_map/all_to_all | solution.py:115
  158.0 119.9 %all-reduce.7.cloned.1.call-start = ((), (), s32[]{:S(2)}) async-start(), calls=%async_computation.20 | async-start | bytes 7340032
  168.7 109.2 %copy-start.9 = (bf16[4,4,3584]{2,1,0:T(4,128)(2,1)S(1)}, bf16[4,4,3584]{2,1,0:T(4,128)(2,1)}, u32[]{:S(2)}) copy-start(bf16[4,4,3584]{2,1,0:T(4,128)(2,1)} %param.27) | copy-start | bytes 344068
  168.7 110.4 %copy-start.12 = (f32[3584]{0:T(1024)S(1)}, f32[3584]{0:T(1024)}, u32[]{:S(2)}) copy-start(f32[3584]{0:T(1024)} %param.28) | copy-start | bytes 43012
  282.3 35.9 %all-to-all-start.18 = ((bf16[128,1,2,3584]{3,2,1,0:T(2,128)(2,1)}), bf16[128,1,2,3584]{3,2,1,0:T(2,128)(2,1)}, u32[]{:S(2)}, u32[]{:S(2)}) async-start(bf16[128,1,2,3584]{3,2,1,0:T(2,128)(2,1)} %bitcast.106), calls=%async_computation.18 | async-start | bytes 3670016 | tf_op jit(solution)/shard_map/all_to_all | solution.py:153
  318.2 33.0 %all-to-all-start.13 = ((bf16[128,1,2,3584]{3,2,1,0:T(2,128)(2,1)}), bf16[128,1,2,3584]{3,2,1,0:T(2,128)(2,1)}, u32[]{:S(2)}, u32[]{:S(2)}) async-start(bf16[128,1,2,3584]{3,2,1,0:T(2,128)(2,1)} %bitcast.77), calls=%async_computation.13 | async-start | bytes 3670016 | tf_op jit(solution)/shard_map/all_to_all | solution.py:153
  351.2 33.0 %all-to-all-start.8 = ((bf16[128,1,2,3584]{3,2,1,0:T(2,128)(2,1)}), bf16[128,1,2,3584]{3,2,1,0:T(2,128)(2,1)}, u32[]{:S(2)}, u32[]{:S(2)}) async-start(bf16[128,1,2,3584]{3,2,1,0:T(2,128)(2,1)} %bitcast.48), calls=%async_computation.8 | async-start | bytes 3670016 | tf_op jit(solution)/shard_map/all_to_all | solution.py:153
  384.2 32.7 %all-to-all-start.3 = ((bf16[128,1,2,3584]{3,2,1,0:T(2,128)(2,1)}), bf16[128,1,2,3584]{3,2,1,0:T(2,128)(2,1)S(1)}, u32[]{:S(2)}, u32[]{:S(2)}) async-start(bf16[128,1,2,3584]{3,2,1,0:T(2,128)(2,1)} %bitcast.13), calls=%async_computation.3 | async-start | bytes 3670016 | tf_op jit(solution)/shard_map/all_to_all | solution.py:153
  418.2 32.5 %all-to-all-start.19 = ((bf16[128,1,2,3584]{3,2,1,0:T(2,128)(2,1)}), bf16[128,1,2,3584]{3,2,1,0:T(2,128)(2,1)S(1)}, u32[]{:S(2)}, u32[]{:S(2)}) async-start(bf16[128,1,2,3584]{3,2,1,0:T(2,128)(2,1)} %copy.257), calls=%async_computation.19 | async-start | bytes 3670016 | tf_op jit(solution)/shard_map/all_to_all | solution.py:158
  450.7 33.2 %all-to-all-start.14 = ((bf16[128,1,2,3584]{3,2,1,0:T(2,128)(2,1)}), bf16[128,1,2,3584]{3,2,1,0:T(2,128)(2,1)}, u32[]{:S(2)}, u32[]{:S(2)}) async-start(bf16[128,1,2,3584]{3,2,1,0:T(2,128)(2,1)} %copy.240), calls=%async_computation.14 | async-start | bytes 3670016 | tf_op jit(solution)/shard_map/all_to_all | solution.py:158
  483.9 33.3 %all-to-all-start.9 = ((bf16[128,1,2,3584]{3,2,1,0:T(2,128)(2,1)}), bf16[128,1,2,3584]{3,2,1,0:T(2,128)(2,1)}, u32[]{:S(2)}, u32[]{:S(2)}) async-start(bf16[128,1,2,3584]{3,2,1,0:T(2,128)(2,1)} %copy.223), calls=%async_computation.9 | async-start | bytes 3670016 | tf_op jit(solution)/shard_map/all_to_all | solution.py:158
  517.2 33.3 %all-to-all-start.4 = ((bf16[128,1,2,3584]{3,2,1,0:T(2,128)(2,1)}), bf16[128,1,2,3584]{3,2,1,0:T(2,128)(2,1)}, u32[]{:S(2)}, u32[]{:S(2)}) async-start(bf16[128,1,2,3584]{3,2,1,0:T(2,128)(2,1)} %copy.206), calls=%async_computation.4 | async-start | bytes 3670016 | tf_op jit(solution)/shard_map/all_to_all | solution.py:158
  (41 other events, 386.6 us)
Sparse Core Ops, SparseCore 0:
  168.9 109.0 all-reduce.6
where the time goes:
time: 578 us; the launch traced here: 568 us
  waiting for transfers between devices  291 us (50%)
  starting transfers between devices  105 us (18%)
  matrix products  85.1 us (15%)
  local copies, waits for them, and re-layouts  61.2 us (11%)
  between operations  15.8 us (3%)
  other arithmetic  9.12 us (2%)
    unnamed x2, waiting for transfers between devices  106 us
    all_to_all x4, waiting for transfers between devices, per_device(): lax.all_to_all(outbound, ('dp', 'ep'), split_axis=0, concat_axis=0, tiled...  82.4 us
    all_to_all x4, waiting for transfers between devices, per_device(): lax.all_to_all(finished, ('dp', 'ep'), split_axis=0, concat_axis=0, tiled...  43.7 us
    all_to_all x4, starting transfers between devices, per_device(): lax.all_to_all(outbound, ('dp', 'ep'), split_axis=0, concat_axis=0, tiled...  25.1 us
    all_to_all x4, starting transfers between devices, per_device(): lax.all_to_all(query_rotary[current], 'ep', split_axis=0, concat_axis=1,...  23.5 us
    dot_general x4, matrix products, feed_forward(): jnp.einsum('...emd,edh->...emh', received, expert_gate, preferred_element...  23.4 us
    dot_general x4, matrix products, feed_forward(): jnp.einsum('...emd,edh->...emh', received, expert_up, preferred_element_t...  23.3 us
    all_to_all x4, waiting for transfers between devices, per_device(): lax.all_to_all(absorbed.reshape(group_rows, head_local * LAT), 'ep', spli...  22.9 us
  transfers between devices with their start and end apart: 21, of which 21 were waited for; matrix products, arithmetic and copies ran while one was open for 23% of the time, Pallas kernels for 0%

commit v1 on v0

v1 whole, which is shorter than its diff:
```python
import jax
import jax.numpy as jnp
from jax import lax
from jax.sharding import PartitionSpec as P

D = 3584
HEADS = 64
LAT = 512
ROPE = 64
NOPE = 128
VHEAD = 128
MOST = 2
STEPS = 4
EXPERTS = 128
LMAX = 64
ROWS_DEV = 4
CHIPS = 16
HC = 4
RS = STEPS * ROWS_DEV

SAME_CORE = [[2 * chip + core for chip in range(CHIPS)] for core in range(2)]
OTHER_CORE = [(i, i ^ 1) for i in range(2 * CHIPS)]


def other_core(x):
    return lax.ppermute(x, "ep", OTHER_CORE)


def exchange(x):
    return lax.all_to_all(x, "ep", 0, 0, tiled=True, axis_index_groups=SAME_CORE)


def attend(absorbed, rotary, cache_latent, cache_rotary, lengths, new_latent, new_rotary):
    scale = 1.0 / (NOPE + ROPE) ** 0.5
    f32 = jnp.float32
    cached = jnp.einsum("clqd,lpd->lcqp", absorbed, cache_latent, preferred_element_type=f32)
    cached = cached + jnp.einsum("clqe,lep->lcqp", rotary, cache_rotary, preferred_element_type=f32)
    fresh = jnp.einsum("clqd,jld->lcqj", absorbed, new_latent, preferred_element_type=f32)
    fresh = fresh + jnp.einsum("clqe,jle->lcqj", rotary, new_rotary, preferred_element_type=f32)
    visible = jnp.arange(LMAX, dtype=jnp.int32)[None, :] < lengths[:, None]
    step = jnp.arange(HC * STEPS, dtype=jnp.int32) % STEPS
    known = jnp.arange(STEPS, dtype=jnp.int32)[None, :] <= step[:, None]
    cached = jnp.where(visible[:, None, None, :], cached * scale, -jnp.inf)
    fresh = jnp.where(known[None, None], fresh * scale, -jnp.inf)
    peak = jnp.maximum(jnp.max(cached, axis=-1), jnp.max(fresh, axis=-1))[..., None]
    cached = jnp.exp(cached - peak)
    fresh = jnp.exp(fresh - peak)
    total = jnp.sum(cached, axis=-1, keepdims=True) + jnp.sum(fresh, axis=-1, keepdims=True)
    cached = (cached / total).astype(jnp.bfloat16)
    fresh = (fresh / total).astype(jnp.bfloat16)
    mixed = jnp.einsum("lcqp,lpd->clqd", cached, cache_latent, preferred_element_type=f32)
    mixed = mixed + jnp.einsum("lcqj,jld->clqd", fresh, new_latent, preferred_element_type=f32)
    return mixed.astype(jnp.bfloat16)


def per_device(
    query_plain,
    query_rotary,
    key_up,
    value_up,
    output_weight,
    cache_latent,
    cache_rotary,
    lengths,
    new_latent,
    new_rotary,
    residual,
    norm_gain,
    expert_ids,
    gate_weights,
    expert_gate,
    expert_up,
    expert_down,
):
    f32 = jnp.float32
    bf16 = jnp.bfloat16
    core = lax.axis_index("ep") % 2
    expert = lax.axis_index("dp") * lax.axis_size("ep") + lax.axis_index("ep")

    ids = jnp.swapaxes(expert_ids, 0, 1).reshape(RS, -1)
    weights = jnp.swapaxes(gate_weights, 0, 1).reshape(RS, -1)
    meta = jnp.concatenate([ids.astype(f32), weights], axis=1)
    meta = lax.all_gather(meta, ("dp", "ep"), axis=0, tiled=True)

    queries = jnp.concatenate([query_plain, query_rotary], axis=2)
    queries = queries.reshape(STEPS, CHIPS, 2, ROWS_DEV, 2 * (NOPE + ROPE))
    kept = lax.dynamic_index_in_dim(queries, core, axis=2, keepdims=False)
    given = lax.dynamic_index_in_dim(queries, 1 - core, axis=2, keepdims=False)
    given = other_core(given)
    key_map = jnp.concatenate([key_up, other_core(key_up)], axis=0)
    value_map = jnp.concatenate([value_up, other_core(value_up)], axis=0)
    out_map = jnp.concatenate([output_weight, other_core(output_weight)], axis=0)
    split = 2 * NOPE
    plain = jnp.stack([kept[..., :split], given[..., :split]], axis=3)
    plain = plain.reshape(STEPS, CHIPS, ROWS_DEV, HC, NOPE)
    rotary = jnp.stack([kept[..., split:], given[..., split:]], axis=3)
    rotary = rotary.reshape(STEPS, CHIPS, ROWS_DEV, HC, ROPE)
    absorbed = jnp.einsum("sclhn,hnd->clhsd", plain, key_map, preferred_element_type=f32)
    absorbed = absorbed.astype(bf16).reshape(CHIPS, ROWS_DEV, HC * STEPS, LAT)
    rotary = jnp.transpose(rotary, (1, 2, 3, 0, 4)).reshape(CHIPS, ROWS_DEV, HC * STEPS, ROPE)
    sent = exchange(jnp.concatenate([absorbed, rotary], axis=3))
    mixed = attend(
        sent[..., :LAT],
        sent[..., LAT:],
        cache_latent,
        cache_rotary,
        lengths,
        new_latent,
        new_rotary,
    )
    mixed = exchange(mixed).reshape(CHIPS, ROWS_DEV, HC, STEPS, LAT)
    values = jnp.einsum("clhsd,hdv->clshv", mixed, value_map, preferred_element_type=f32)
    values = values.astype(bf16).reshape(CHIPS * RS, HC * VHEAD)
    parts = jnp.dot(values, out_map, preferred_element_type=f32).astype(bf16)
    parts = exchange(parts.reshape(CHIPS, RS, D))
    attention = jnp.sum(parts.astype(f32), axis=0)
    hidden = jnp.swapaxes(residual, 0, 1).reshape(RS, D).astype(f32) + attention
    normed = (
        hidden * lax.rsqrt(jnp.mean(hidden * hidden, axis=-1, keepdims=True) + 1e-06) * norm_gain
    ).astype(bf16)

    rows = lax.all_gather(normed, ("dp", "ep"), axis=0, tiled=True)
    same = meta[:, :8] == expert.astype(f32)
    weight = jnp.sum(jnp.where(same, meta[:, 8:], 0.0), axis=1)
    named = jnp.any(same, axis=1).astype(jnp.int32).reshape(EXPERTS, ROWS_DEV, STEPS)
    rank = jnp.cumsum(named, axis=1) - named
    place = jnp.arange(EXPERTS, dtype=jnp.int32)[:, None, None] % 16 * (MOST * STEPS)
    place = place + jnp.arange(STEPS, dtype=jnp.int32)[None, None, :] * MOST + rank
    place = jnp.where(named > 0, place, -1).reshape(8, 1, 256)
    pick = place == jnp.arange(128, dtype=jnp.int32)[None, :, None]
    slot_weight = jnp.sum(jnp.where(pick, weight.reshape(8, 1, 256), 0.0), axis=2)
    slots = jnp.einsum(
        "tsr,trd->tsd", pick.astype(bf16), rows.reshape(8, 256, D), preferred_element_type=f32
    )
    slots = slots.astype(bf16).reshape(8 * 128, D)
    gate = jnp.dot(slots, expert_gate[0], preferred_element_type=f32)
    upward = jnp.dot(slots, expert_up[0], preferred_element_type=f32)
    inner = (jax.nn.silu(gate) * upward).astype(bf16)
    result = jnp.dot(inner, expert_down[0], preferred_element_type=f32)
    result = (result * slot_weight.reshape(-1, 1)).astype(bf16)

    back = lax.all_to_all(
        result.reshape(EXPERTS, MOST * STEPS, D), ("dp", "ep"), 0, 0, tiled=True
    ).reshape(EXPERTS * MOST * STEPS, D)
    chosen = ids.reshape(ROWS_DEV, STEPS, -1)
    earlier = jnp.tril(jnp.ones((ROWS_DEV, ROWS_DEV), jnp.int32), -1)
    twins = jnp.any(chosen[:, None, :, :, None] == chosen[None, :, :, None, :], axis=-1)
    rank = jnp.sum(twins.astype(jnp.int32) * earlier[:, :, None, None], axis=1)
    target = chosen * (MOST * STEPS) + rank
    target = target + jnp.arange(STEPS, dtype=jnp.int32)[None, :, None] * MOST
    target = target.reshape(RS, -1, 1)
    slot_index = jnp.arange(EXPERTS * MOST * STEPS, dtype=jnp.int32)
    take = jnp.any(target == slot_index[None, None, :], axis=1).astype(bf16)
    routed = jnp.dot(take, back, preferred_element_type=f32)
    out = (hidden + routed).astype(bf16)
    return jnp.swapaxes(out.reshape(ROWS_DEV, STEPS, D), 0, 1)


def solution(mesh):
    return jax.shard_map(
        per_device,
        mesh=mesh,
        in_specs=(
            P(None, "dp", "ep"),
            P(None, "dp", "ep"),
            P("ep", None, None),
            P("ep", None, None),
            P("ep", None),
            P(("dp", "ep"), None, None),
            P(("dp", "ep"), None, None),
            P(("dp", "ep")),
            P(None, ("dp", "ep"), None),
            P(None, ("dp", "ep"), None),
            P(None, ("dp", "ep"), None),
            P(),
            P(None, ("dp", "ep"), None),
            P(None, ("dp", "ep"), None),
            P(("dp", "ep"), None, None),
            P(("dp", "ep"), None, None),
            P(("dp", "ep"), None, None),
        ),
        out_specs=P(None, ("dp", "ep"), None),
        check_vma=False,
    )
```

time: 578 us -> 329 us (0.57); the launches traced: 568 us -> 327 us
  waiting for transfers between devices: 291 us -> 187 us
  starting transfers between devices: 105 us -> 24.9 us
  local copies, waits for them, and re-layouts: 61.2 us -> 6.46 us
  blocking collectives: 0 us -> 34.7 us
  matrix products: 85.1 us -> 51.8 us
    unnamed x2 -> x1, waiting for transfers between devices: 106 us -> 0.02 us
    all_to_all x20 -> x4, starting transfers between devices: 105 us -> 24.1 us  [the longest x3 15.5 us: exchange(): lax.all_to_all(x, 'ep', 0, 0, tiled=True, axis_index_groups=SAME_CORE)]
    all_gather x0 -> x1, waiting for transfers between devices: none -> 37.6 us  [per_device(): rows = lax.all_gather(normed, ('dp', 'ep'), axis=0, tiled=True)]
    all_to_all x20 -> x4, waiting for transfers between devices: 185 us -> 149 us  [the longest x1 86.9 us: per_device(): lax.all_to_all(result.reshape(EXPERTS, MOST * STEPS, D), ('dp', 'ep'), 0,...]
    all_gather x0 -> x1, blocking collectives: none -> 34.7 us  [per_device(): meta = lax.all_gather(meta, ('dp', 'ep'), axis=0, tiled=True)]
    dot_general x52 -> x14, matrix products: 85.1 us -> 51.8 us  [the longest x1 10.8 us: per_device(): gate = jnp.dot(slots, expert_gate[0], preferred_element_type=f32)]
    reshape x20 -> x7, local copies, waits for them, and re-layouts: 24.7 us -> 1.78 us  [the longest x2 0.73 us: per_device(): return jnp.swapaxes(out.reshape(ROWS_DEV, STEPS, D), 0, 1)]
    convert_element_type x8 -> x6, local copies, waits for them, and re-layouts: 13.5 us -> 1.8 us  [the longest x1 1.07 us: attend(): return mixed.astype(jnp.bfloat16)]
  transfers between devices with their start and end apart: 21 -> 9, of which waited for: 21 -> 6; matrix products, arithmetic and copies ran while one was open for 23% -> 4% of each run, Pallas kernels for 0% -> 0%
where the time goes in v1:
time: 329 us; the launch traced here: 327 us
  waiting for transfers between devices  187 us (57%)
  matrix products  51.8 us (16%)
  blocking collectives  34.7 us (11%)
  starting transfers between devices  24.9 us (8%)
  between operations  14 us (4%)
  other arithmetic  7.74 us (2%)
  local copies, waits for them, and re-layouts  6.46 us (2%)
    all_to_all x1, waiting for transfers between devices, per_device(): lax.all_to_all(result.reshape(EXPERTS, MOST * STEPS, D), ('dp', 'ep'), 0,...  86.9 us
    all_to_all x3, waiting for transfers between devices, exchange(): lax.all_to_all(x, 'ep', 0, 0, tiled=True, axis_index_groups=SAME_CORE)  61.9 us
    all_gather x1, waiting for transfers between devices, per_device(): rows = lax.all_gather(normed, ('dp', 'ep'), axis=0, tiled=True)  37.6 us
    all_gather x1, blocking collectives, per_device(): meta = lax.all_gather(meta, ('dp', 'ep'), axis=0, tiled=True)  34.7 us
    all_to_all x3, starting transfers between devices, exchange(): lax.all_to_all(x, 'ep', 0, 0, tiled=True, axis_index_groups=SAME_CORE)  15.5 us
    dot_general x1, matrix products, per_device(): gate = jnp.dot(slots, expert_gate[0], preferred_element_type=f32)  10.8 us
    dot_general x1, matrix products, per_device(): upward = jnp.dot(slots, expert_up[0], preferred_element_type=f32)  10.3 us
    dot_general x1, matrix products, per_device(): result = jnp.dot(inner, expert_down[0], preferred_element_type=f32)  9.87 us
  transfers between devices with their start and end apart: 9, of which 6 were waited for; matrix products, arithmetic and copies ran while one was open for 4% of the time, Pallas kernels for 0%

profile of v1, /device:TPU:0, one launch (start us, length us, event | category | flops | bytes accessed | tf_op | source)
XLA Modules:
  0.0 327.2 jit_solution(11632176249486040240)
XLA Ops:
  6.5 1.1 pad_maximum_fusion.1
  8.6 1.0 collective-permute-done.2
  11.6 1.2 pad_maximum_fusion
  12.8 8.0 %all-to-all-start = ((bf16[16,4,16,576]{3,2,1,0:T(8,128)(2,1)}), bf16[16,4,16,576]{3,2,1,0:T(8,128)(2,1)S(1)}, u32[]{:S(2)}, u32[]{:S(2)}) async-start(bf16[16,4,16,576]{3,2,1,0:T(8,128)(2,1)} %pad_maximum_fusion), calls=%async_computation | async-start | bytes 2621440 | tf_op jit(solution)/shard_map/all_to_all | solution.py:30
  21.1 21.2 %all-to-all-done = bf16[16,4,16,576]{3,2,1,0:T(8,128)(2,1)S(1)} async-done(((bf16[16,4,16,576]{3,2,1,0:T(8,128)(2,1)}), bf16[16,4,16,576]{3,2,1,0:T(8,128)(2,1)S(1)}, u32[]{:S(2)}, u32[]{:S(2)}) %all-to-all-start) | async-done | bytes 1179680 | tf_op jit(solution)/shard_map/all_to_all | solution.py:30
  43.2 1.3 fusion.67
  46.7 1.1 copy.131
  47.7 3.7 %all-to-all-start.1 = ((bf16[16,4,16,512]{3,2,1,0:T(8,128)(2,1)}), bf16[16,4,16,512]{3,2,1,0:T(8,128)(2,1)S(1)}, u32[]{:S(2)}, u32[]{:S(2)}) async-start(bf16[16,4,16,512]{3,2,1,0:T(8,128)(2,1)} %copy.131), calls=%async_computation.1 | async-start | bytes 2097152 | tf_op jit(solution)/shard_map/all_to_all | solution.py:30
  51.5 15.9 %all-to-all-done.1 = bf16[16,4,16,512]{3,2,1,0:T(8,128)(2,1)S(1)} async-done(((bf16[16,4,16,512]{3,2,1,0:T(8,128)(2,1)}), bf16[16,4,16,512]{3,2,1,0:T(8,128)(2,1)S(1)}, u32[]{:S(2)}, u32[]{:S(2)}) %all-to-all-start.1) | async-done | bytes 1048608 | tf_op jit(solution)/shard_map/all_to_all | solution.py:30
  68.7 1.4 fusion.24
  70.3 3.9 %convolution_convert_fusion.1 = bf16[256,3584]{1,0:T(8,128)(2,1)} fusion(bf16[256,3584]{1,0:T(8,128)(2,1)} %collective-permute-done.3, bf16[256,3584]{1,0:T(8,128)(2,1)S(1)} %copy-done.8, bf16[32,8,4,128]{3,2,1,0:T(4,128)(2,1)S(1)} %bitcast.114), kind=kOutput, calls=%fused_computation.10 | convolution fusion | flops 947781632 | bytes 5767168 | tf_op jit(solution)/shard_map/dot_general | solution.py:114
  74.2 3.8 %all-to-all-start.2 = ((bf16[16,16,3584]{2,1,0:T(8,128)(2,1)}), bf16[16,16,3584]{2,1,0:T(8,128)(2,1)S(1)}, u32[]{:S(2)}, u32[]{:S(2)}) async-start(bf16[16,16,3584]{2,1,0:T(8,128)(2,1)} %bitcast.107), calls=%async_computation.2 | async-start | bytes 3670016 | tf_op jit(solution)/shard_map/all_to_all | solution.py:30
  78.4 24.8 %all-to-all-done.2 = bf16[16,16,3584]{2,1,0:T(8,128)(2,1)S(1)} async-done(((bf16[16,16,3584]{2,1,0:T(8,128)(2,1)}), bf16[16,16,3584]{2,1,0:T(8,128)(2,1)S(1)}, u32[]{:S(2)}, u32[]{:S(2)}) %all-to-all-start.2) | async-done | bytes 1835040 | tf_op jit(solution)/shard_map/all_to_all | solution.py:30
  103.9 0.7 multiply_convert_fusion.2
  104.8 34.7 %all_gather.6 = f32[2048,16]{1,0:T(8,128)S(1)} all-gather(f32[16,16]{1,0:T(8,128)S(1)} %pad_maximum_fusion.4), channel_id=1, replica_groups=mesh['dp'=4,'ep'=32] {'dp','ep'}, dimensions={0}, use_global_device_ids=true | all-gather | bytes 132096 | tf_op jit(solution)/shard_map/all_gather | solution.py:83
  142.2 37.6 %all-gather.2.cloned.1.call-done = bf16[2048,3584]{1,0:T(8,128)(2,1)} async-done(((bf16[16,3584]{1,0:T(8,128)(2,1)}), bf16[2048,3584]{1,0:T(8,128)(2,1)}) %all-gather.2.cloned.1.call-update) | async-done | bytes 14680080 | tf_op jit(solution)/shard_map/all_gather | solution.py:122
  179.9 7.3 %convolution_convert_fusion = bf16[8,128,3584]{2,1,0:T(8,128)(2,1)S(1)} fusion(bf16[8,256,3584]{2,1,0:T(8,128)(2,1)} %bitcast.104, s32[8,256]{1,0:T(8,128)S(1)} %add_select_fusion), kind=kOutput, calls=%fused_computation.1 | convolution fusion | flops 1882980352 | bytes 22028288 | tf_op jit(solution)/shard_map/tsr,trd->tsd/dot_general | solution.py:132
  187.2 10.3 %fusion.3 = f32[1024,1024]{1,0:T(8,128)S(1)} fusion(bf16[1024,3584]{1,0:T(8,128)(2,1)S(1)} %bitcast.105, bf16[1,3584,1024]{2,1,0:T(8,128)(2,1)} %param.32), kind=kOutput, calls=%fused_computation.5 | convolution fusion | flops 7516192768 | bytes 18874368 | tf_op jit(solution)/shard_map/dot_general | solution.py:137
  197.5 10.8 %multiply_convert_fusion.1 = bf16[1024,1024]{1,0:T(8,128)(2,1)S(1)} fusion(f32[1024,1024]{1,0:T(8,128)S(1)} %fusion.3, bf16[1024,3584]{1,0:T(8,128)(2,1)S(1)} %bitcast.106, bf16[1,3584,1024]{2,1,0:T(8,128)(2,1)} %param.31), kind=kOutput, calls=%fused_computation.13 | convolution fusion | flops 7522484224 | bytes 20971520 | tf_op jit(solution)/shard_map/dot_general | solution.py:136
  208.3 9.9 %fusion.7 = bf16[128,8,3584]{2,1,0:T(8,128)(2,1)} fusion(f32[1024]{0:T(1024)S(1)} %bitcast.122, bf16[1024,1024]{1,0:T(8,128)(2,1)S(1)} %multiply_convert_fusion.1, bf16[1,1024,3584]{2,1,0:T(8,128)(2,1)S(1)} %bitcast.124), kind=kOutput, calls=%fused_computation.9 | convolution fusion | flops 7523532800 | bytes 16781312 | tf_op jit(solution)/shard_map/dot_general | solution.py:139
  218.2 8.6 %all-to-all-start.3 = ((bf16[128,8,3584]{2,1,0:T(8,128)(2,1)}), bf16[128,8,3584]{2,1,0:T(8,128)(2,1)}, u32[]{:S(2)}, u32[]{:S(2)}) async-start(bf16[128,8,3584]{2,1,0:T(8,128)(2,1)} %fusion.7), calls=%async_computation.3 | async-start | bytes 14680064 | tf_op jit(solution)/shard_map/all_to_all | solution.py:142
  226.8 1.3 compare_reduce_fusion
  228.6 86.9 %all-to-all-done.3 = bf16[128,8,3584]{2,1,0:T(8,128)(2,1)} async-done(((bf16[128,8,3584]{2,1,0:T(8,128)(2,1)}), bf16[128,8,3584]{2,1,0:T(8,128)(2,1)}, u32[]{:S(2)}, u32[]{:S(2)}) %all-to-all-start.3) | async-done | bytes 7340064 | tf_op jit(solution)/shard_map/all_to_all | solution.py:142
  315.4 4.1 %fusion.13 = bf16[16,3584]{1,0:T(8,128)(2,1)S(1)} fusion(f32[16,3584]{1,0:T(8,128)S(1)} %get-tuple-element.6, pred[16,1024]{1,0:T(8,128)(4,1)S(1)} %fusion.36, bf16[128,8,3584]{2,1,0:T(8,128)(2,1)} %all-to-all-done.3), kind=kOutput, calls=%fused_computation.12 | convolution fusion | flops 117555200 | bytes 7700480 | tf_op jit(solution)/shard_map/dot_general | solution.py:154
  (108 shorter events, 12.5 us)
Async XLA Ops:
  6.5 38.0 %copy-start = (bf16[4,64,512]{2,1,0:T(8,128)(2,1)S(1)}, bf16[4,64,512]{2,1,0:T(8,128)(2,1)}, u32[]{:S(2)}) copy-start(bf16[4,64,512]{2,1,0:T(8,128)(2,1)} %param.22) | copy-start | bytes 786436
  6.5 4.0 %copy-start.9 = (bf16[2,128,512]{2,1,0:T(8,128)(2,1)S(1)}, bf16[2,128,512]{2,1,0:T(8,128)(2,1)}, u32[]{:S(2)}) copy-start(bf16[2,128,512]{2,1,0:T(8,128)(2,1)} %param.19) | copy-start | bytes 786436
  6.5 4.0 %collective-permute-start.1 = (bf16[2,128,512]{2,1,0:T(8,128)(2,1)}, bf16[2,128,512]{2,1,0:T(8,128)(2,1)S(1)}, u32[]{:S(2)}, u32[]{:S(2)}) collective-permute-start(bf16[2,128,512]{2,1,0:T(8,128)(2,1)} %param.19), channel_id=1, source_target_pairs={{0,1},{1,0},{2,3},{3,2},{4,5},{5,4},{6,7},{7,6},{8,9},{9,8},{10,11... | collective-permute-start | bytes 786440 | tf_op jit(solution)/shard_map/ppermute | solution.py:26
  8.0 1.6 collective-permute-start.2
  11.0 9.8 %copy-start.8 = (bf16[256,3584]{1,0:T(8,128)(2,1)S(1)}, bf16[256,3584]{1,0:T(8,128)(2,1)}, u32[]{:S(2)}) copy-start(bf16[256,3584]{1,0:T(8,128)(2,1)} %param.21) | copy-start | bytes 5505028
  11.0 10.0 %copy-start.13 = (s32[4]{0:T(128)S(1)}, s32[4]{0:T(128)}, u32[]{:S(2)}) copy-start(s32[4]{0:T(128)} %param.24) | copy-start | bytes 52
  11.0 31.3 %copy-start.12 = (bf16[4,4,64]{2,1,0:T(4,128)(2,1)S(1)}, bf16[4,4,64]{2,1,0:T(4,128)(2,1)}, u32[]{:S(2)}) copy-start(bf16[4,4,64]{2,1,0:T(4,128)(2,1)} %param.26) | copy-start | bytes 6148
  11.0 31.9 %copy-start.3 = (bf16[4,64,64]{2,1,0:T(8,128)(2,1)S(1)}, bf16[4,64,64]{2,1,0:T(8,128)(2,1)}, u32[]{:S(2)}) copy-start(bf16[4,64,64]{2,1,0:T(8,128)(2,1)} %param.23) | copy-start | bytes 98308
  11.0 32.2 %copy-start.5 = (bf16[4,4,512]{2,1,0:T(4,128)(2,1)S(1)}, bf16[4,4,512]{2,1,0:T(4,128)(2,1)}, u32[]{:S(2)}) copy-start(bf16[4,4,512]{2,1,0:T(4,128)(2,1)} %param.25) | copy-start | bytes 49156
  12.8 29.4 %all-to-all-start = ((bf16[16,4,16,576]{3,2,1,0:T(8,128)(2,1)}), bf16[16,4,16,576]{3,2,1,0:T(8,128)(2,1)S(1)}, u32[]{:S(2)}, u32[]{:S(2)}) async-start(bf16[16,4,16,576]{3,2,1,0:T(8,128)(2,1)} %pad_maximum_fusion), calls=%async_computation | async-start | bytes 2621440 | tf_op jit(solution)/shard_map/all_to_all | solution.py:30
  20.8 49.5 %collective-permute-start.3 = (bf16[256,3584]{1,0:T(8,128)(2,1)S(1)}, bf16[256,3584]{1,0:T(8,128)(2,1)}, u32[]{:S(2)}, u32[]{:S(2)}) collective-permute-start(bf16[256,3584]{1,0:T(8,128)(2,1)S(1)} %copy-done.8), channel_id=1, source_target_pairs={{0,1},{1,0},{2,3},{3,2},{4,5},{5,4},{6,7},{7,6},{8,9},{9,8},{10,11... | collective-permute-start | bytes 5505032 | tf_op jit(solution)/shard_map/ppermute | solution.py:26
  46.1 5.2 %copy-start.10 = (bf16[2,512,128]{2,1,0:T(8,128)(2,1)S(1)}, bf16[2,512,128]{2,1,0:T(8,128)(2,1)}, u32[]{:S(2)}) copy-start(bf16[2,512,128]{2,1,0:T(8,128)(2,1)} %param.20) | copy-start | bytes 786436
  47.7 19.7 %all-to-all-start.1 = ((bf16[16,4,16,512]{3,2,1,0:T(8,128)(2,1)}), bf16[16,4,16,512]{3,2,1,0:T(8,128)(2,1)S(1)}, u32[]{:S(2)}, u32[]{:S(2)}) async-start(bf16[16,4,16,512]{3,2,1,0:T(8,128)(2,1)} %copy.131), calls=%async_computation.1 | async-start | bytes 2097152 | tf_op jit(solution)/shard_map/all_to_all | solution.py:30
  51.4 16.6 %collective-permute-start = (bf16[2,512,128]{2,1,0:T(8,128)(2,1)S(1)}, bf16[2,512,128]{2,1,0:T(8,128)(2,1)S(1)}, u32[]{:S(2)}, u32[]{:S(2)}) collective-permute-start(bf16[2,512,128]{2,1,0:T(8,128)(2,1)S(1)} %copy-done.10), channel_id=1, source_target_pairs={{0,1},{1,0},{2,3},{3,2},{4,5},{5,4},{6,7},{7,6},{8,9},{9,8},{10,11... | collective-permute-start | bytes 786440 | tf_op jit(solution)/shard_map/ppermute | solution.py:26
  70.3 7.8 %copy-start.2 = (bf16[4,4,3584]{2,1,0:T(4,128)(2,1)S(1)}, bf16[4,4,3584]{2,1,0:T(4,128)(2,1)}, u32[]{:S(2)}) copy-start(bf16[4,4,3584]{2,1,0:T(4,128)(2,1)} %param.27) | copy-start | bytes 344068
  74.2 29.6 %copy-start.6 = (f32[3584]{0:T(1024)S(1)}, f32[3584]{0:T(1024)}, u32[]{:S(2)}) copy-start(f32[3584]{0:T(1024)} %param.28) | copy-start | bytes 43012
  74.2 30.4 %copy-start.7 = (f32[4,4,8]{2,1,0:T(4,128)S(1)}, f32[4,4,8]{2,1,0:T(4,128)}, u32[]{:S(2)}) copy-start(f32[4,4,8]{2,1,0:T(4,128)} %param.30) | copy-start | bytes 1540
  74.2 30.4 %copy-start.4 = (s32[4,4,8]{2,1,0:T(4,128)S(1)}, s32[4,4,8]{2,1,0:T(4,128)}, u32[]{:S(2)}) copy-start(s32[4,4,8]{2,1,0:T(4,128)} %param.29) | copy-start | bytes 1540
  74.2 28.9 %all-to-all-start.2 = ((bf16[16,16,3584]{2,1,0:T(8,128)(2,1)}), bf16[16,16,3584]{2,1,0:T(8,128)(2,1)S(1)}, u32[]{:S(2)}, u32[]{:S(2)}) async-start(bf16[16,16,3584]{2,1,0:T(8,128)(2,1)} %bitcast.107), calls=%async_computation.2 | async-start | bytes 3670016 | tf_op jit(solution)/shard_map/all_to_all | solution.py:30
  78.1 101.8 %all-gather.2.cloned.1.call-start = ((), (), s32[]{:S(2)}) async-start(), calls=%async_computation.4 | async-start | bytes 14794752 | tf_op jit(solution)/shard_map/all_gather | solution.py:122
  187.2 21.1 %slice-start = ((s8[7340032]{0:T(1024)(128)(4,1)}), s8[4194304]{0:T(1024)(128)(4,1)S(1)}, s32[]{:S(2)}) async-start(s8[7340032]{0:T(1024)(128)(4,1)} %bitcast.123), calls=%async_computation.5 | async-start | bytes 8388608
  197.5 10.8 %slice-start.1 = ((s8[7340032]{0:T(1024)(128)(4,1)}), s8[3145728]{0:T(1024)(128)(4,1)S(1)}, s32[]{:S(2)}) async-start(s8[7340032]{0:T(1024)(128)(4,1)} %bitcast.123), calls=%async_computation.6 | async-start | bytes 6291456
  218.2 97.3 %all-to-all-start.3 = ((bf16[128,8,3584]{2,1,0:T(8,128)(2,1)}), bf16[128,8,3584]{2,1,0:T(8,128)(2,1)}, u32[]{:S(2)}, u32[]{:S(2)}) async-start(bf16[128,8,3584]{2,1,0:T(8,128)(2,1)} %fusion.7), calls=%async_computation.3 | async-start | bytes 14680064 | tf_op jit(solution)/shard_map/all_to_all | solution.py:142
  226.8 93.5 %copy-start.1 = (bf16[4,64,512]{2,1,0:T(8,128)(2,1)S(1)}, bf16[4,64,512]{2,1,0:T(8,128)(2,1)}, u32[]{:S(2)}) copy-start(bf16[4,64,512]{2,1,0:T(8,128)(2,1)} %param.22) | copy-start | bytes 786436
  (1 other events, 0.7 us)
Sparse Core Ops, SparseCore 0:
  104.8 75.0 all-gather.1

commit v2 on v1

--- a/solution.py
+++ b/solution.py
@@ -1,6 +1,11 @@
+import functools
+
 import jax
 import jax.numpy as jnp
+import numpy as np
 from jax import lax
+from jax.experimental import pallas as pl
+from jax.experimental.pallas import tpu as pltpu
 from jax.sharding import PartitionSpec as P
 
 D = 3584
@@ -10,6 +15,10 @@
 NOPE = 128
 VHEAD = 128
 MOST = 2
+TOP = 8
+BLOCK = 256
+SLOTS = 128
+BESIDE = 128
 STEPS = 4
 EXPERTS = 128
 LMAX = 64
@@ -20,6 +29,154 @@
 
 SAME_CORE = [[2 * chip + core for chip in range(CHIPS)] for core in range(2)]
 OTHER_CORE = [(i, i ^ 1) for i in range(2 * CHIPS)]
+PLANES = [
+    [y * 32 + first * unit + second * (10 - unit) + core for second in range(4) for y in range(4)]
+    for core, unit in ((0, 8), (1, 2))
+    for first in range(4)
+]
+
+
+SEATS = MOST * STEPS
+
+
+def place_of(axis):
+    group = lax.axis_index("ep")
+    return {"y": lax.axis_index("dp"), "x": group // 8, "z": group // 2 % 4}[axis]
+
+
+def shift(x, turn, by):
+    if turn == 2:
+        return lax.ppermute(x, "dp", [(i, (i + by) % 4) for i in range(4)])
+    pairs = []
+    for i in range(2 * CHIPS):
+        unit = 8 if i % 2 == turn else 2
+        pairs.append((i, i + ((i // unit + by) % 4 - i // unit % 4) * unit))
+    return lax.ppermute(x, "ep", pairs)
+
+
+def plane_exchange(x):
+    return lax.all_to_all(x, ("dp", "ep"), 0, 0, tiled=True, axis_index_groups=PLANES)
+
+
+def routing(expert_ids, gate_weights):
+    ids = jnp.swapaxes(expert_ids, 0, 1).reshape(RS, -1).astype(jnp.float32)
+    rest = jnp.swapaxes(gate_weights, 0, 1).reshape(RS, -1)
+    columns = [ids]
+    for _ in range(3):
+        columns.append(lax.reduce_precision(rest, 8, 7))
+        rest = rest - columns[-1]
+    columns = jnp.concatenate(columns, axis=1)
+    return jnp.pad(columns, ((0, 0), (0, BESIDE - columns.shape[1]))).astype(jnp.bfloat16)
+
+
+def pick_kernel(pieces, experts, *refs):
+    f32 = jnp.float32
+    count = sum(pieces) // BLOCK
+    columns, rows = refs[: len(pieces)], refs[len(pieces) : 2 * len(pieces)]
+    picked, put, weight = refs[-4:-2], refs[-2], refs[-1]
+
+    @pl.when(pl.program_id(0) == 0)
+    def _():
+        shape = (BLOCK, BLOCK)
+        this, other = (lax.broadcasted_iota(jnp.int32, shape, i) for i in (0, 1))
+        earlier = (
+            (this // RS == other // RS)
+            & (this % STEPS == other % STEPS)
+            & (this % RS // STEPS > other % RS // STEPS)
+        ).astype(jnp.bfloat16)
+        shape = (BLOCK, BESIDE)
+        row, lane = (lax.broadcasted_iota(jnp.int32, shape, i) for i in (0, 1))
+        base = (row // RS * SEATS + row % STEPS * MOST).astype(f32)
+        beside = jnp.concatenate([c[...] for c in columns], axis=0).astype(f32)
+        for block in range(count):
+            ids = beside[block * BLOCK : (block + 1) * BLOCK]
+            weights = sum(pltpu.roll(ids, BESIDE - i * TOP, 1) for i in (1, 2, 3))
+            for i in range(2):
+                same = (ids == experts[i].astype(f32)) & (lane < TOP)
+                amount = jnp.sum(jnp.where(same, weights, 0.0), axis=1, keepdims=True)
+                named = jnp.max(jnp.where(same, 1.0, 0.0), axis=1, keepdims=True)
+                named = jnp.broadcast_to(named, shape)
+                rank = jnp.dot(earlier, named.astype(jnp.bfloat16), preferred_element_type=f32)
+                seat = jnp.where(named > 0.0, rank + base, -1.0)
+                put[block, i] = jnp.where(seat == lane.astype(f32), 1.0, 0.0).astype(jnp.bfloat16)
+                weight[block, i] = jnp.broadcast_to(amount, shape)
+
+    x = jnp.concatenate([r[...] for r in rows], axis=0)
+    for block in range(count):
+        for i in range(2):
+            slots = lax.dot_general(
+                put[block, i],
+                x[block * BLOCK : (block + 1) * BLOCK],
+                (((0,), (0,)), ((), ())),
+                preferred_element_type=f32,
+            )
+            picked[i][block * SLOTS : (block + 1) * SLOTS] = slots.astype(jnp.bfloat16)
+
+
+def pick(experts, pieces, after=()):
+    sizes = tuple(p.shape[0] for p in pieces)
+    blocks = sum(sizes) // BLOCK
+    tile = 512
+    spec = pl.BlockSpec((blocks, 2, BLOCK, SLOTS), lambda i: (0, 0, 0, 0))
+    out = pl.BlockSpec((blocks * SLOTS, tile), lambda i: (0, i))
+    return pl.pallas_call(
+        functools.partial(pick_kernel, sizes),
+        grid=(D // tile,),
+        in_specs=[pl.BlockSpec(memory_space=pltpu.SMEM)]
+        + [pl.BlockSpec((n, BESIDE), lambda i: (0, D // BESIDE)) for n in sizes]
+        + [pl.BlockSpec((n, tile), lambda i: (0, i)) for n in sizes]
+        + [pl.BlockSpec(memory_space=pl.ANY) for _ in after],
+        out_specs=[out, out, spec, spec],
+        out_shape=[
+            jax.ShapeDtypeStruct((blocks * SLOTS, D), jnp.bfloat16),
+            jax.ShapeDtypeStruct((blocks * SLOTS, D), jnp.bfloat16),
+            jax.ShapeDtypeStruct((blocks, 2, BLOCK, SLOTS), jnp.bfloat16),
+            jax.ShapeDtypeStruct((blocks, 2, BLOCK, SLOTS), jnp.float32),
+        ],
+        compiler_params=pltpu.CompilerParams(vmem_limit_bytes=40 * 2**20),
+    )(experts, *pieces, *pieces, *after)
+
+
+def experts_kernel(own, twin, gate, upward, down, out, total):
+    f32 = jnp.float32
+    tile = pl.program_id(0)
+    half = own.shape[0]
+
+    @pl.when(tile == 0)
+    def _():
+        total[...] = jnp.zeros_like(total)
+
+    x = jnp.concatenate([own[...], twin[...]], axis=0)
+    g = jnp.dot(x, gate[0], preferred_element_type=f32)
+    u = jnp.dot(x, upward[0], preferred_element_type=f32)
+    inner = (g / (1.0 + jnp.exp(-g)) * u).astype(jnp.bfloat16)
+    total[...] += jnp.dot(inner, down[0], preferred_element_type=f32)
+
+    @pl.when(tile == pl.num_programs(0) - 1)
+    def _():
+        out[0] = total[:half].astype(jnp.bfloat16)
+        out[1] = total[half:].astype(jnp.bfloat16)
+
+
+def run_experts(own, twin, gate, upward, down, tile=256):
+    rows, hidden = own.shape[0], gate.shape[2]
+    whole = pl.BlockSpec((rows, D), lambda i: (0, 0))
+    return pl.pallas_call(
+        experts_kernel,
+        grid=(hidden // tile,),
+        in_specs=[
+            whole,
+            whole,
+            pl.BlockSpec((1, D, tile), lambda i: (0, 0, i)),
+            pl.BlockSpec((1, D, tile), lambda i: (0, 0, i)),
+            pl.BlockSpec((1, tile, D), lambda i: (0, i, 0)),
+        ],
+        out_specs=pl.BlockSpec((2, rows, D), lambda i: (0, 0, 0)),
+        out_shape=jax.ShapeDtypeStruct((2, rows, D), jnp.bfloat16),
+        scratch_shapes=[pltpu.VMEM((2 * rows, D), jnp.float32)],
+        compiler_params=pltpu.CompilerParams(vmem_limit_bytes=40 * 2**20),
+        cost_estimate=pl.CostEstimate(flops=rows * D, bytes_accessed=rows * D, transcendentals=0),
+    )(own, twin, gate, upward, down)
 
 
 def other_core(x):
@@ -76,11 +233,6 @@
     bf16 = jnp.bfloat16
     core = lax.axis_index("ep") % 2
     expert = lax.axis_index("dp") * lax.axis_size("ep") + lax.axis_index("ep")
-
-    ids = jnp.swapaxes(expert_ids, 0, 1).reshape(RS, -1)
-    weights = jnp.swapaxes(gate_weights, 0, 1).reshape(RS, -1)
-    meta = jnp.concatenate([ids.astype(f32), weights], axis=1)
-    meta = lax.all_gather(meta, ("dp", "ep"), axis=0, tiled=True)
 
     queries = jnp.concatenate([query_plain, query_rotary], axis=2)
     queries = queries.reshape(STEPS, CHIPS, 2, ROWS_DEV, 2 * (NOPE + ROPE))
@@ -119,40 +271,48 @@
         hidden * lax.rsqrt(jnp.mean(hidden * hidden, axis=-1, keepdims=True) + 1e-06) * norm_gain
     ).astype(bf16)
 
-    rows = lax.all_gather(normed, ("dp", "ep"), axis=0, tiled=True)
-    same = meta[:, :8] == expert.astype(f32)
-    weight = jnp.sum(jnp.where(same, meta[:, 8:], 0.0), axis=1)
-    named = jnp.any(same, axis=1).astype(jnp.int32).reshape(EXPERTS, ROWS_DEV, STEPS)
-    rank = jnp.cumsum(named, axis=1) - named
-    place = jnp.arange(EXPERTS, dtype=jnp.int32)[:, None, None] % 16 * (MOST * STEPS)
-    place = place + jnp.arange(STEPS, dtype=jnp.int32)[None, None, :] * MOST + rank
-    place = jnp.where(named > 0, place, -1).reshape(8, 1, 256)
-    pick = place == jnp.arange(128, dtype=jnp.int32)[None, :, None]
-    slot_weight = jnp.sum(jnp.where(pick, weight.reshape(8, 1, 256), 0.0), axis=2)
-    slots = jnp.einsum(
-        "tsr,trd->tsd", pick.astype(bf16), rows.reshape(8, 256, D), preferred_element_type=f32
+    pair = jnp.stack([expert, expert ^ 1])
+
+    def experts(own, twin):
+        return run_experts(own, other_core(twin), expert_gate, expert_up, expert_down)
+
+    def spread(put, weight, own, twin):
+        total = 0.0
+        for i, half in enumerate((own, twin)):
+            back = jnp.dot(put[i], half, preferred_element_type=f32)
+            total = total + back * weight[i, :, :1]
+        return total.astype(bf16)
+
+    rows = jnp.concatenate([normed, routing(expert_ids, gate_weights)], axis=1)
+    rows = plane_exchange(jnp.broadcast_to(rows[None], (16, RS, D + BESIDE)))
+    rows = rows.reshape(BLOCK, D + BESIDE)
+    half = BLOCK // 2
+    before = shift(rows, 0, 1)
+    after = shift(rows, 0, -1)
+    far = [shift(before[:half], 0, 1), shift(after[half:], 0, -1)]
+    own, twin, put, weight = pick(pair, [rows])
+    result = experts(own, twin)
+    own_sum = spread(put[0], weight[0], result[0], other_core(result[1]))
+    own, twin, put, weight = pick(pair, [after, before], [result])
+    result = experts(own, twin)
+    own, twin = result[0], other_core(result[1])
+    after, before = (
+        spread(put[i], weight[i], own[i * SLOTS :][:SLOTS], twin[i * SLOTS :][:SLOTS])
+        for i in range(2)
     )
-    slots = slots.astype(bf16).reshape(8 * 128, D)
-    gate = jnp.dot(slots, expert_gate[0], preferred_element_type=f32)
-    upward = jnp.dot(slots, expert_up[0], preferred_element_type=f32)
-    inner = (jax.nn.silu(gate) * upward).astype(bf16)
-    result = jnp.dot(inner, expert_down[0], preferred_element_type=f32)
-    result = (result * slot_weight.reshape(-1, 1)).astype(bf16)
-
-    back = lax.all_to_all(
-        result.reshape(EXPERTS, MOST * STEPS, D), ("dp", "ep"), 0, 0, tiled=True
-    ).reshape(EXPERTS * MOST * STEPS, D)
-    chosen = ids.reshape(ROWS_DEV, STEPS, -1)
-    earlier = jnp.tril(jnp.ones((ROWS_DEV, ROWS_DEV), jnp.int32), -1)
-    twins = jnp.any(chosen[:, None, :, :, None] == chosen[None, :, :, None, :], axis=-1)
-    rank = jnp.sum(twins.astype(jnp.int32) * earlier[:, :, None, None], axis=1)
-    target = chosen * (MOST * STEPS) + rank
-    target = target + jnp.arange(STEPS, dtype=jnp.int32)[None, :, None] * MOST
-    target = target.reshape(RS, -1, 1)
-    slot_index = jnp.arange(EXPERTS * MOST * STEPS, dtype=jnp.int32)
-    take = jnp.any(target == slot_index[None, None, :], axis=1).astype(bf16)
-    routed = jnp.dot(take, back, preferred_element_type=f32)
-    out = (hidden + routed).astype(bf16)
+    own, twin, put, weight = pick(pair, far, [result])
+    result = experts(own, twin)
+    far = spread(put[0], weight[0], result[0], other_core(result[1]))
+
+    up = shift(far[:half], 0, 1)
+    down = shift(far[half:], 0, -1)
+    after = jnp.concatenate([after[:half] + up, after[half:]], axis=0)
+    before = jnp.concatenate([before[:half], before[half:] + down], axis=0)
+    after = shift(after, 0, 1)
+    before = shift(before, 0, -1)
+    total = own_sum.astype(f32) + after.astype(f32) + before.astype(f32)
+    routed = plane_exchange(total.astype(bf16).reshape(16, RS, D))
+    out = (hidden + jnp.sum(routed.astype(f32), axis=0)).astype(bf16)
     return jnp.swapaxes(out.reshape(ROWS_DEV, STEPS, D), 0, 1)
 
 

time: 329 us -> 269 us (0.82)
  waiting for transfers between devices: 187 us -> 103 us
  Pallas kernels: 0 us -> 49.7 us
  matrix products: 51.8 us -> 14 us
  blocking collectives: 34.7 us -> 54.9 us
  between operations: 14 us -> 0.81 us
  starting transfers between devices: 24.9 us -> 30.3 us
  local copies, waits for them, and re-layouts: 6.46 us -> 11.3 us
    all_to_all x1 -> x0, waiting for transfers between devices: 86.9 us -> none  [per_device(): lax.all_to_all(result.reshape(EXPERTS, MOST * STEPS, D), ('dp', 'ep'), 0,...]
    all_to_all x0 -> x2, blocking collectives: none -> 54.9 us  [plane_exchange(): lax.all_to_all(x, ('dp', 'ep'), 0, 0, tiled=True, axis_index_groups=PLANES)]
    pallas_call x0 -> x6, Pallas kernels: none -> 49.7 us  [the longest x3 36.6 us: run_experts(): pl.pallas_call(experts_kernel, grid=(hidden // tile,), in_specs=[whole, w...]
    all_gather x1 -> x0, waiting for transfers between devices: 37.6 us -> none  [per_device(): rows = lax.all_gather(normed, ('dp', 'ep'), axis=0, tiled=True)]
    dot_general x5 -> x8, matrix products: 42.4 us -> 5.48 us  [spread(): back = jnp.dot(put[i], half, preferred_element_type=f32)]
    all_gather x1 -> x0, blocking collectives: 34.7 us -> none  [per_device(): meta = lax.all_gather(meta, ('dp', 'ep'), axis=0, tiled=True)]
    ppermute x0 -> x8, waiting for transfers between devices: none -> 32.1 us  [shift(): return lax.ppermute(x, 'ep', pairs)]
    ppermute x0 -> x8, starting transfers between devices: none -> 12.5 us  [shift(): return lax.ppermute(x, 'ep', pairs)]
  transfers between devices with their start and end apart: 9 -> 21, of which waited for: 6 -> 12; matrix products, arithmetic and copies ran while one was open for 4% -> 6% of each run, Pallas kernels for 0% -> 11%
where the time goes in v2:
time: 269 us
  waiting for transfers between devices  103 us (38%)
  blocking collectives  54.9 us (20%)
  Pallas kernels  49.7 us (18%)
  starting transfers between devices  30.3 us (11%)
  matrix products  14 us (5%)
  local copies, waits for them, and re-layouts  11.3 us (4%)
  other arithmetic  4.56 us (2%)
    all_to_all x3, waiting for transfers between devices, exchange(): lax.all_to_all(x, 'ep', 0, 0, tiled=True, axis_index_groups=SAME_CORE)  61.8 us
    all_to_all x2, blocking collectives, plane_exchange(): lax.all_to_all(x, ('dp', 'ep'), 0, 0, tiled=True, axis_index_groups=PLANES)  54.9 us
    pallas_call x3, Pallas kernels, run_experts(): pl.pallas_call(experts_kernel, grid=(hidden // tile,), in_specs=[whole, w...  36.6 us
    ppermute x8, waiting for transfers between devices, shift(): return lax.ppermute(x, 'ep', pairs)  32.1 us
    all_to_all x3, starting transfers between devices, exchange(): lax.all_to_all(x, 'ep', 0, 0, tiled=True, axis_index_groups=SAME_CORE)  15.6 us
    pallas_call x3, Pallas kernels, pick(): pl.pallas_call(functools.partial(pick_kernel, sizes), grid=(D // tile,),...  13.1 us
    ppermute x8, starting transfers between devices, shift(): return lax.ppermute(x, 'ep', pairs)  12.5 us
    ppermute x10, waiting for transfers between devices, other_core(): return lax.ppermute(x, 'ep', OTHER_CORE)  9.24 us
  transfers between devices with their start and end apart: 21, of which 12 were waited for; matrix products, arithmetic and copies ran while one was open for 6% of the time, Pallas kernels for 11%

profile of v2, /device:TPU:0, one launch (start us, length us, event | category | flops | bytes accessed | tf_op | source)
XLA Modules:
  0.0 268.7 jit_solution(11855730973389754825)
XLA Ops:
  6.2 8.1 %all-to-all-start = ((bf16[16,4,16,576]{3,2,1,0:T(8,128)(2,1)}), bf16[16,4,16,576]{3,2,1,0:T(8,128)(2,1)S(1)}, u32[]{:S(2)}, u32[]{:S(2)}) async-start(bf16[16,4,16,576]{3,2,1,0:T(8,128)(2,1)} %pad_maximum_fusion.2), calls=%async_computation | async-start | bytes 2621440 | tf_op jit(solution)/shard_map/all_to_all | solution.py:187
  14.5 20.9 %all-to-all-done = bf16[16,4,16,576]{3,2,1,0:T(8,128)(2,1)S(1)} async-done(((bf16[16,4,16,576]{3,2,1,0:T(8,128)(2,1)}), bf16[16,4,16,576]{3,2,1,0:T(8,128)(2,1)S(1)}, u32[]{:S(2)}, u32[]{:S(2)}) %all-to-all-start) | async-done | bytes 1179680 | tf_op jit(solution)/shard_map/all_to_all | solution.py:187
  40.8 3.7 %all-to-all-start.1 = ((bf16[16,4,16,512]{3,2,1,0:T(8,128)(2,1)}), bf16[16,4,16,512]{3,2,1,0:T(8,128)(2,1)S(1)}, u32[]{:S(2)}, u32[]{:S(2)}) async-start(bf16[16,4,16,512]{3,2,1,0:T(8,128)(2,1)} %copy.86), calls=%async_computation.1 | async-start | bytes 2097152 | tf_op jit(solution)/shard_map/all_to_all | solution.py:187
  44.6 15.7 %all-to-all-done.1 = bf16[16,4,16,512]{3,2,1,0:T(8,128)(2,1)S(1)} async-done(((bf16[16,4,16,512]{3,2,1,0:T(8,128)(2,1)}), bf16[16,4,16,512]{3,2,1,0:T(8,128)(2,1)S(1)}, u32[]{:S(2)}, u32[]{:S(2)}) %all-to-all-start.1) | async-done | bytes 1048608 | tf_op jit(solution)/shard_map/all_to_all | solution.py:187
  61.7 3.9 %convolution_convert_fusion = bf16[256,3584]{1,0:T(8,128)(2,1)} fusion(bf16[256,3584]{1,0:T(8,128)(2,1)} %collective-permute-done.3, bf16[256,3584]{1,0:T(8,128)(2,1)S(1)} %copy-done.11, bf16[32,8,4,128]{3,2,1,0:T(4,128)(2,1)S(1)} %bitcast.142), kind=kOutput, calls=%fused_computation.19 | convolution fusion | flops 947781632 | bytes 5767168 | tf_op jit(solution)/shard_map/dot_general | solution.py:266
  65.5 3.8 %all-to-all-start.2 = ((bf16[16,16,3584]{2,1,0:T(8,128)(2,1)}), bf16[16,16,3584]{2,1,0:T(8,128)(2,1)S(1)}, u32[]{:S(2)}, u32[]{:S(2)}) async-start(bf16[16,16,3584]{2,1,0:T(8,128)(2,1)} %bitcast.135), calls=%async_computation.2 | async-start | bytes 3670016 | tf_op jit(solution)/shard_map/all_to_all | solution.py:187
  69.7 25.2 %all-to-all-done.2 = bf16[16,16,3584]{2,1,0:T(8,128)(2,1)S(1)} async-done(((bf16[16,16,3584]{2,1,0:T(8,128)(2,1)}), bf16[16,16,3584]{2,1,0:T(8,128)(2,1)S(1)}, u32[]{:S(2)}, u32[]{:S(2)}) %all-to-all-start.2) | async-done | bytes 1835040 | tf_op jit(solution)/shard_map/all_to_all | solution.py:187
  95.7 27.4 %all_to_all.25 = bf16[16,16,3712]{2,1,0:T(8,128)(2,1)S(1)} all-to-all(bf16[16,16,3712]{2,1,0:T(8,128)(2,1)S(1)} %broadcast_in_dim.30), channel_id=1, replica_groups={{0,32,64,96,2,34,66,98,4,36,68,100,6,38,70,102},{8,40,72,104,10,42,74,1..., dimensions={0} | all-to-all | bytes 3801088 | tf_op jit(solution)/shard_map/all_to_all | solution.py:58
  123.1 2.5 collective-permute-start.6
  125.7 3.2 %shard_map.163 = (bf16[128,3584]{1,0:T(8,128)(2,1)S(1)}, bf16[128,3584]{1,0:T(8,128)(2,1)S(1)}, bf16[1,2,256,128]{3,2,1,0:T(8,128)(2,1)S(1)}, f32[1,2,256,128]{3,2,1,0:T(8,128)S(1)}) custom-call(s32[2]{0:T(128)S(1)} %pad_add_fusion.experts, bf16[256,3712]{1,0:T(8,128)(2,1)S(1)} %bitcast.130, bf16[256,3712]{1,0:T(8,128)(2,1)S(1)} %bitcast.131), custom_call_target="tpu_custom_call" | custom-call | tf_op jit(solution)/shard_map/pallas_call | solution.py:122
  129.2 2.5 collective-permute-done.4.twin
  131.7 3.1 %copy-done.2 = bf16[1,3584,1024]{2,1,0:T(8,128)(2,1)S(1)} copy-done((bf16[1,3584,1024]{2,1,0:T(8,128)(2,1)S(1)}, bf16[1,3584,1024]{2,1,0:T(8,128)(2,1)}, u32[]{:S(2)}) %copy-start.2) | copy-done | bytes 7340056
  134.7 10.4 %shard_map.164.refs_4_ = bf16[2,128,3584]{2,1,0:T(8,128)(2,1)S(1)} custom-call(bf16[128,3584]{1,0:T(8,128)(2,1)S(1)} %get-tuple-element.18.own, bf16[128,3584]{1,0:T(8,128)(2,1)S(1)} %collective-permute-done.4.twin, bf16[1,3584,1024]{2,1,0:T(8,128)(2,1)S(1)} %copy-done.2, bf16[1,3584,1024]{2,1,0:T(8,128)(2,1)} %upward.5, bf16[1,1024,3584]{2,1,0:T(8,128)(2,1)} %down.5), custom_call_target="tpu_custom_call" | custom-call | flops 458752 | bytes 458752 | tf_op jit(solution)/shard_map/pallas_call | solution.py:164
  147.1 3.7 %collective-permute-done.7.refs_1_.refs_3_ = bf16[256,3712]{1,0:T(8,128)(2,1)} collective-permute-done((bf16[256,3712]{1,0:T(8,128)(2,1)S(1)}, bf16[256,3712]{1,0:T(8,128)(2,1)}, u32[]{:S(2)}, u32[]{:S(2)}) %collective-permute-start.7) | collective-permute-done | bytes 1900576 | tf_op jit(solution)/shard_map/ppermute | solution.py:54
  150.8 6.3 %shard_map.165 = (bf16[256,3584]{1,0:T(8,128)(2,1)S(1)}, bf16[256,3584]{1,0:T(8,128)(2,1)S(1)}, bf16[2,2,256,128]{3,2,1,0:T(8,128)(2,1)S(1)}, f32[2,2,256,128]{3,2,1,0:T(8,128)S(1)}) custom-call(s32[2]{0:T(128)S(1)} %pad_add_fusion.experts, bf16[256,3712]{1,0:T(8,128)(2,1)} %collective-permute-done.6.refs_0_.refs_2_, ...), custom_call_target="tpu_custom_call" | custom-call | tf_op jit(solution)/shard_map/pallas_call | solution.py:122
  159.9 3.3 %collective-permute-start.11 = (bf16[128,3712]{1,0:T(8,128)(2,1)S(1)}, bf16[128,3712]{1,0:T(8,128)(2,1)S(1)}, u32[]{:S(2)}, u32[]{:S(2)}) collective-permute-start(bf16[128,3712]{1,0:T(8,128)(2,1)S(1)} %slice.206), channel_id=1, source_target_pairs={{0,24},{1,7},{2,26},{3,1},{4,28},{5,3},{6,30},{7,5},{8,0},{9,15},{... | collective-permute-start | bytes 2850824 | tf_op jit(solution)/shard_map/ppermute | solution.py:54
  163.2 15.8 %shard_map.166.refs_4_ = bf16[2,256,3584]{2,1,0:T(8,128)(2,1)S(1)} custom-call(bf16[256,3584]{1,0:T(8,128)(2,1)S(1)} %get-tuple-element.22.own, bf16[256,3584]{1,0:T(8,128)(2,1)S(1)} %collective-permute-done.8.twin, bf16[1,3584,1024]{2,1,0:T(8,128)(2,1)} %gate.5, bf16[1,3584,1024]{2,1,0:T(8,128)(2,1)} %upward.5, bf16[1,1024,3584]{2,1,0:T(8,128)(2,1)} %down.5), custom_call_target="tpu_custom_call" | custom-call | flops 917504 | bytes 917504 | tf_op jit(solution)/shard_map/pallas_call | solution.py:164
  179.0 3.5 %shard_map.167 = (bf16[128,3584]{1,0:T(8,128)(2,1)S(1)}, bf16[128,3584]{1,0:T(8,128)(2,1)S(1)}, bf16[1,2,256,128]{3,2,1,0:T(8,128)(2,1)S(1)}, f32[1,2,256,128]{3,2,1,0:T(8,128)S(1)}) custom-call(s32[2]{0:T(128)S(1)} %pad_add_fusion.experts, bf16[128,3712]{1,0:T(8,128)(2,1)S(1)} %collective-permute-done.10.refs_0_.refs_2_, ...), custom_call_target="tpu_custom_call" | custom-call | tf_op jit(solution)/shard_map/pallas_call | solution.py:122
  185.1 10.4 %shard_map.168 = bf16[2,128,3584]{2,1,0:T(8,128)(2,1)S(1)} custom-call(bf16[128,3584]{1,0:T(8,128)(2,1)S(1)} %get-tuple-element.26.own, bf16[128,3584]{1,0:T(8,128)(2,1)S(1)} %collective-permute-done.12.twin, bf16[1,3584,1024]{2,1,0:T(8,128)(2,1)S(1)} %bitcast.127, bf16[1,3584,1024]{2,1,0:T(8,128)(2,1)} %upward.5, bf16[1,1024,3584]{2,1,0:T(8,128)(2,1)} %down.5), custom_call_target="tpu_custom_call" | custom-call | flops 458752 | bytes 458752 | tf_op jit(solution)/shard_map/pallas_call | solution.py:164
  199.6 3.2 %collective-permute-start.16 = (bf16[128,3584]{1,0:T(8,128)(2,1)S(1)}, bf16[128,3584]{1,0:T(8,128)(2,1)S(1)}, u32[]{:S(2)}, u32[]{:S(2)}) collective-permute-start(bf16[128,3584]{1,0:T(8,128)(2,1)S(1)} %get-tuple-element.40), channel_id=1, source_target_pairs={{0,24},{1,7},{2,26},{3,1},{4,28},{5,3},{6,30},{7,5},{8,0},{9,15},{... | collective-permute-start | bytes 2752520 | tf_op jit(solution)/shard_map/ppermute | solution.py:54
  205.4 8.8 %collective-permute-done.14 = bf16[128,3584]{1,0:T(8,128)(2,1)S(1)} collective-permute-done((bf16[128,3584]{1,0:T(8,128)(2,1)S(1)}, bf16[128,3584]{1,0:T(8,128)(2,1)S(1)}, u32[]{:S(2)}, u32[]{:S(2)}) %collective-permute-start.14) | collective-permute-done | bytes 917536 | tf_op jit(solution)/shard_map/ppermute | solution.py:54
  214.9 3.3 %collective-permute-start.17 = (bf16[256,3584]{1,0:T(8,128)(2,1)S(1)}, bf16[256,3584]{1,0:T(8,128)(2,1)S(1)}, u32[]{:S(2)}, u32[]{:S(2)}) collective-permute-start(bf16[256,3584]{1,0:T(8,128)(2,1)S(1)} %pad_maximum_fusion.1), channel_id=1, source_target_pairs={{0,24},{1,7},{2,26},{3,1},{4,28},{5,3},{6,30},{7,5},{8,0},{9,15},{... | collective-permute-start | bytes 5505032 | tf_op jit(solution)/shard_map/ppermute | solution.py:54
  221.4 17.6 %collective-permute-done.15 = bf16[256,3584]{1,0:T(8,128)(2,1)S(1)} collective-permute-done((bf16[256,3584]{1,0:T(8,128)(2,1)S(1)}, bf16[256,3584]{1,0:T(8,128)(2,1)S(1)}, u32[]{:S(2)}, u32[]{:S(2)}) %collective-permute-start.15) | collective-permute-done | bytes 1835040 | tf_op jit(solution)/shard_map/ppermute | solution.py:54
  240.1 27.5 %all_to_all.26 = bf16[16,16,3584]{2,1,0:T(8,128)(2,1)S(1)} all-to-all(bf16[16,16,3584]{2,1,0:T(8,128)(2,1)S(1)} %bitcast.134), channel_id=1, replica_groups={{0,32,64,96,2,34,66,98,4,36,68,100,6,38,70,102},{8,40,72,104,10,42,74,1..., dimensions={0} | all-to-all | bytes 3670016 | tf_op jit(solution)/shard_map/all_to_all | solution.py:58
  (143 shorter events, 34.0 us)
Async XLA Ops:
  0.0 37.7 %copy-start = (bf16[4,64,512]{2,1,0:T(8,128)(2,1)S(1)}, bf16[4,64,512]{2,1,0:T(8,128)(2,1)}, u32[]{:S(2)}) copy-start(bf16[4,64,512]{2,1,0:T(8,128)(2,1)} %param.22) | copy-start | bytes 786436
  1.4 1.5 collective-permute-start.2
  1.5 2.4 collective-permute-start.1
  4.9 30.4 %copy-start.14 = (bf16[4,4,64]{2,1,0:T(4,128)(2,1)S(1)}, bf16[4,4,64]{2,1,0:T(4,128)(2,1)}, u32[]{:S(2)}) copy-start(bf16[4,4,64]{2,1,0:T(4,128)(2,1)} %param.26) | copy-start | bytes 6148
  6.2 30.1 %copy-start.7 = (bf16[4,4,512]{2,1,0:T(4,128)(2,1)S(1)}, bf16[4,4,512]{2,1,0:T(4,128)(2,1)}, u32[]{:S(2)}) copy-start(bf16[4,4,512]{2,1,0:T(4,128)(2,1)} %param.25) | copy-start | bytes 49156
  6.2 29.2 %all-to-all-start = ((bf16[16,4,16,576]{3,2,1,0:T(8,128)(2,1)}), bf16[16,4,16,576]{3,2,1,0:T(8,128)(2,1)S(1)}, u32[]{:S(2)}, u32[]{:S(2)}) async-start(bf16[16,4,16,576]{3,2,1,0:T(8,128)(2,1)} %pad_maximum_fusion.2), calls=%async_computation | async-start | bytes 2621440 | tf_op jit(solution)/shard_map/all_to_all | solution.py:187
  14.3 47.4 %collective-permute-start.3 = (bf16[256,3584]{1,0:T(8,128)(2,1)S(1)}, bf16[256,3584]{1,0:T(8,128)(2,1)}, u32[]{:S(2)}, u32[]{:S(2)}) collective-permute-start(bf16[256,3584]{1,0:T(8,128)(2,1)S(1)} %copy-done.11), channel_id=1, source_target_pairs={{0,1},{1,0},{2,3},{3,2},{4,5},{5,4},{6,7},{7,6},{8,9},{9,8},{10,11... | collective-permute-start | bytes 5505032 | tf_op jit(solution)/shard_map/ppermute | solution.py:183
  40.8 19.6 %all-to-all-start.1 = ((bf16[16,4,16,512]{3,2,1,0:T(8,128)(2,1)}), bf16[16,4,16,512]{3,2,1,0:T(8,128)(2,1)S(1)}, u32[]{:S(2)}, u32[]{:S(2)}) async-start(bf16[16,4,16,512]{3,2,1,0:T(8,128)(2,1)} %copy.86), calls=%async_computation.1 | async-start | bytes 2097152 | tf_op jit(solution)/shard_map/all_to_all | solution.py:187
  44.6 16.4 %collective-permute-start = (bf16[2,512,128]{2,1,0:T(8,128)(2,1)S(1)}, bf16[2,512,128]{2,1,0:T(8,128)(2,1)S(1)}, u32[]{:S(2)}, u32[]{:S(2)}) collective-permute-start(bf16[2,512,128]{2,1,0:T(8,128)(2,1)S(1)} %copy-done.13), channel_id=1, source_target_pairs={{0,1},{1,0},{2,3},{3,2},{4,5},{5,4},{6,7},{7,6},{8,9},{9,8},{10,11... | collective-permute-start | bytes 786440 | tf_op jit(solution)/shard_map/ppermute | solution.py:183
  65.5 29.3 %all-to-all-start.2 = ((bf16[16,16,3584]{2,1,0:T(8,128)(2,1)}), bf16[16,16,3584]{2,1,0:T(8,128)(2,1)S(1)}, u32[]{:S(2)}, u32[]{:S(2)}) async-start(bf16[16,16,3584]{2,1,0:T(8,128)(2,1)} %bitcast.135), calls=%async_computation.2 | async-start | bytes 3670016 | tf_op jit(solution)/shard_map/all_to_all | solution.py:187
  123.1 24.0 %collective-permute-start.6 = (bf16[256,3712]{1,0:T(8,128)(2,1)S(1)}, bf16[256,3712]{1,0:T(8,128)(2,1)}, u32[]{:S(2)}, u32[]{:S(2)}) collective-permute-start(bf16[256,3712]{1,0:T(8,128)(2,1)S(1)} %bitcast.128), channel_id=1, source_target_pairs={{0,24},{1,7},{2,26},{3,1},{4,28},{5,3},{6,30},{7,5},{8,0},{9,15},{... | collective-permute-start | bytes 5701640 | tf_op jit(solution)/shard_map/ppermute | solution.py:54
  125.6 25.2 %collective-permute-start.7 = (bf16[256,3712]{1,0:T(8,128)(2,1)S(1)}, bf16[256,3712]{1,0:T(8,128)(2,1)}, u32[]{:S(2)}, u32[]{:S(2)}) collective-permute-start(bf16[256,3712]{1,0:T(8,128)(2,1)S(1)} %bitcast.129), channel_id=1, source_target_pairs={{0,8},{1,3},{2,10},{3,5},{4,12},{5,7},{6,14},{7,1},{8,16},{9,11},{... | collective-permute-start | bytes 5701640 | tf_op jit(solution)/shard_map/ppermute | solution.py:54
  128.9 2.7 %collective-permute-start.4 = (bf16[128,3584]{1,0:T(8,128)(2,1)S(1)}, bf16[128,3584]{1,0:T(8,128)(2,1)S(1)}, u32[]{:S(2)}, u32[]{:S(2)}) collective-permute-start(bf16[128,3584]{1,0:T(8,128)(2,1)S(1)} %get-tuple-element.19), channel_id=1, source_target_pairs={{0,1},{1,0},{2,3},{3,2},{4,5},{5,4},{6,7},{7,6},{8,9},{9,8},{10,11... | collective-permute-start | bytes 2752520 | tf_op jit(solution)/shard_map/ppermute | solution.py:183
  157.2 6.0 %collective-permute-start.8 = (bf16[256,3584]{1,0:T(8,128)(2,1)S(1)}, bf16[256,3584]{1,0:T(8,128)(2,1)S(1)}, u32[]{:S(2)}, u32[]{:S(2)}) collective-permute-start(bf16[256,3584]{1,0:T(8,128)(2,1)S(1)} %get-tuple-element.23), channel_id=1, source_target_pairs={{0,1},{1,0},{2,3},{3,2},{4,5},{5,4},{6,7},{7,6},{8,9},{9,8},{10,11... | collective-permute-start | bytes 5505032 | tf_op jit(solution)/shard_map/ppermute | solution.py:183
  158.6 20.4 %collective-permute-start.10 = (bf16[128,3712]{1,0:T(8,128)(2,1)S(1)}, bf16[128,3712]{1,0:T(8,128)(2,1)S(1)}, u32[]{:S(2)}, u32[]{:S(2)}) collective-permute-start(bf16[128,3712]{1,0:T(8,128)(2,1)S(1)} %slice.205), channel_id=1, source_target_pairs={{0,8},{1,3},{2,10},{3,5},{4,12},{5,7},{6,14},{7,1},{8,16},{9,11},{... | collective-permute-start | bytes 2850824 | tf_op jit(solution)/shard_map/ppermute | solution.py:54
  159.9 19.1 %collective-permute-start.11 = (bf16[128,3712]{1,0:T(8,128)(2,1)S(1)}, bf16[128,3712]{1,0:T(8,128)(2,1)S(1)}, u32[]{:S(2)}, u32[]{:S(2)}) collective-permute-start(bf16[128,3712]{1,0:T(8,128)(2,1)S(1)} %slice.206), channel_id=1, source_target_pairs={{0,24},{1,7},{2,26},{3,1},{4,28},{5,3},{6,30},{7,5},{8,0},{9,15},{... | collective-permute-start | bytes 2850824 | tf_op jit(solution)/shard_map/ppermute | solution.py:54
  182.5 2.6 collective-permute-start.12
  195.6 2.6 collective-permute-start.13
  195.9 6.9 %collective-permute-start.9 = (bf16[256,3584]{1,0:T(8,128)(2,1)S(1)}, bf16[256,3584]{1,0:T(8,128)(2,1)S(1)}, u32[]{:S(2)}, u32[]{:S(2)}) collective-permute-start(bf16[256,3584]{1,0:T(8,128)(2,1)S(1)} %slice_bitcast_fusion), channel_id=1, source_target_pairs={{0,1},{1,0},{2,3},{3,2},{4,5},{5,4},{6,7},{7,6},{8,9},{9,8},{10,11... | collective-permute-start | bytes 5505032 | tf_op jit(solution)/shard_map/ppermute | solution.py:183
  199.5 14.7 %collective-permute-start.14 = (bf16[128,3584]{1,0:T(8,128)(2,1)S(1)}, bf16[128,3584]{1,0:T(8,128)(2,1)S(1)}, u32[]{:S(2)}, u32[]{:S(2)}) collective-permute-start(bf16[128,3584]{1,0:T(8,128)(2,1)S(1)} %get-tuple-element.39), channel_id=1, source_target_pairs={{0,8},{1,3},{2,10},{3,5},{4,12},{5,7},{6,14},{7,1},{8,16},{9,11},{... | collective-permute-start | bytes 2752520 | tf_op jit(solution)/shard_map/ppermute | solution.py:54
  199.6 15.0 %collective-permute-start.16 = (bf16[128,3584]{1,0:T(8,128)(2,1)S(1)}, bf16[128,3584]{1,0:T(8,128)(2,1)S(1)}, u32[]{:S(2)}, u32[]{:S(2)}) collective-permute-start(bf16[128,3584]{1,0:T(8,128)(2,1)S(1)} %get-tuple-element.40), channel_id=1, source_target_pairs={{0,24},{1,7},{2,26},{3,1},{4,28},{5,3},{6,30},{7,5},{8,0},{9,15},{... | collective-permute-start | bytes 2752520 | tf_op jit(solution)/shard_map/ppermute | solution.py:54
  214.5 24.5 %collective-permute-start.15 = (bf16[256,3584]{1,0:T(8,128)(2,1)S(1)}, bf16[256,3584]{1,0:T(8,128)(2,1)S(1)}, u32[]{:S(2)}, u32[]{:S(2)}) collective-permute-start(bf16[256,3584]{1,0:T(8,128)(2,1)S(1)} %pad_maximum_fusion), channel_id=1, source_target_pairs={{0,8},{1,3},{2,10},{3,5},{4,12},{5,7},{6,14},{7,1},{8,16},{9,11},{... | collective-permute-start | bytes 5505032 | tf_op jit(solution)/shard_map/ppermute | solution.py:54
  214.9 24.1 %collective-permute-start.17 = (bf16[256,3584]{1,0:T(8,128)(2,1)S(1)}, bf16[256,3584]{1,0:T(8,128)(2,1)S(1)}, u32[]{:S(2)}, u32[]{:S(2)}) collective-permute-start(bf16[256,3584]{1,0:T(8,128)(2,1)S(1)} %pad_maximum_fusion.1), channel_id=1, source_target_pairs={{0,24},{1,7},{2,26},{3,1},{4,28},{5,3},{6,30},{7,5},{8,0},{9,15},{... | collective-permute-start | bytes 5505032 | tf_op jit(solution)/shard_map/ppermute | solution.py:54
  218.2 2.6 collective-permute-start.5
  (15 other events, 184.0 us)

commit v3 on v2

--- a/solution.py
+++ b/solution.py
@@ -22,6 +22,7 @@
 STEPS = 4
 EXPERTS = 128
 LMAX = 64
+KEYS = 128
 ROWS_DEV = 4
 CHIPS = 16
 HC = 4
@@ -73,7 +74,7 @@
     f32 = jnp.float32
     count = sum(pieces) // BLOCK
     columns, rows = refs[: len(pieces)], refs[len(pieces) : 2 * len(pieces)]
-    picked, put, weight = refs[-4:-2], refs[-2], refs[-1]
+    *picked, put, weight, turned = refs[-5:]
 
     @pl.when(pl.program_id(0) == 0)
     def _():
@@ -99,15 +100,17 @@
                 rank = jnp.dot(earlier, named.astype(jnp.bfloat16), preferred_element_type=f32)
                 seat = jnp.where(named > 0.0, rank + base, -1.0)
                 put[block, i] = jnp.where(seat == lane.astype(f32), 1.0, 0.0).astype(jnp.bfloat16)
+                seat = jnp.transpose(seat)
+                slot = lax.broadcasted_iota(jnp.int32, seat.shape, 0).astype(f32)
+                turned[block, i] = jnp.where(seat == slot, 1.0, 0.0).astype(jnp.bfloat16)
                 weight[block, i] = jnp.broadcast_to(amount, shape)
 
     x = jnp.concatenate([r[...] for r in rows], axis=0)
     for block in range(count):
         for i in range(2):
-            slots = lax.dot_general(
-                put[block, i],
+            slots = jnp.dot(
+                turned[block, i],
                 x[block * BLOCK : (block + 1) * BLOCK],
-                (((0,), (0,)), ((), ())),
                 preferred_element_type=f32,
             )
             picked[i][block * SLOTS : (block + 1) * SLOTS] = slots.astype(jnp.bfloat16)
@@ -116,7 +119,7 @@
 def pick(experts, pieces, after=()):
     sizes = tuple(p.shape[0] for p in pieces)
     blocks = sum(sizes) // BLOCK
-    tile = 512
+    tile = 1792
     spec = pl.BlockSpec((blocks, 2, BLOCK, SLOTS), lambda i: (0, 0, 0, 0))
     out = pl.BlockSpec((blocks * SLOTS, tile), lambda i: (0, i))
     return pl.pallas_call(
@@ -133,11 +136,12 @@
             jax.ShapeDtypeStruct((blocks, 2, BLOCK, SLOTS), jnp.bfloat16),
             jax.ShapeDtypeStruct((blocks, 2, BLOCK, SLOTS), jnp.float32),
         ],
+        scratch_shapes=[pltpu.VMEM((blocks, 2, SLOTS, BLOCK), jnp.bfloat16)],
         compiler_params=pltpu.CompilerParams(vmem_limit_bytes=40 * 2**20),
     )(experts, *pieces, *pieces, *after)
 
 
-def experts_kernel(own, twin, gate, upward, down, out, total):
+def experts_kernel(own, twin, gate, upward, down, own_out, twin_out, total):
     f32 = jnp.float32
     tile = pl.program_id(0)
     half = own.shape[0]
@@ -154,8 +158,8 @@
 
     @pl.when(tile == pl.num_programs(0) - 1)
     def _():
-        out[0] = total[:half].astype(jnp.bfloat16)
-        out[1] = total[half:].astype(jnp.bfloat16)
+        own_out[...] = total[:half].astype(jnp.bfloat16)
+        twin_out[...] = total[half:].astype(jnp.bfloat16)
 
 
 def run_experts(own, twin, gate, upward, down, tile=256):
@@ -171,14 +175,38 @@
             pl.BlockSpec((1, D, tile), lambda i: (0, 0, i)),
             pl.BlockSpec((1, tile, D), lambda i: (0, i, 0)),
         ],
-        out_specs=pl.BlockSpec((2, rows, D), lambda i: (0, 0, 0)),
-        out_shape=jax.ShapeDtypeStruct((2, rows, D), jnp.bfloat16),
+        out_specs=[whole, whole],
+        out_shape=[jax.ShapeDtypeStruct((rows, D), jnp.bfloat16)] * 2,
         scratch_shapes=[pltpu.VMEM((2 * rows, D), jnp.float32)],
         compiler_params=pltpu.CompilerParams(vmem_limit_bytes=40 * 2**20),
         cost_estimate=pl.CostEstimate(flops=rows * D, bytes_accessed=rows * D, transcendentals=0),
     )(own, twin, gate, upward, down)
 
 
+def spread_kernel(put, weight, own, twin, low, high):
+    total = 0.0
+    for i, half in enumerate((own, twin)):
+        back = jnp.dot(put[0, i], half[...], preferred_element_type=jnp.float32)
+        total = total + back * weight[0, i, :, :1]
+    total = total.astype(jnp.bfloat16)
+    low[...] = total[: BLOCK // 2]
+    high[...] = total[BLOCK // 2 :]
+
+
+def spread(put, weight, own, twin):
+    tile = 1792
+    table = pl.BlockSpec((1, 2, BLOCK, SLOTS), lambda i: (0, 0, 0, 0))
+    columns = pl.BlockSpec((SLOTS, tile), lambda i: (0, i))
+    return pl.pallas_call(
+        spread_kernel,
+        grid=(D // tile,),
+        in_specs=[table, table, columns, columns],
+        out_specs=[pl.BlockSpec((BLOCK // 2, tile), lambda i: (0, i))] * 2,
+        out_shape=[jax.ShapeDtypeStruct((BLOCK // 2, D), jnp.bfloat16)] * 2,
+        compiler_params=pltpu.CompilerParams(vmem_limit_bytes=40 * 2**20),
+    )(put, weight, own, twin)
+
+
 def other_core(x):
     return lax.ppermute(x, "ep", OTHER_CORE)
 
@@ -187,27 +215,41 @@
     return lax.all_to_all(x, "ep", 0, 0, tiled=True, axis_index_groups=SAME_CORE)
 
 
-def attend(absorbed, rotary, cache_latent, cache_rotary, lengths, new_latent, new_rotary):
+def attend_kernel(lengths, queries, keys, rotary_keys, mixed):
+    f32 = jnp.float32
     scale = 1.0 / (NOPE + ROPE) ** 0.5
-    f32 = jnp.float32
-    cached = jnp.einsum("clqd,lpd->lcqp", absorbed, cache_latent, preferred_element_type=f32)
-    cached = cached + jnp.einsum("clqe,lep->lcqp", rotary, cache_rotary, preferred_element_type=f32)
-    fresh = jnp.einsum("clqd,jld->lcqj", absorbed, new_latent, preferred_element_type=f32)
-    fresh = fresh + jnp.einsum("clqe,jle->lcqj", rotary, new_rotary, preferred_element_type=f32)
-    visible = jnp.arange(LMAX, dtype=jnp.int32)[None, :] < lengths[:, None]
-    step = jnp.arange(HC * STEPS, dtype=jnp.int32) % STEPS
-    known = jnp.arange(STEPS, dtype=jnp.int32)[None, :] <= step[:, None]
-    cached = jnp.where(visible[:, None, None, :], cached * scale, -jnp.inf)
-    fresh = jnp.where(known[None, None], fresh * scale, -jnp.inf)
-    peak = jnp.maximum(jnp.max(cached, axis=-1), jnp.max(fresh, axis=-1))[..., None]
-    cached = jnp.exp(cached - peak)
-    fresh = jnp.exp(fresh - peak)
-    total = jnp.sum(cached, axis=-1, keepdims=True) + jnp.sum(fresh, axis=-1, keepdims=True)
-    cached = (cached / total).astype(jnp.bfloat16)
-    fresh = (fresh / total).astype(jnp.bfloat16)
-    mixed = jnp.einsum("lcqp,lpd->clqd", cached, cache_latent, preferred_element_type=f32)
-    mixed = mixed + jnp.einsum("lcqj,jld->clqd", fresh, new_latent, preferred_element_type=f32)
-    return mixed.astype(jnp.bfloat16)
+    shape = (CHIPS * HC * STEPS, KEYS)
+    step, place = lax.broadcasted_iota(jnp.int32, shape, 0) % STEPS, lax.broadcasted_iota(jnp.int32, shape, 1)
+    known = (place >= LMAX) & (place - LMAX <= step)
+    for row in range(ROWS_DEV):
+        query = queries[:, row].reshape(shape[0], LAT + ROPE)
+        key = keys[row]
+        score = lax.dot_general(
+            query[:, :LAT], key, (((1,), (1,)), ((), ())), preferred_element_type=f32
+        )
+        score = score + jnp.dot(query[:, LAT:], rotary_keys[row], preferred_element_type=f32)
+        live = known | ((place < LMAX) & (place < lengths[row]))
+        score = jnp.where(live, score * scale, -jnp.inf)
+        prob = jnp.exp(score - jnp.max(score, axis=1, keepdims=True))
+        prob = (prob / jnp.sum(prob, axis=1, keepdims=True)).astype(jnp.bfloat16)
+        out = jnp.dot(prob, key, preferred_element_type=f32).astype(jnp.bfloat16)
+        mixed[:, row] = out.reshape(CHIPS, HC * STEPS, LAT)
+
+
+def attend(queries, cache_latent, cache_rotary, lengths, new_latent, new_rotary):
+    spare = KEYS - LMAX - STEPS
+    keys = jnp.concatenate([cache_latent, jnp.swapaxes(new_latent, 0, 1)], axis=1)
+    keys = jnp.pad(keys, ((0, 0), (0, spare), (0, 0)))
+    rotary_keys = jnp.concatenate([cache_rotary, jnp.transpose(new_rotary, (1, 2, 0))], axis=2)
+    rotary_keys = jnp.pad(rotary_keys, ((0, 0), (0, 0), (0, spare)))
+    return pl.pallas_call(
+        attend_kernel,
+        in_specs=[pl.BlockSpec(memory_space=pltpu.SMEM)]
+        + [pl.BlockSpec(memory_space=pltpu.VMEM)] * 3,
+        out_specs=pl.BlockSpec(memory_space=pltpu.VMEM),
+        out_shape=jax.ShapeDtypeStruct((CHIPS, ROWS_DEV, HC * STEPS, LAT), jnp.bfloat16),
+        compiler_params=pltpu.CompilerParams(vmem_limit_bytes=40 * 2**20),
+    )(lengths, queries, keys, rotary_keys)
 
 
 def per_device(
@@ -251,15 +293,7 @@
     absorbed = absorbed.astype(bf16).reshape(CHIPS, ROWS_DEV, HC * STEPS, LAT)
     rotary = jnp.transpose(rotary, (1, 2, 3, 0, 4)).reshape(CHIPS, ROWS_DEV, HC * STEPS, ROPE)
     sent = exchange(jnp.concatenate([absorbed, rotary], axis=3))
-    mixed = attend(
-        sent[..., :LAT],
-        sent[..., LAT:],
-        cache_latent,
-        cache_rotary,
-        lengths,
-        new_latent,
-        new_rotary,
-    )
+    mixed = attend(sent, cache_latent, cache_rotary, lengths, new_latent, new_rotary)
     mixed = exchange(mixed).reshape(CHIPS, ROWS_DEV, HC, STEPS, LAT)
     values = jnp.einsum("clhsd,hdv->clshv", mixed, value_map, preferred_element_type=f32)
     values = values.astype(bf16).reshape(CHIPS * RS, HC * VHEAD)
@@ -273,45 +307,41 @@
 
     pair = jnp.stack([expert, expert ^ 1])
 
+    streamed = [
+        pltpu.with_memory_space_constraint(w, pltpu.HBM)
+        for w in (expert_gate, expert_up, expert_down)
+    ]
+
     def experts(own, twin):
-        return run_experts(own, other_core(twin), expert_gate, expert_up, expert_down)
-
-    def spread(put, weight, own, twin):
-        total = 0.0
-        for i, half in enumerate((own, twin)):
-            back = jnp.dot(put[i], half, preferred_element_type=f32)
-            total = total + back * weight[i, :, :1]
-        return total.astype(bf16)
+        return run_experts(own, other_core(twin), *streamed)
+
+    def work(pieces, after=()):
+        own, twin, put, weight = pick(pair, pieces, after)
+        own, twin = experts(own, twin)
+        return own, spread(put, weight, own, other_core(twin))
 
     rows = jnp.concatenate([normed, routing(expert_ids, gate_weights)], axis=1)
     rows = plane_exchange(jnp.broadcast_to(rows[None], (16, RS, D + BESIDE)))
     rows = rows.reshape(BLOCK, D + BESIDE)
     half = BLOCK // 2
-    before = shift(rows, 0, 1)
-    after = shift(rows, 0, -1)
-    far = [shift(before[:half], 0, 1), shift(after[half:], 0, -1)]
-    own, twin, put, weight = pick(pair, [rows])
-    result = experts(own, twin)
-    own_sum = spread(put[0], weight[0], result[0], other_core(result[1]))
-    own, twin, put, weight = pick(pair, [after, before], [result])
-    result = experts(own, twin)
-    own, twin = result[0], other_core(result[1])
-    after, before = (
-        spread(put[i], weight[i], own[i * SLOTS :][:SLOTS], twin[i * SLOTS :][:SLOTS])
-        for i in range(2)
-    )
-    own, twin, put, weight = pick(pair, far, [result])
-    result = experts(own, twin)
-    far = spread(put[0], weight[0], result[0], other_core(result[1]))
-
-    up = shift(far[:half], 0, 1)
-    down = shift(far[half:], 0, -1)
-    after = jnp.concatenate([after[:half] + up, after[half:]], axis=0)
-    before = jnp.concatenate([before[:half], before[half:] + down], axis=0)
-    after = shift(after, 0, 1)
-    before = shift(before, 0, -1)
-    total = own_sum.astype(f32) + after.astype(f32) + before.astype(f32)
-    routed = plane_exchange(total.astype(bf16).reshape(16, RS, D))
+    low, high = rows[:half], rows[half:]
+    before_low, after_high = shift(low, 0, 1), shift(high, 0, -1)
+    before_high, after_low = shift(high, 0, 1), shift(low, 0, -1)
+    far = [shift(before_low, 0, 1), shift(after_high, 0, -1)]
+
+    result, (first_low, first_high) = work([before_low, after_high])
+    result, (near_low, near_high) = work([after_low, before_high], [result])
+    result, (far_low, far_high) = work(far, [result, first_low])
+    first_low, first_high = shift(first_low, 0, -1), shift(first_high, 0, 1)
+    far_low, far_high = shift(far_low, 0, 1), shift(far_high, 0, -1)
+    near_low, near_high = shift(near_low + far_low, 0, 1), shift(near_high + far_high, 0, -1)
+    _, (low, high) = work([rows], [result, first_low, first_high])
+    total = [
+        sum(x.astype(f32) for x in parts).astype(bf16)
+        for parts in ((low, first_low, near_low), (high, first_high, near_high))
+    ]
+    total = jnp.concatenate(total, axis=0)
+    routed = plane_exchange(total.reshape(16, RS, D))
     out = (hidden + jnp.sum(routed.astype(f32), axis=0)).astype(bf16)
     return jnp.swapaxes(out.reshape(ROWS_DEV, STEPS, D), 0, 1)
 

time: 269 us -> 257 us (0.955)
  waiting for transfers between devices: 103 us -> 87.7 us
  Pallas kernels: 49.7 us -> 62.9 us
  matrix products: 14 us -> 5.56 us
  starting transfers between devices: 30.3 us -> 36.7 us
  local copies, waits for them, and re-layouts: 11.3 us -> 5.15 us
    pallas_call x0 -> x5, Pallas kernels: none -> 9.71 us  [the longest x4 6.24 us: spread(): pl.pallas_call(spread_kernel, grid=(D // tile,), in_specs=[table, table,...]
    dot_general x14 -> x0, matrix products: 9.27 us -> none  [the longest x8 5.48 us: spread(): back = jnp.dot(put[i], half, preferred_element_type=f32)]
    ppermute x8 -> x12, waiting for transfers between devices: 32.1 us -> 23 us  [shift(): return lax.ppermute(x, 'ep', pairs)]
    pallas_call x3 -> x4, Pallas kernels: 36.6 us -> 44.1 us  [run_experts(): pl.pallas_call(experts_kernel, grid=(hidden // tile,), in_specs=[whole, w...]
    ppermute x10 -> x12, waiting for transfers between devices: 9.24 us -> 2.98 us  [other_core(): return lax.ppermute(x, 'ep', OTHER_CORE)]
    ppermute x8 -> x12, starting transfers between devices: 12.5 us -> 18.6 us  [shift(): return lax.ppermute(x, 'ep', pairs)]
    pallas_call x3 -> x4, Pallas kernels: 13.1 us -> 9.1 us  [pick(): pl.pallas_call(functools.partial(pick_kernel, sizes), grid=(D // tile,),...]
    unnamed x38 -> x26, local copies, waits for them, and re-layouts: 3.21 us -> 0.25 us
  transfers between devices with their start and end apart: 21 -> 27, of which waited for: 12 -> 10; matrix products, arithmetic and copies ran while one was open for 6% -> 2% of each run, Pallas kernels for 11% -> 24%
where the time goes in v3:
time: 257 us
  waiting for transfers between devices  87.7 us (34%)
  Pallas kernels  62.9 us (24%)
  blocking collectives  53.6 us (21%)
  starting transfers between devices  36.7 us (14%)
  matrix products  5.56 us (2%)
  local copies, waits for them, and re-layouts  5.15 us (2%)
  other arithmetic  4.73 us (2%)
    all_to_all x3, waiting for transfers between devices, exchange(): lax.all_to_all(x, 'ep', 0, 0, tiled=True, axis_index_groups=SAME_CORE)  61.8 us
    all_to_all x2, blocking collectives, plane_exchange(): lax.all_to_all(x, ('dp', 'ep'), 0, 0, tiled=True, axis_index_groups=PLANES)  53.6 us
    pallas_call x4, Pallas kernels, run_experts(): pl.pallas_call(experts_kernel, grid=(hidden // tile,), in_specs=[whole, w...  44.1 us
    ppermute x12, waiting for transfers between devices, shift(): return lax.ppermute(x, 'ep', pairs)  23 us
    ppermute x12, starting transfers between devices, shift(): return lax.ppermute(x, 'ep', pairs)  18.6 us
    all_to_all x3, starting transfers between devices, exchange(): lax.all_to_all(x, 'ep', 0, 0, tiled=True, axis_index_groups=SAME_CORE)  15.6 us
    pallas_call x4, Pallas kernels, pick(): pl.pallas_call(functools.partial(pick_kernel, sizes), grid=(D // tile,),...  9.1 us
    pallas_call x4, Pallas kernels, spread(): pl.pallas_call(spread_kernel, grid=(D // tile,), in_specs=[table, table,...  6.24 us
  transfers between devices with their start and end apart: 27, of which 10 were waited for; matrix products, arithmetic and copies ran while one was open for 2% of the time, Pallas kernels for 24%

profile of v3, /device:TPU:0, one launch (start us, length us, event | category | flops | bytes accessed | tf_op | source)
XLA Modules:
  0.0 257.0 jit_solution(1631694361517646551)
XLA Ops:
  6.5 8.1 %all-to-all-start = ((bf16[16,4,16,576]{3,2,1,0:T(8,128)(2,1)}), bf16[16,4,16,576]{3,2,1,0:T(8,128)(2,1)S(1)}, u32[]{:S(2)}, u32[]{:S(2)}) async-start(bf16[16,4,16,576]{3,2,1,0:T(8,128)(2,1)} %pad_maximum_fusion.1), calls=%async_computation | async-start | bytes 2621440 | tf_op jit(solution)/shard_map/all_to_all | solution.py:215
  15.1 20.9 %all-to-all-done.queries = bf16[16,4,16,576]{3,2,1,0:T(8,128)(2,1)S(1)} async-done(((bf16[16,4,16,576]{3,2,1,0:T(8,128)(2,1)}), bf16[16,4,16,576]{3,2,1,0:T(8,128)(2,1)S(1)}, u32[]{:S(2)}, u32[]{:S(2)}) %all-to-all-start) | async-done | bytes 1179680 | tf_op jit(solution)/shard_map/all_to_all | solution.py:215
  36.0 3.5 %shard_map.163 = bf16[16,4,16,512]{3,2,1,0:T(8,128)(2,1)} custom-call(s32[4]{0:T(128)S(1)} %copy-done, bf16[16,4,16,576]{3,2,1,0:T(8,128)(2,1)S(1)} %all-to-all-done.queries, bf16[4,128,512]{2,1,0:T(8,128)(2,1)S(1)} %fusion.7.keys, bf16[4,64,128]{2,1,0:T(8,128)(2,1)S(1)} %fusion.18.rotary_keys), custom_call_target="tpu_custom_call" | custom-call | tf_op jit(solution)/shard_map/pallas_call | solution.py:245
  39.5 3.7 %all-to-all-start.1 = ((bf16[16,4,16,512]{3,2,1,0:T(8,128)(2,1)}), bf16[16,4,16,512]{3,2,1,0:T(8,128)(2,1)S(1)}, u32[]{:S(2)}, u32[]{:S(2)}) async-start(bf16[16,4,16,512]{3,2,1,0:T(8,128)(2,1)} %shard_map.163), calls=%async_computation.1 | async-start | bytes 2097152 | tf_op jit(solution)/shard_map/all_to_all | solution.py:215
  43.3 15.9 %all-to-all-done.1 = bf16[16,4,16,512]{3,2,1,0:T(8,128)(2,1)S(1)} async-done(((bf16[16,4,16,512]{3,2,1,0:T(8,128)(2,1)}), bf16[16,4,16,512]{3,2,1,0:T(8,128)(2,1)S(1)}, u32[]{:S(2)}, u32[]{:S(2)}) %all-to-all-start.1) | async-done | bytes 1048608 | tf_op jit(solution)/shard_map/all_to_all | solution.py:215
  60.4 4.4 %convolution_convert_fusion = bf16[256,3584]{1,0:T(8,128)(2,1)} fusion(bf16[256,3584]{1,0:T(8,128)(2,1)} %collective-permute-done.3, bf16[256,3584]{1,0:T(8,128)(2,1)} %param.21, bf16[32,8,4,128]{3,2,1,0:T(4,128)(2,1)S(1)} %bitcast.74), kind=kOutput, calls=%fused_computation | convolution fusion | flops 947781632 | bytes 5767168 | tf_op jit(solution)/shard_map/dot_general | solution.py:300
  64.8 3.8 %all-to-all-start.2 = ((bf16[16,16,3584]{2,1,0:T(8,128)(2,1)}), bf16[16,16,3584]{2,1,0:T(8,128)(2,1)S(1)}, u32[]{:S(2)}, u32[]{:S(2)}) async-start(bf16[16,16,3584]{2,1,0:T(8,128)(2,1)} %bitcast.67), calls=%async_computation.2 | async-start | bytes 3670016 | tf_op jit(solution)/shard_map/all_to_all | solution.py:215
  69.0 24.9 %all-to-all-done.2 = bf16[16,16,3584]{2,1,0:T(8,128)(2,1)S(1)} async-done(((bf16[16,16,3584]{2,1,0:T(8,128)(2,1)}), bf16[16,16,3584]{2,1,0:T(8,128)(2,1)S(1)}, u32[]{:S(2)}, u32[]{:S(2)}) %all-to-all-start.2) | async-done | bytes 1835040 | tf_op jit(solution)/shard_map/all_to_all | solution.py:215
  94.7 27.4 %all_to_all.25 = bf16[16,16,3712]{2,1,0:T(8,128)(2,1)S(1)} all-to-all(bf16[16,16,3712]{2,1,0:T(8,128)(2,1)S(1)} %broadcast_in_dim.2), channel_id=1, replica_groups={{0,32,64,96,2,34,66,98,4,36,68,100,6,38,70,102},{8,40,72,104,10,42,74,1..., dimensions={0} | all-to-all | bytes 3801088 | tf_op jit(solution)/shard_map/all_to_all | solution.py:59
  128.9 9.8 %collective-permute-done.4.refs_0_.refs_2_ = bf16[128,3712]{1,0:T(8,128)(2,1)S(1)} collective-permute-done((bf16[128,3712]{1,0:T(8,128)(2,1)}, bf16[128,3712]{1,0:T(8,128)(2,1)S(1)}, u32[]{:S(2)}, u32[]{:S(2)}) %collective-permute-start.4) | collective-permute-done | bytes 950304 | tf_op jit(solution)/shard_map/ppermute | solution.py:55
  138.9 2.6 %shard_map.164 = (bf16[128,3584]{1,0:T(8,128)(2,1)S(1)}, bf16[128,3584]{1,0:T(8,128)(2,1)S(1)}, bf16[1,2,256,128]{3,2,1,0:T(8,128)(2,1)S(1)}, f32[1,2,256,128]{3,2,1,0:T(8,128)S(1)}) custom-call(s32[2]{0:T(128)S(1)} %pad_add_fusion.experts, bf16[128,3712]{1,0:T(8,128)(2,1)S(1)} %collective-permute-done.4.refs_0_.refs_2_, ...), custom_call_target="tpu_custom_call" | custom-call | tf_op jit(solution)/shard_map/pallas_call | solution.py:125
  145.1 11.0 %shard_map.165 = (bf16[128,3584]{1,0:T(8,128)(2,1)S(1)}, bf16[128,3584]{1,0:T(8,128)(2,1)S(1)}) custom-call(bf16[128,3584]{1,0:T(8,128)(2,1)S(1)} %get-tuple-element.37.own, bf16[128,3584]{1,0:T(8,128)(2,1)S(1)} %collective-permute-done.10.twin, bf16[1,3584,1024]{2,1,0:T(8,128)(2,1)} %gate.7, bf16[1,3584,1024]{2,1,0:T(8,128)(2,1)} %upward.7, ...), custom_call_target="tpu_custom_call" | custom-call | flops 458752 | bytes 458752 | tf_op jit(solution)/shard_map/pallas_call | solution.py:168
  156.1 2.2 shard_map.166
  160.9 11.0 %shard_map.167 = (bf16[128,3584]{1,0:T(8,128)(2,1)S(1)}, bf16[128,3584]{1,0:T(8,128)(2,1)S(1)}) custom-call(bf16[128,3584]{1,0:T(8,128)(2,1)S(1)} %get-tuple-element.40.own, bf16[128,3584]{1,0:T(8,128)(2,1)S(1)} %collective-permute-done.11.twin, bf16[1,3584,1024]{2,1,0:T(8,128)(2,1)} %gate.7, bf16[1,3584,1024]{2,1,0:T(8,128)(2,1)} %upward.7, ...), custom_call_target="tpu_custom_call" | custom-call | flops 458752 | bytes 458752 | tf_op jit(solution)/shard_map/pallas_call | solution.py:168
  173.5 2.2 shard_map.169
  176.8 2.3 collective-permute-start.14
  179.2 11.0 %shard_map.170 = (bf16[128,3584]{1,0:T(8,128)(2,1)S(1)}, bf16[128,3584]{1,0:T(8,128)(2,1)S(1)}) custom-call(bf16[128,3584]{1,0:T(8,128)(2,1)S(1)} %get-tuple-element.47.own, bf16[128,3584]{1,0:T(8,128)(2,1)S(1)} %collective-permute-done.13.twin, bf16[1,3584,1024]{2,1,0:T(8,128)(2,1)} %gate.7, bf16[1,3584,1024]{2,1,0:T(8,128)(2,1)} %upward.7, ...), custom_call_target="tpu_custom_call" | custom-call | flops 458752 | bytes 458752 | tf_op jit(solution)/shard_map/pallas_call | solution.py:168
  190.5 2.1 shard_map.171
  194.9 3.3 %collective-permute-start.22 = (bf16[128,3584]{1,0:T(8,128)(2,1)S(1)}, bf16[128,3584]{1,0:T(8,128)(2,1)S(1)}, u32[]{:S(2)}, u32[]{:S(2)}) collective-permute-start(bf16[128,3584]{1,0:T(8,128)(2,1)S(1)} %get-tuple-element.68), channel_id=1, source_target_pairs={{0,24},{1,7},{2,26},{3,1},{4,28},{5,3},{6,30},{7,5},{8,0},{9,15},{... | collective-permute-start | bytes 2752520 | tf_op jit(solution)/shard_map/ppermute | solution.py:55
  198.1 11.0 %shard_map.172 = (bf16[128,3584]{1,0:T(8,128)(2,1)S(1)}, bf16[128,3584]{1,0:T(8,128)(2,1)S(1)}) custom-call(bf16[128,3584]{1,0:T(8,128)(2,1)S(1)} %get-tuple-element.53.own, bf16[128,3584]{1,0:T(8,128)(2,1)S(1)} %collective-permute-done.16.twin, bf16[1,3584,1024]{2,1,0:T(8,128)(2,1)} %gate.7, bf16[1,3584,1024]{2,1,0:T(8,128)(2,1)} %upward.7, ...), custom_call_target="tpu_custom_call" | custom-call | flops 458752 | bytes 458752 | tf_op jit(solution)/shard_map/pallas_call | solution.py:168
  211.0 3.3 %collective-permute-start.23 = (bf16[128,3584]{1,0:T(8,128)(2,1)S(1)}, bf16[128,3584]{1,0:T(8,128)(2,1)S(1)}, u32[]{:S(2)}, u32[]{:S(2)}) collective-permute-start(bf16[128,3584]{1,0:T(8,128)(2,1)S(1)} %add.70), channel_id=1, source_target_pairs={{0,24},{1,7},{2,26},{3,1},{4,28},{5,3},{6,30},{7,5},{8,0},{9,15},{... | collective-permute-start | bytes 2752520 | tf_op jit(solution)/shard_map/ppermute | solution.py:55
  216.2 9.0 %collective-permute-done.23 = bf16[128,3584]{1,0:T(8,128)(2,1)S(1)} collective-permute-done((bf16[128,3584]{1,0:T(8,128)(2,1)S(1)}, bf16[128,3584]{1,0:T(8,128)(2,1)S(1)}, u32[]{:S(2)}, u32[]{:S(2)}) %collective-permute-start.23) | collective-permute-done | bytes 917536 | tf_op jit(solution)/shard_map/ppermute | solution.py:55
  225.6 3.6 %collective-permute-done.21 = bf16[128,3584]{1,0:T(8,128)(2,1)S(1)} collective-permute-done((bf16[128,3584]{1,0:T(8,128)(2,1)S(1)}, bf16[128,3584]{1,0:T(8,128)(2,1)S(1)}, u32[]{:S(2)}, u32[]{:S(2)}) %collective-permute-start.21) | collective-permute-done | bytes 917536 | tf_op jit(solution)/shard_map/ppermute | solution.py:55
  229.7 26.2 %all_to_all.26 = bf16[16,16,3584]{2,1,0:T(8,128)(2,1)S(1)} all-to-all(bf16[16,16,3584]{2,1,0:T(8,128)(2,1)S(1)} %bitcast.66), channel_id=1, replica_groups={{0,32,64,96,2,34,66,98,4,36,68,100,6,38,70,102},{8,40,72,104,10,42,74,1..., dimensions={0} | all-to-all | bytes 3670016 | tf_op jit(solution)/shard_map/all_to_all | solution.py:59
  (120 shorter events, 33.0 us)
Async XLA Ops:
  0.0 4.2 %collective-permute-start.1 = (bf16[2,128,512]{2,1,0:T(8,128)(2,1)}, bf16[2,128,512]{2,1,0:T(8,128)(2,1)S(1)}, u32[]{:S(2)}, u32[]{:S(2)}) collective-permute-start(bf16[2,128,512]{2,1,0:T(8,128)(2,1)} %param.19), channel_id=1, source_target_pairs={{0,1},{1,0},{2,3},{3,2},{4,5},{5,4},{6,7},{7,6},{8,9},{9,8},{10,11... | collective-permute-start | bytes 786440 | tf_op jit(solution)/shard_map/ppermute | solution.py:211
  6.5 29.6 %all-to-all-start = ((bf16[16,4,16,576]{3,2,1,0:T(8,128)(2,1)}), bf16[16,4,16,576]{3,2,1,0:T(8,128)(2,1)S(1)}, u32[]{:S(2)}, u32[]{:S(2)}) async-start(bf16[16,4,16,576]{3,2,1,0:T(8,128)(2,1)} %pad_maximum_fusion.1), calls=%async_computation | async-start | bytes 2621440 | tf_op jit(solution)/shard_map/all_to_all | solution.py:215
  14.6 45.8 %collective-permute-start.3 = (bf16[256,3584]{1,0:T(8,128)(2,1)}, bf16[256,3584]{1,0:T(8,128)(2,1)}, u32[]{:S(2)}, u32[]{:S(2)}) collective-permute-start(bf16[256,3584]{1,0:T(8,128)(2,1)} %param.21), channel_id=1, source_target_pairs={{0,1},{1,0},{2,3},{3,2},{4,5},{5,4},{6,7},{7,6},{8,9},{9,8},{10,11... | collective-permute-start | bytes 5505032 | tf_op jit(solution)/shard_map/ppermute | solution.py:211
  39.5 19.7 %all-to-all-start.1 = ((bf16[16,4,16,512]{3,2,1,0:T(8,128)(2,1)}), bf16[16,4,16,512]{3,2,1,0:T(8,128)(2,1)S(1)}, u32[]{:S(2)}, u32[]{:S(2)}) async-start(bf16[16,4,16,512]{3,2,1,0:T(8,128)(2,1)} %shard_map.163), calls=%async_computation.1 | async-start | bytes 2097152 | tf_op jit(solution)/shard_map/all_to_all | solution.py:215
  43.2 16.3 %collective-permute-start = (bf16[2,512,128]{2,1,0:T(8,128)(2,1)S(1)}, bf16[2,512,128]{2,1,0:T(8,128)(2,1)S(1)}, u32[]{:S(2)}, u32[]{:S(2)}) collective-permute-start(bf16[2,512,128]{2,1,0:T(8,128)(2,1)S(1)} %copy-done.10), channel_id=1, source_target_pairs={{0,1},{1,0},{2,3},{3,2},{4,5},{5,4},{6,7},{7,6},{8,9},{9,8},{10,11... | collective-permute-start | bytes 786440 | tf_op jit(solution)/shard_map/ppermute | solution.py:211
  64.8 29.1 %all-to-all-start.2 = ((bf16[16,16,3584]{2,1,0:T(8,128)(2,1)}), bf16[16,16,3584]{2,1,0:T(8,128)(2,1)S(1)}, u32[]{:S(2)}, u32[]{:S(2)}) async-start(bf16[16,16,3584]{2,1,0:T(8,128)(2,1)} %bitcast.67), calls=%async_computation.2 | async-start | bytes 3670016 | tf_op jit(solution)/shard_map/all_to_all | solution.py:215
  123.5 15.2 %collective-permute-start.4 = (bf16[128,3712]{1,0:T(8,128)(2,1)}, bf16[128,3712]{1,0:T(8,128)(2,1)S(1)}, u32[]{:S(2)}, u32[]{:S(2)}) collective-permute-start(bf16[128,3712]{1,0:T(8,128)(2,1)} %bitcast.26), channel_id=1, source_target_pairs={{0,8},{1,3},{2,10},{3,5},{4,12},{5,7},{6,14},{7,1},{8,16},{9,11},{... | collective-permute-start | bytes 2850824 | tf_op jit(solution)/shard_map/ppermute | solution.py:55
  124.8 14.1 %collective-permute-start.6 = (bf16[128,3712]{1,0:T(8,128)(2,1)}, bf16[128,3712]{1,0:T(8,128)(2,1)}, u32[]{:S(2)}, u32[]{:S(2)}) collective-permute-start(bf16[128,3712]{1,0:T(8,128)(2,1)} %bitcast.27), channel_id=1, source_target_pairs={{0,24},{1,7},{2,26},{3,1},{4,28},{5,3},{6,30},{7,5},{8,0},{9,15},{... | collective-permute-start | bytes 2850824 | tf_op jit(solution)/shard_map/ppermute | solution.py:55
  126.8 29.3 %collective-permute-start.8 = (bf16[128,3712]{1,0:T(8,128)(2,1)}, bf16[128,3712]{1,0:T(8,128)(2,1)S(1)}, u32[]{:S(2)}, u32[]{:S(2)}) collective-permute-start(bf16[128,3712]{1,0:T(8,128)(2,1)} %bitcast.26), channel_id=1, source_target_pairs={{0,24},{1,7},{2,26},{3,1},{4,28},{5,3},{6,30},{7,5},{8,0},{9,15},{... | collective-permute-start | bytes 2850824 | tf_op jit(solution)/shard_map/ppermute | solution.py:55
  128.1 28.0 %collective-permute-start.9 = (bf16[128,3712]{1,0:T(8,128)(2,1)}, bf16[128,3712]{1,0:T(8,128)(2,1)S(1)}, u32[]{:S(2)}, u32[]{:S(2)}) collective-permute-start(bf16[128,3712]{1,0:T(8,128)(2,1)} %bitcast.27), channel_id=1, source_target_pairs={{0,8},{1,3},{2,10},{3,5},{4,12},{5,7},{6,14},{7,1},{8,16},{9,11},{... | collective-permute-start | bytes 2850824 | tf_op jit(solution)/shard_map/ppermute | solution.py:55
  141.5 3.6 %collective-permute-start.10 = (bf16[128,3584]{1,0:T(8,128)(2,1)S(1)}, bf16[128,3584]{1,0:T(8,128)(2,1)S(1)}, u32[]{:S(2)}, u32[]{:S(2)}) collective-permute-start(bf16[128,3584]{1,0:T(8,128)(2,1)S(1)} %get-tuple-element.38), channel_id=1, source_target_pairs={{0,1},{1,0},{2,3},{3,2},{4,5},{5,4},{6,7},{7,6},{8,9},{9,8},{10,11... | collective-permute-start | bytes 2752520 | tf_op jit(solution)/shard_map/ppermute | solution.py:211
  141.6 31.9 %collective-permute-start.5 = (bf16[128,3712]{1,0:T(8,128)(2,1)S(1)}, bf16[128,3712]{1,0:T(8,128)(2,1)S(1)}, u32[]{:S(2)}, u32[]{:S(2)}) collective-permute-start(bf16[128,3712]{1,0:T(8,128)(2,1)S(1)} %collective-permute-done.4.refs_0_.refs_2_), channel_id=1, source_target_pairs={{0,8},{1,3},{2,10},{3,5},{4,12},{5,7},{6,14},{7,1},{8,16},{9,11},{... | collective-permute-start | bytes 2850824 | tf_op jit(solution)/shard_map/ppermute | solution.py:55
  143.2 30.3 %collective-permute-start.7 = (bf16[128,3712]{1,0:T(8,128)(2,1)}, bf16[128,3712]{1,0:T(8,128)(2,1)S(1)}, u32[]{:S(2)}, u32[]{:S(2)}) collective-permute-start(bf16[128,3712]{1,0:T(8,128)(2,1)} %collective-permute-done.6.refs_1_.refs_3_), channel_id=1, source_target_pairs={{0,24},{1,7},{2,26},{3,1},{4,28},{5,3},{6,30},{7,5},{8,0},{9,15},{... | collective-permute-start | bytes 2850824 | tf_op jit(solution)/shard_map/ppermute | solution.py:55
  158.4 13.5 %collective-permute-start.12 = (bf16[128,3584]{1,0:T(8,128)(2,1)S(1)}, bf16[128,3584]{1,0:T(8,128)(2,1)S(1)}, u32[]{:S(2)}, u32[]{:S(2)}) collective-permute-start(bf16[128,3584]{1,0:T(8,128)(2,1)S(1)} %get-tuple-element.45), channel_id=1, source_target_pairs={{0,1},{1,0},{2,3},{3,2},{4,5},{5,4},{6,7},{7,6},{8,9},{9,8},{10,11... | collective-permute-start | bytes 2752520 | tf_op jit(solution)/shard_map/ppermute | solution.py:211
  175.7 3.5 %collective-permute-start.13 = (bf16[128,3584]{1,0:T(8,128)(2,1)S(1)}, bf16[128,3584]{1,0:T(8,128)(2,1)S(1)}, u32[]{:S(2)}, u32[]{:S(2)}) collective-permute-start(bf16[128,3584]{1,0:T(8,128)(2,1)S(1)} %get-tuple-element.48), channel_id=1, source_target_pairs={{0,1},{1,0},{2,3},{3,2},{4,5},{5,4},{6,7},{7,6},{8,9},{9,8},{10,11... | collective-permute-start | bytes 2752520 | tf_op jit(solution)/shard_map/ppermute | solution.py:211
  175.9 14.6 %collective-permute-start.15 = (bf16[128,3584]{1,0:T(8,128)(2,1)S(1)}, bf16[128,3584]{1,0:T(8,128)(2,1)S(1)}, u32[]{:S(2)}, u32[]{:S(2)}) collective-permute-start(bf16[128,3584]{1,0:T(8,128)(2,1)S(1)} %get-tuple-element.50), channel_id=1, source_target_pairs={{0,8},{1,3},{2,10},{3,5},{4,12},{5,7},{6,14},{7,1},{8,16},{9,11},{... | collective-permute-start | bytes 2752520 | tf_op jit(solution)/shard_map/ppermute | solution.py:55
  176.8 13.7 %collective-permute-start.14 = (bf16[128,3584]{1,0:T(8,128)(2,1)S(1)}, bf16[128,3584]{1,0:T(8,128)(2,1)S(1)}, u32[]{:S(2)}, u32[]{:S(2)}) collective-permute-start(bf16[128,3584]{1,0:T(8,128)(2,1)S(1)} %get-tuple-element.46.refs_5_), channel_id=1, source_target_pairs={{0,24},{1,7},{2,26},{3,1},{4,28},{5,3},{6,30},{7,5},{8,0},{9,15},{... | collective-permute-start | bytes 2752520 | tf_op jit(solution)/shard_map/ppermute | solution.py:55
  192.7 5.5 %collective-permute-start.16 = (bf16[128,3584]{1,0:T(8,128)(2,1)S(1)}, bf16[128,3584]{1,0:T(8,128)(2,1)S(1)}, u32[]{:S(2)}, u32[]{:S(2)}) collective-permute-start(bf16[128,3584]{1,0:T(8,128)(2,1)S(1)} %get-tuple-element.54), channel_id=1, source_target_pairs={{0,1},{1,0},{2,3},{3,2},{4,5},{5,4},{6,7},{7,6},{8,9},{9,8},{10,11... | collective-permute-start | bytes 2752520 | tf_op jit(solution)/shard_map/ppermute | solution.py:211
  193.0 16.3 %collective-permute-start.18 = (bf16[128,3584]{1,0:T(8,128)(2,1)S(1)}, bf16[128,3584]{1,0:T(8,128)(2,1)S(1)}, u32[]{:S(2)}, u32[]{:S(2)}) collective-permute-start(bf16[128,3584]{1,0:T(8,128)(2,1)S(1)} %get-tuple-element.60), channel_id=1, source_target_pairs={{0,1},{1,0},{2,3},{3,2},{4,5},{5,4},{6,7},{7,6},{8,9},{9,8},{10,11... | collective-permute-start | bytes 2752520 | tf_op jit(solution)/shard_map/ppermute | solution.py:211
  194.9 16.0 %collective-permute-start.22 = (bf16[128,3584]{1,0:T(8,128)(2,1)S(1)}, bf16[128,3584]{1,0:T(8,128)(2,1)S(1)}, u32[]{:S(2)}, u32[]{:S(2)}) collective-permute-start(bf16[128,3584]{1,0:T(8,128)(2,1)S(1)} %get-tuple-element.68), channel_id=1, source_target_pairs={{0,24},{1,7},{2,26},{3,1},{4,28},{5,3},{6,30},{7,5},{8,0},{9,15},{... | collective-permute-start | bytes 2752520 | tf_op jit(solution)/shard_map/ppermute | solution.py:55
  198.1 16.2 %collective-permute-start.20 = (bf16[128,3584]{1,0:T(8,128)(2,1)S(1)}, bf16[128,3584]{1,0:T(8,128)(2,1)S(1)}, u32[]{:S(2)}, u32[]{:S(2)}) collective-permute-start(bf16[128,3584]{1,0:T(8,128)(2,1)S(1)} %get-tuple-element.65), channel_id=1, source_target_pairs={{0,8},{1,3},{2,10},{3,5},{4,12},{5,7},{6,14},{7,1},{8,16},{9,11},{... | collective-permute-start | bytes 2752520 | tf_op jit(solution)/shard_map/ppermute | solution.py:55
  209.2 5.5 %collective-permute-start.17 = (bf16[128,3584]{1,0:T(8,128)(2,1)S(1)}, bf16[128,3584]{1,0:T(8,128)(2,1)S(1)}, u32[]{:S(2)}, u32[]{:S(2)}) collective-permute-start(bf16[128,3584]{1,0:T(8,128)(2,1)S(1)} %get-tuple-element.56), channel_id=1, source_target_pairs={{0,1},{1,0},{2,3},{3,2},{4,5},{5,4},{6,7},{7,6},{8,9},{9,8},{10,11... | collective-permute-start | bytes 2752520 | tf_op jit(solution)/shard_map/ppermute | solution.py:211
  211.0 14.2 %collective-permute-start.23 = (bf16[128,3584]{1,0:T(8,128)(2,1)S(1)}, bf16[128,3584]{1,0:T(8,128)(2,1)S(1)}, u32[]{:S(2)}, u32[]{:S(2)}) collective-permute-start(bf16[128,3584]{1,0:T(8,128)(2,1)S(1)} %add.70), channel_id=1, source_target_pairs={{0,24},{1,7},{2,26},{3,1},{4,28},{5,3},{6,30},{7,5},{8,0},{9,15},{... | collective-permute-start | bytes 2752520 | tf_op jit(solution)/shard_map/ppermute | solution.py:55
  214.6 14.7 %collective-permute-start.21 = (bf16[128,3584]{1,0:T(8,128)(2,1)S(1)}, bf16[128,3584]{1,0:T(8,128)(2,1)S(1)}, u32[]{:S(2)}, u32[]{:S(2)}) collective-permute-start(bf16[128,3584]{1,0:T(8,128)(2,1)S(1)} %add.67), channel_id=1, source_target_pairs={{0,8},{1,3},{2,10},{3,5},{4,12},{5,7},{6,14},{7,1},{8,16},{9,11},{... | collective-permute-start | bytes 2752520 | tf_op jit(solution)/shard_map/ppermute | solution.py:55
  (14 other events, 138.2 us)

commit v4 on v3

--- a/solution.py
+++ b/solution.py
@@ -137,7 +137,7 @@
             jax.ShapeDtypeStruct((blocks, 2, BLOCK, SLOTS), jnp.float32),
         ],
         scratch_shapes=[pltpu.VMEM((blocks, 2, SLOTS, BLOCK), jnp.bfloat16)],
-        compiler_params=pltpu.CompilerParams(vmem_limit_bytes=40 * 2**20),
+        compiler_params=pltpu.CompilerParams(vmem_limit_bytes=10 * 2**20),
     )(experts, *pieces, *pieces, *after)
 
 
@@ -151,7 +151,8 @@
         total[...] = jnp.zeros_like(total)
 
     x = jnp.concatenate([own[...], twin[...]], axis=0)
-    g = jnp.dot(x, gate[0], preferred_element_type=f32)
+    columns = pl.ds(pl.multiple_of(tile * down.shape[1], down.shape[1]), down.shape[1])
+    g = jnp.dot(x, gate[0, :, columns], preferred_element_type=f32)
     u = jnp.dot(x, upward[0], preferred_element_type=f32)
     inner = (g / (1.0 + jnp.exp(-g)) * u).astype(jnp.bfloat16)
     total[...] += jnp.dot(inner, down[0], preferred_element_type=f32)
@@ -171,16 +172,29 @@
         in_specs=[
             whole,
             whole,
-            pl.BlockSpec((1, D, tile), lambda i: (0, 0, i)),
+            pl.BlockSpec(memory_space=pltpu.VMEM),
             pl.BlockSpec((1, D, tile), lambda i: (0, 0, i)),
             pl.BlockSpec((1, tile, D), lambda i: (0, i, 0)),
         ],
         out_specs=[whole, whole],
         out_shape=[jax.ShapeDtypeStruct((rows, D), jnp.bfloat16)] * 2,
         scratch_shapes=[pltpu.VMEM((2 * rows, D), jnp.float32)],
-        compiler_params=pltpu.CompilerParams(vmem_limit_bytes=40 * 2**20),
+        compiler_params=pltpu.CompilerParams(vmem_limit_bytes=24 * 2**20),
         cost_estimate=pl.CostEstimate(flops=rows * D, bytes_accessed=rows * D, transcendentals=0),
     )(own, twin, gate, upward, down)
+
+
+def mark_kernel(*refs):
+    refs[-1][...] = jnp.zeros_like(refs[-1])
+
+
+def mark(*arrays):
+    return pl.pallas_call(
+        mark_kernel,
+        in_specs=[pl.BlockSpec(memory_space=pl.ANY) for _ in arrays],
+        out_shape=jax.ShapeDtypeStruct((8, 128), jnp.float32),
+        compiler_params=pltpu.CompilerParams(vmem_limit_bytes=2**20),
+    )(*arrays)
 
 
 def spread_kernel(put, weight, own, twin, low, high):
@@ -203,7 +217,7 @@
         in_specs=[table, table, columns, columns],
         out_specs=[pl.BlockSpec((BLOCK // 2, tile), lambda i: (0, i))] * 2,
         out_shape=[jax.ShapeDtypeStruct((BLOCK // 2, D), jnp.bfloat16)] * 2,
-        compiler_params=pltpu.CompilerParams(vmem_limit_bytes=40 * 2**20),
+        compiler_params=pltpu.CompilerParams(vmem_limit_bytes=10 * 2**20),
     )(put, weight, own, twin)
 
 
@@ -248,7 +262,7 @@
         + [pl.BlockSpec(memory_space=pltpu.VMEM)] * 3,
         out_specs=pl.BlockSpec(memory_space=pltpu.VMEM),
         out_shape=jax.ShapeDtypeStruct((CHIPS, ROWS_DEV, HC * STEPS, LAT), jnp.bfloat16),
-        compiler_params=pltpu.CompilerParams(vmem_limit_bytes=40 * 2**20),
+        compiler_params=pltpu.CompilerParams(vmem_limit_bytes=16 * 2**20),
     )(lengths, queries, keys, rotary_keys)
 
 
@@ -307,13 +321,17 @@
 
     pair = jnp.stack([expert, expert ^ 1])
 
-    streamed = [
-        pltpu.with_memory_space_constraint(w, pltpu.HBM)
-        for w in (expert_gate, expert_up, expert_down)
+    weights = [
+        pltpu.with_memory_space_constraint(w, place)
+        for w, place in (
+            (expert_gate, pltpu.VMEM),
+            (expert_up, pltpu.HBM),
+            (expert_down, pltpu.HBM),
+        )
     ]
 
     def experts(own, twin):
-        return run_experts(own, other_core(twin), *streamed)
+        return run_experts(own, other_core(twin), *weights)
 
     def work(pieces, after=()):
         own, twin, put, weight = pick(pair, pieces, after)
@@ -329,7 +347,8 @@
     before_high, after_low = shift(high, 0, 1), shift(low, 0, -1)
     far = [shift(before_low, 0, 1), shift(after_high, 0, -1)]
 
-    result, (first_low, first_high) = work([before_low, after_high])
+    here = mark(rows[:16, :128], weights[0])
+    result, (first_low, first_high) = work([before_low, after_high], [here])
     result, (near_low, near_high) = work([after_low, before_high], [result])
     result, (far_low, far_high) = work(far, [result, first_low])
     first_low, first_high = shift(first_low, 0, -1), shift(first_high, 0, 1)

time: 257 us -> 255 us (level)
  local copies, waits for them, and re-layouts: 5.15 us -> 9.91 us
  Pallas kernels: 62.9 us -> 58.3 us
  waiting for transfers between devices: 87.7 us -> 85.1 us
    pallas_call x4, Pallas kernels: 44.1 us -> 39.5 us  [run_experts(): pl.pallas_call(experts_kernel, grid=(hidden // tile,), in_specs=[whole, w...]
    unnamed x26 -> x38, local copies, waits for them, and re-layouts: 0.25 us -> 4.28 us
    ppermute x12, waiting for transfers between devices: 23 us -> 20.3 us  [shift(): return lax.ppermute(x, 'ep', pairs)]
  transfers between devices with their start and end apart: 27 -> 27, of which waited for: 10 -> 10; matrix products, arithmetic and copies ran while one was open for 2% -> 2% of each run, Pallas kernels for 24% -> 22%
where the time goes in v4:
time: 255 us; the launch traced here: 254 us
  waiting for transfers between devices  85.1 us (33%)
  Pallas kernels  58.3 us (23%)
  blocking collectives  53.7 us (21%)
  starting transfers between devices  37 us (15%)
  local copies, waits for them, and re-layouts  9.91 us (4%)
  matrix products  4.99 us (2%)
  other arithmetic  4.69 us (2%)
    all_to_all x3, waiting for transfers between devices, exchange(): lax.all_to_all(x, 'ep', 0, 0, tiled=True, axis_index_groups=SAME_CORE)  61.8 us
    all_to_all x2, blocking collectives, plane_exchange(): lax.all_to_all(x, ('dp', 'ep'), 0, 0, tiled=True, axis_index_groups=PLANES)  53.7 us
    pallas_call x4, Pallas kernels, run_experts(): pl.pallas_call(experts_kernel, grid=(hidden // tile,), in_specs=[whole, w...  39.5 us
    ppermute x12, waiting for transfers between devices, shift(): return lax.ppermute(x, 'ep', pairs)  20.3 us
    ppermute x12, starting transfers between devices, shift(): return lax.ppermute(x, 'ep', pairs)  18.6 us
    all_to_all x3, starting transfers between devices, exchange(): lax.all_to_all(x, 'ep', 0, 0, tiled=True, axis_index_groups=SAME_CORE)  15.6 us
    pallas_call x4, Pallas kernels, pick(): pl.pallas_call(functools.partial(pick_kernel, sizes), grid=(D // tile,),...  9.16 us
    pallas_call x4, Pallas kernels, spread(): pl.pallas_call(spread_kernel, grid=(D // tile,), in_specs=[table, table,...  6.21 us
  transfers between devices with their start and end apart: 27, of which 10 were waited for; matrix products, arithmetic and copies ran while one was open for 2% of the time, Pallas kernels for 22%

profile of v4, /device:TPU:0, one launch (start us, length us, event | category | flops | bytes accessed | tf_op | source)
XLA Modules:
  0.0 254.3 jit_solution(5710128294237007132)
XLA Ops:
  6.4 8.1 %all-to-all-start = ((bf16[16,4,16,576]{3,2,1,0:T(8,128)(2,1)}), bf16[16,4,16,576]{3,2,1,0:T(8,128)(2,1)S(1)}, u32[]{:S(2)}, u32[]{:S(2)}) async-start(bf16[16,4,16,576]{3,2,1,0:T(8,128)(2,1)} %pad_maximum_fusion.1), calls=%async_computation | async-start | bytes 2621440 | tf_op jit(solution)/shard_map/all_to_all | solution.py:229
  15.1 20.9 %all-to-all-done.queries = bf16[16,4,16,576]{3,2,1,0:T(8,128)(2,1)S(1)} async-done(((bf16[16,4,16,576]{3,2,1,0:T(8,128)(2,1)}), bf16[16,4,16,576]{3,2,1,0:T(8,128)(2,1)S(1)}, u32[]{:S(2)}, u32[]{:S(2)}) %all-to-all-start) | async-done | bytes 1179680 | tf_op jit(solution)/shard_map/all_to_all | solution.py:229
  36.0 3.4 %shard_map.163 = bf16[16,4,16,512]{3,2,1,0:T(8,128)(2,1)} custom-call(s32[4]{0:T(128)S(1)} %copy-done.3, bf16[16,4,16,576]{3,2,1,0:T(8,128)(2,1)S(1)} %all-to-all-done.queries, bf16[4,128,512]{2,1,0:T(8,128)(2,1)S(1)} %fusion.7.keys, bf16[4,64,128]{2,1,0:T(8,128)(2,1)S(1)} %fusion.18.rotary_keys), custom_call_target="tpu_custom_call" | custom-call | tf_op jit(solution)/shard_map/pallas_call | solution.py:259
  39.4 3.7 %all-to-all-start.1 = ((bf16[16,4,16,512]{3,2,1,0:T(8,128)(2,1)}), bf16[16,4,16,512]{3,2,1,0:T(8,128)(2,1)S(1)}, u32[]{:S(2)}, u32[]{:S(2)}) async-start(bf16[16,4,16,512]{3,2,1,0:T(8,128)(2,1)} %shard_map.163), calls=%async_computation.1 | async-start | bytes 2097152 | tf_op jit(solution)/shard_map/all_to_all | solution.py:229
  43.2 15.9 %all-to-all-done.1 = bf16[16,4,16,512]{3,2,1,0:T(8,128)(2,1)S(1)} async-done(((bf16[16,4,16,512]{3,2,1,0:T(8,128)(2,1)}), bf16[16,4,16,512]{3,2,1,0:T(8,128)(2,1)S(1)}, u32[]{:S(2)}, u32[]{:S(2)}) %all-to-all-start.1) | async-done | bytes 1048608 | tf_op jit(solution)/shard_map/all_to_all | solution.py:229
  60.9 3.8 %convolution_convert_fusion = bf16[256,3584]{1,0:T(8,128)(2,1)} fusion(bf16[256,3584]{1,0:T(8,128)(2,1)} %collective-permute-done.3, bf16[256,3584]{1,0:T(8,128)(2,1)S(1)} %copy-done.12, bf16[32,8,4,128]{3,2,1,0:T(4,128)(2,1)S(1)} %bitcast.77), kind=kOutput, calls=%fused_computation | convolution fusion | flops 947781632 | bytes 5767168 | tf_op jit(solution)/shard_map/dot_general | solution.py:314
  64.8 3.8 %all-to-all-start.2 = ((bf16[16,16,3584]{2,1,0:T(8,128)(2,1)}), bf16[16,16,3584]{2,1,0:T(8,128)(2,1)S(1)}, u32[]{:S(2)}, u32[]{:S(2)}) async-start(bf16[16,16,3584]{2,1,0:T(8,128)(2,1)} %bitcast.70), calls=%async_computation.2 | async-start | bytes 3670016 | tf_op jit(solution)/shard_map/all_to_all | solution.py:229
  68.9 24.9 %all-to-all-done.2 = bf16[16,16,3584]{2,1,0:T(8,128)(2,1)S(1)} async-done(((bf16[16,16,3584]{2,1,0:T(8,128)(2,1)}), bf16[16,16,3584]{2,1,0:T(8,128)(2,1)S(1)}, u32[]{:S(2)}, u32[]{:S(2)}) %all-to-all-start.2) | async-done | bytes 1835040 | tf_op jit(solution)/shard_map/all_to_all | solution.py:229
  94.7 27.6 %all_to_all.25 = bf16[16,16,3712]{2,1,0:T(8,128)(2,1)S(1)} all-to-all(bf16[16,16,3712]{2,1,0:T(8,128)(2,1)S(1)} %broadcast_in_dim.2), channel_id=1, replica_groups={{0,32,64,96,2,34,66,98,4,36,68,100,6,38,70,102},{8,40,72,104,10,42,74,1..., dimensions={0} | all-to-all | bytes 3801088 | tf_op jit(solution)/shard_map/all_to_all | solution.py:59
  130.2 3.1 %copy-done = bf16[1,3584,1024]{2,1,0:T(8,128)(2,1)S(1)} copy-done((bf16[1,3584,1024]{2,1,0:T(8,128)(2,1)S(1)}, bf16[1,3584,1024]{2,1,0:T(8,128)(2,1)}, u32[]{:S(2)}) %copy-start) | copy-done | bytes 7340056
  133.3 6.2 %collective-permute-done.4.refs_0_.refs_2_ = bf16[128,3712]{1,0:T(8,128)(2,1)} collective-permute-done((bf16[128,3712]{1,0:T(8,128)(2,1)}, bf16[128,3712]{1,0:T(8,128)(2,1)}, u32[]{:S(2)}, u32[]{:S(2)}) %collective-permute-start.4) | collective-permute-done | bytes 950304 | tf_op jit(solution)/shard_map/ppermute | solution.py:55
  139.6 2.7 %shard_map.165 = (bf16[128,3584]{1,0:T(8,128)(2,1)S(1)}, bf16[128,3584]{1,0:T(8,128)(2,1)S(1)}, bf16[1,2,256,128]{3,2,1,0:T(8,128)(2,1)S(1)}, f32[1,2,256,128]{3,2,1,0:T(8,128)S(1)}) custom-call(s32[2]{0:T(128)S(1)} %pad_add_fusion.experts, bf16[128,3712]{1,0:T(8,128)(2,1)} %collective-permute-done.4.refs_0_.refs_2_, ...), custom_call_target="tpu_custom_call" | custom-call | tf_op jit(solution)/shard_map/pallas_call | solution.py:125
  145.9 9.8 %shard_map.166 = (bf16[128,3584]{1,0:T(8,128)(2,1)S(1)}, bf16[128,3584]{1,0:T(8,128)(2,1)S(1)}) custom-call(bf16[128,3584]{1,0:T(8,128)(2,1)S(1)} %get-tuple-element.37.own, bf16[128,3584]{1,0:T(8,128)(2,1)S(1)} %collective-permute-done.10.twin, bf16[1,3584,1024]{2,1,0:T(8,128)(2,1)S(1)} %bitcast.65, bf16[1,3584,1024]{2,1,0:T(8,128)(2,1)} %upward.7, ...), custom_call_target="tpu_custom_call" | custom-call | flops 458752 | bytes 458752 | tf_op jit(solution)/shard_map/pallas_call | solution.py:169
  155.7 2.2 shard_map.167
  160.5 9.8 %shard_map.168 = (bf16[128,3584]{1,0:T(8,128)(2,1)S(1)}, bf16[128,3584]{1,0:T(8,128)(2,1)S(1)}) custom-call(bf16[128,3584]{1,0:T(8,128)(2,1)S(1)} %get-tuple-element.40.own, bf16[128,3584]{1,0:T(8,128)(2,1)S(1)} %collective-permute-done.11.twin, bf16[1,3584,1024]{2,1,0:T(8,128)(2,1)S(1)} %bitcast.65, bf16[1,3584,1024]{2,1,0:T(8,128)(2,1)} %upward.7, ...), custom_call_target="tpu_custom_call" | custom-call | flops 458752 | bytes 458752 | tf_op jit(solution)/shard_map/pallas_call | solution.py:169
  171.9 2.2 shard_map.170
  175.2 2.3 collective-permute-start.14
  177.6 10.0 %shard_map.171 = (bf16[128,3584]{1,0:T(8,128)(2,1)S(1)}, bf16[128,3584]{1,0:T(8,128)(2,1)S(1)}) custom-call(bf16[128,3584]{1,0:T(8,128)(2,1)S(1)} %get-tuple-element.47.own, bf16[128,3584]{1,0:T(8,128)(2,1)S(1)} %collective-permute-done.13.twin, bf16[1,3584,1024]{2,1,0:T(8,128)(2,1)S(1)} %bitcast.65, bf16[1,3584,1024]{2,1,0:T(8,128)(2,1)} %upward.7, ...), custom_call_target="tpu_custom_call" | custom-call | flops 458752 | bytes 458752 | tf_op jit(solution)/shard_map/pallas_call | solution.py:169
  193.4 3.3 %collective-permute-start.22 = (bf16[128,3584]{1,0:T(8,128)(2,1)S(1)}, bf16[128,3584]{1,0:T(8,128)(2,1)S(1)}, u32[]{:S(2)}, u32[]{:S(2)}) collective-permute-start(bf16[128,3584]{1,0:T(8,128)(2,1)S(1)} %get-tuple-element.68), channel_id=1, source_target_pairs={{0,24},{1,7},{2,26},{3,1},{4,28},{5,3},{6,30},{7,5},{8,0},{9,15},{... | collective-permute-start | bytes 2752520 | tf_op jit(solution)/shard_map/ppermute | solution.py:55
  196.7 9.8 %shard_map.173 = (bf16[128,3584]{1,0:T(8,128)(2,1)S(1)}, bf16[128,3584]{1,0:T(8,128)(2,1)S(1)}) custom-call(bf16[128,3584]{1,0:T(8,128)(2,1)S(1)} %get-tuple-element.53.own, bf16[128,3584]{1,0:T(8,128)(2,1)S(1)} %collective-permute-done.16.twin, bf16[1,3584,1024]{2,1,0:T(8,128)(2,1)S(1)} %bitcast.65, bf16[1,3584,1024]{2,1,0:T(8,128)(2,1)} %upward.7, ...), custom_call_target="tpu_custom_call" | custom-call | flops 458752 | bytes 458752 | tf_op jit(solution)/shard_map/pallas_call | solution.py:169
  208.5 3.3 %collective-permute-start.23 = (bf16[128,3584]{1,0:T(8,128)(2,1)S(1)}, bf16[128,3584]{1,0:T(8,128)(2,1)S(1)}, u32[]{:S(2)}, u32[]{:S(2)}) collective-permute-start(bf16[128,3584]{1,0:T(8,128)(2,1)S(1)} %add.70), channel_id=1, source_target_pairs={{0,24},{1,7},{2,26},{3,1},{4,28},{5,3},{6,30},{7,5},{8,0},{9,15},{... | collective-permute-start | bytes 2752520 | tf_op jit(solution)/shard_map/ppermute | solution.py:55
  213.6 9.0 %collective-permute-done.23 = bf16[128,3584]{1,0:T(8,128)(2,1)S(1)} collective-permute-done((bf16[128,3584]{1,0:T(8,128)(2,1)S(1)}, bf16[128,3584]{1,0:T(8,128)(2,1)S(1)}, u32[]{:S(2)}, u32[]{:S(2)}) %collective-permute-start.23) | collective-permute-done | bytes 917536 | tf_op jit(solution)/shard_map/ppermute | solution.py:55
  223.0 3.6 %collective-permute-done.21 = bf16[128,3584]{1,0:T(8,128)(2,1)S(1)} collective-permute-done((bf16[128,3584]{1,0:T(8,128)(2,1)S(1)}, bf16[128,3584]{1,0:T(8,128)(2,1)S(1)}, u32[]{:S(2)}, u32[]{:S(2)}) %collective-permute-start.21) | collective-permute-done | bytes 917536 | tf_op jit(solution)/shard_map/ppermute | solution.py:55
  227.1 26.0 %all_to_all.26 = bf16[16,16,3584]{2,1,0:T(8,128)(2,1)S(1)} all-to-all(bf16[16,16,3584]{2,1,0:T(8,128)(2,1)S(1)} %bitcast.69), channel_id=1, replica_groups={{0,32,64,96,2,34,66,98,4,36,68,100,6,38,70,102},{8,40,72,104,10,42,74,1..., dimensions={0} | all-to-all | bytes 3670016 | tf_op jit(solution)/shard_map/all_to_all | solution.py:59
  (135 shorter events, 37.9 us)
Async XLA Ops:
  0.0 4.2 %collective-permute-start.1 = (bf16[2,128,512]{2,1,0:T(8,128)(2,1)}, bf16[2,128,512]{2,1,0:T(8,128)(2,1)S(1)}, u32[]{:S(2)}, u32[]{:S(2)}) collective-permute-start(bf16[2,128,512]{2,1,0:T(8,128)(2,1)} %param.19), channel_id=1, source_target_pairs={{0,1},{1,0},{2,3},{3,2},{4,5},{5,4},{6,7},{7,6},{8,9},{9,8},{10,11... | collective-permute-start | bytes 786440 | tf_op jit(solution)/shard_map/ppermute | solution.py:225
  6.4 29.6 %all-to-all-start = ((bf16[16,4,16,576]{3,2,1,0:T(8,128)(2,1)}), bf16[16,4,16,576]{3,2,1,0:T(8,128)(2,1)S(1)}, u32[]{:S(2)}, u32[]{:S(2)}) async-start(bf16[16,4,16,576]{3,2,1,0:T(8,128)(2,1)} %pad_maximum_fusion.1), calls=%async_computation | async-start | bytes 2621440 | tf_op jit(solution)/shard_map/all_to_all | solution.py:229
  14.6 45.8 %collective-permute-start.3 = (bf16[256,3584]{1,0:T(8,128)(2,1)}, bf16[256,3584]{1,0:T(8,128)(2,1)}, u32[]{:S(2)}, u32[]{:S(2)}) collective-permute-start(bf16[256,3584]{1,0:T(8,128)(2,1)} %param.21), channel_id=1, source_target_pairs={{0,1},{1,0},{2,3},{3,2},{4,5},{5,4},{6,7},{7,6},{8,9},{9,8},{10,11... | collective-permute-start | bytes 5505032 | tf_op jit(solution)/shard_map/ppermute | solution.py:225
  39.4 19.7 %all-to-all-start.1 = ((bf16[16,4,16,512]{3,2,1,0:T(8,128)(2,1)}), bf16[16,4,16,512]{3,2,1,0:T(8,128)(2,1)S(1)}, u32[]{:S(2)}, u32[]{:S(2)}) async-start(bf16[16,4,16,512]{3,2,1,0:T(8,128)(2,1)} %shard_map.163), calls=%async_computation.1 | async-start | bytes 2097152 | tf_op jit(solution)/shard_map/all_to_all | solution.py:229
  43.1 16.3 %collective-permute-start = (bf16[2,512,128]{2,1,0:T(8,128)(2,1)S(1)}, bf16[2,512,128]{2,1,0:T(8,128)(2,1)S(1)}, u32[]{:S(2)}, u32[]{:S(2)}) collective-permute-start(bf16[2,512,128]{2,1,0:T(8,128)(2,1)S(1)} %copy-done.14), channel_id=1, source_target_pairs={{0,1},{1,0},{2,3},{3,2},{4,5},{5,4},{6,7},{7,6},{8,9},{9,8},{10,11... | collective-permute-start | bytes 786440 | tf_op jit(solution)/shard_map/ppermute | solution.py:225
  64.8 29.1 %all-to-all-start.2 = ((bf16[16,16,3584]{2,1,0:T(8,128)(2,1)}), bf16[16,16,3584]{2,1,0:T(8,128)(2,1)S(1)}, u32[]{:S(2)}, u32[]{:S(2)}) async-start(bf16[16,16,3584]{2,1,0:T(8,128)(2,1)} %bitcast.70), calls=%async_computation.2 | async-start | bytes 3670016 | tf_op jit(solution)/shard_map/all_to_all | solution.py:229
  124.2 15.3 %collective-permute-start.4 = (bf16[128,3712]{1,0:T(8,128)(2,1)}, bf16[128,3712]{1,0:T(8,128)(2,1)}, u32[]{:S(2)}, u32[]{:S(2)}) collective-permute-start(bf16[128,3712]{1,0:T(8,128)(2,1)} %bitcast.26), channel_id=1, source_target_pairs={{0,8},{1,3},{2,10},{3,5},{4,12},{5,7},{6,14},{7,1},{8,16},{9,11},{... | collective-permute-start | bytes 2850824 | tf_op jit(solution)/shard_map/ppermute | solution.py:55
  125.5 14.1 %collective-permute-start.6 = (bf16[128,3712]{1,0:T(8,128)(2,1)}, bf16[128,3712]{1,0:T(8,128)(2,1)}, u32[]{:S(2)}, u32[]{:S(2)}) collective-permute-start(bf16[128,3712]{1,0:T(8,128)(2,1)} %bitcast.27), channel_id=1, source_target_pairs={{0,24},{1,7},{2,26},{3,1},{4,28},{5,3},{6,30},{7,5},{8,0},{9,15},{... | collective-permute-start | bytes 2850824 | tf_op jit(solution)/shard_map/ppermute | solution.py:55
  127.4 28.3 %collective-permute-start.8 = (bf16[128,3712]{1,0:T(8,128)(2,1)}, bf16[128,3712]{1,0:T(8,128)(2,1)S(1)}, u32[]{:S(2)}, u32[]{:S(2)}) collective-permute-start(bf16[128,3712]{1,0:T(8,128)(2,1)} %bitcast.26), channel_id=1, source_target_pairs={{0,24},{1,7},{2,26},{3,1},{4,28},{5,3},{6,30},{7,5},{8,0},{9,15},{... | collective-permute-start | bytes 2850824 | tf_op jit(solution)/shard_map/ppermute | solution.py:55
  128.8 26.9 %collective-permute-start.9 = (bf16[128,3712]{1,0:T(8,128)(2,1)}, bf16[128,3712]{1,0:T(8,128)(2,1)S(1)}, u32[]{:S(2)}, u32[]{:S(2)}) collective-permute-start(bf16[128,3712]{1,0:T(8,128)(2,1)} %bitcast.27), channel_id=1, source_target_pairs={{0,8},{1,3},{2,10},{3,5},{4,12},{5,7},{6,14},{7,1},{8,16},{9,11},{... | collective-permute-start | bytes 2850824 | tf_op jit(solution)/shard_map/ppermute | solution.py:55
  142.3 3.6 %collective-permute-start.10 = (bf16[128,3584]{1,0:T(8,128)(2,1)S(1)}, bf16[128,3584]{1,0:T(8,128)(2,1)S(1)}, u32[]{:S(2)}, u32[]{:S(2)}) collective-permute-start(bf16[128,3584]{1,0:T(8,128)(2,1)S(1)} %get-tuple-element.38), channel_id=1, source_target_pairs={{0,1},{1,0},{2,3},{3,2},{4,5},{5,4},{6,7},{7,6},{8,9},{9,8},{10,11... | collective-permute-start | bytes 2752520 | tf_op jit(solution)/shard_map/ppermute | solution.py:225
  142.4 29.5 %collective-permute-start.5 = (bf16[128,3712]{1,0:T(8,128)(2,1)}, bf16[128,3712]{1,0:T(8,128)(2,1)S(1)}, u32[]{:S(2)}, u32[]{:S(2)}) collective-permute-start(bf16[128,3712]{1,0:T(8,128)(2,1)} %collective-permute-done.4.refs_0_.refs_2_), channel_id=1, source_target_pairs={{0,8},{1,3},{2,10},{3,5},{4,12},{5,7},{6,14},{7,1},{8,16},{9,11},{... | collective-permute-start | bytes 2850824 | tf_op jit(solution)/shard_map/ppermute | solution.py:55
  144.0 27.9 %collective-permute-start.7 = (bf16[128,3712]{1,0:T(8,128)(2,1)}, bf16[128,3712]{1,0:T(8,128)(2,1)S(1)}, u32[]{:S(2)}, u32[]{:S(2)}) collective-permute-start(bf16[128,3712]{1,0:T(8,128)(2,1)} %collective-permute-done.6.refs_1_.refs_3_), channel_id=1, source_target_pairs={{0,24},{1,7},{2,26},{3,1},{4,28},{5,3},{6,30},{7,5},{8,0},{9,15},{... | collective-permute-start | bytes 2850824 | tf_op jit(solution)/shard_map/ppermute | solution.py:55
  158.0 12.3 %collective-permute-start.12 = (bf16[128,3584]{1,0:T(8,128)(2,1)S(1)}, bf16[128,3584]{1,0:T(8,128)(2,1)S(1)}, u32[]{:S(2)}, u32[]{:S(2)}) collective-permute-start(bf16[128,3584]{1,0:T(8,128)(2,1)S(1)} %get-tuple-element.45), channel_id=1, source_target_pairs={{0,1},{1,0},{2,3},{3,2},{4,5},{5,4},{6,7},{7,6},{8,9},{9,8},{10,11... | collective-permute-start | bytes 2752520 | tf_op jit(solution)/shard_map/ppermute | solution.py:225
  174.3 14.6 %collective-permute-start.15 = (bf16[128,3584]{1,0:T(8,128)(2,1)S(1)}, bf16[128,3584]{1,0:T(8,128)(2,1)S(1)}, u32[]{:S(2)}, u32[]{:S(2)}) collective-permute-start(bf16[128,3584]{1,0:T(8,128)(2,1)S(1)} %get-tuple-element.50), channel_id=1, source_target_pairs={{0,8},{1,3},{2,10},{3,5},{4,12},{5,7},{6,14},{7,1},{8,16},{9,11},{... | collective-permute-start | bytes 2752520 | tf_op jit(solution)/shard_map/ppermute | solution.py:55
  175.2 13.7 %collective-permute-start.14 = (bf16[128,3584]{1,0:T(8,128)(2,1)S(1)}, bf16[128,3584]{1,0:T(8,128)(2,1)S(1)}, u32[]{:S(2)}, u32[]{:S(2)}) collective-permute-start(bf16[128,3584]{1,0:T(8,128)(2,1)S(1)} %get-tuple-element.46.refs_5_), channel_id=1, source_target_pairs={{0,24},{1,7},{2,26},{3,1},{4,28},{5,3},{6,30},{7,5},{8,0},{9,15},{... | collective-permute-start | bytes 2752520 | tf_op jit(solution)/shard_map/ppermute | solution.py:55
  187.6 4.3 %collective-permute-start.19 = (bf16[128,3584]{1,0:T(8,128)(2,1)S(1)}, bf16[128,3584]{1,0:T(8,128)(2,1)S(1)}, u32[]{:S(2)}, u32[]{:S(2)}) collective-permute-start(bf16[128,3584]{1,0:T(8,128)(2,1)S(1)} %get-tuple-element.64), channel_id=1, source_target_pairs={{0,1},{1,0},{2,3},{3,2},{4,5},{5,4},{6,7},{7,6},{8,9},{9,8},{10,11... | collective-permute-start | bytes 2752520 | tf_op jit(solution)/shard_map/ppermute | solution.py:225
  191.1 5.7 %collective-permute-start.16 = (bf16[128,3584]{1,0:T(8,128)(2,1)S(1)}, bf16[128,3584]{1,0:T(8,128)(2,1)S(1)}, u32[]{:S(2)}, u32[]{:S(2)}) collective-permute-start(bf16[128,3584]{1,0:T(8,128)(2,1)S(1)} %get-tuple-element.54), channel_id=1, source_target_pairs={{0,1},{1,0},{2,3},{3,2},{4,5},{5,4},{6,7},{7,6},{8,9},{9,8},{10,11... | collective-permute-start | bytes 2752520 | tf_op jit(solution)/shard_map/ppermute | solution.py:225
  191.4 15.3 %collective-permute-start.18 = (bf16[128,3584]{1,0:T(8,128)(2,1)S(1)}, bf16[128,3584]{1,0:T(8,128)(2,1)S(1)}, u32[]{:S(2)}, u32[]{:S(2)}) collective-permute-start(bf16[128,3584]{1,0:T(8,128)(2,1)S(1)} %get-tuple-element.60), channel_id=1, source_target_pairs={{0,1},{1,0},{2,3},{3,2},{4,5},{5,4},{6,7},{7,6},{8,9},{9,8},{10,11... | collective-permute-start | bytes 2752520 | tf_op jit(solution)/shard_map/ppermute | solution.py:225
  193.4 14.8 %collective-permute-start.22 = (bf16[128,3584]{1,0:T(8,128)(2,1)S(1)}, bf16[128,3584]{1,0:T(8,128)(2,1)S(1)}, u32[]{:S(2)}, u32[]{:S(2)}) collective-permute-start(bf16[128,3584]{1,0:T(8,128)(2,1)S(1)} %get-tuple-element.68), channel_id=1, source_target_pairs={{0,24},{1,7},{2,26},{3,1},{4,28},{5,3},{6,30},{7,5},{8,0},{9,15},{... | collective-permute-start | bytes 2752520 | tf_op jit(solution)/shard_map/ppermute | solution.py:55
  196.7 15.0 %collective-permute-start.20 = (bf16[128,3584]{1,0:T(8,128)(2,1)S(1)}, bf16[128,3584]{1,0:T(8,128)(2,1)S(1)}, u32[]{:S(2)}, u32[]{:S(2)}) collective-permute-start(bf16[128,3584]{1,0:T(8,128)(2,1)S(1)} %get-tuple-element.65), channel_id=1, source_target_pairs={{0,8},{1,3},{2,10},{3,5},{4,12},{5,7},{6,14},{7,1},{8,16},{9,11},{... | collective-permute-start | bytes 2752520 | tf_op jit(solution)/shard_map/ppermute | solution.py:55
  206.6 5.5 %collective-permute-start.17 = (bf16[128,3584]{1,0:T(8,128)(2,1)S(1)}, bf16[128,3584]{1,0:T(8,128)(2,1)S(1)}, u32[]{:S(2)}, u32[]{:S(2)}) collective-permute-start(bf16[128,3584]{1,0:T(8,128)(2,1)S(1)} %get-tuple-element.56), channel_id=1, source_target_pairs={{0,1},{1,0},{2,3},{3,2},{4,5},{5,4},{6,7},{7,6},{8,9},{9,8},{10,11... | collective-permute-start | bytes 2752520 | tf_op jit(solution)/shard_map/ppermute | solution.py:225
  208.5 14.2 %collective-permute-start.23 = (bf16[128,3584]{1,0:T(8,128)(2,1)S(1)}, bf16[128,3584]{1,0:T(8,128)(2,1)S(1)}, u32[]{:S(2)}, u32[]{:S(2)}) collective-permute-start(bf16[128,3584]{1,0:T(8,128)(2,1)S(1)} %add.70), channel_id=1, source_target_pairs={{0,24},{1,7},{2,26},{3,1},{4,28},{5,3},{6,30},{7,5},{8,0},{9,15},{... | collective-permute-start | bytes 2752520 | tf_op jit(solution)/shard_map/ppermute | solution.py:55
  212.0 14.7 %collective-permute-start.21 = (bf16[128,3584]{1,0:T(8,128)(2,1)S(1)}, bf16[128,3584]{1,0:T(8,128)(2,1)S(1)}, u32[]{:S(2)}, u32[]{:S(2)}) collective-permute-start(bf16[128,3584]{1,0:T(8,128)(2,1)S(1)} %add.67), channel_id=1, source_target_pairs={{0,8},{1,3},{2,10},{3,5},{4,12},{5,7},{6,14},{7,1},{8,16},{9,11},{... | collective-permute-start | bytes 2752520 | tf_op jit(solution)/shard_map/ppermute | solution.py:55
  (20 other events, 220.2 us)

commit v5 on v4

--- a/solution.py
+++ b/solution.py
@@ -119,7 +119,7 @@
 def pick(experts, pieces, after=()):
     sizes = tuple(p.shape[0] for p in pieces)
     blocks = sum(sizes) // BLOCK
-    tile = 1792
+    tile = D
     spec = pl.BlockSpec((blocks, 2, BLOCK, SLOTS), lambda i: (0, 0, 0, 0))
     out = pl.BlockSpec((blocks * SLOTS, tile), lambda i: (0, i))
     return pl.pallas_call(
@@ -137,7 +137,7 @@
             jax.ShapeDtypeStruct((blocks, 2, BLOCK, SLOTS), jnp.float32),
         ],
         scratch_shapes=[pltpu.VMEM((blocks, 2, SLOTS, BLOCK), jnp.bfloat16)],
-        compiler_params=pltpu.CompilerParams(vmem_limit_bytes=10 * 2**20),
+        compiler_params=pltpu.CompilerParams(vmem_limit_bytes=14 * 2**20),
     )(experts, *pieces, *pieces, *after)
 
 
@@ -208,7 +208,7 @@
 
 
 def spread(put, weight, own, twin):
-    tile = 1792
+    tile = D
     table = pl.BlockSpec((1, 2, BLOCK, SLOTS), lambda i: (0, 0, 0, 0))
     columns = pl.BlockSpec((SLOTS, tile), lambda i: (0, i))
     return pl.pallas_call(
@@ -217,7 +217,7 @@
         in_specs=[table, table, columns, columns],
         out_specs=[pl.BlockSpec((BLOCK // 2, tile), lambda i: (0, i))] * 2,
         out_shape=[jax.ShapeDtypeStruct((BLOCK // 2, D), jnp.bfloat16)] * 2,
-        compiler_params=pltpu.CompilerParams(vmem_limit_bytes=10 * 2**20),
+        compiler_params=pltpu.CompilerParams(vmem_limit_bytes=14 * 2**20),
     )(put, weight, own, twin)
 
 

time: 255 us -> 251 us (0.984)
  Pallas kernels: 58.3 us -> 54.4 us
  transfers between devices with their start and end apart: 27 -> 27, of which waited for: 10 -> 10; matrix products, arithmetic and copies ran while one was open for 2% -> 2% of each run, Pallas kernels for 22% -> 21%
where the time goes in v5:
time: 251 us
  waiting for transfers between devices  85.3 us (34%)
  Pallas kernels  54.4 us (22%)
  blocking collectives  53.4 us (21%)
  starting transfers between devices  37.2 us (15%)
  local copies, waits for them, and re-layouts  9.91 us (4%)
  matrix products  4.99 us (2%)
  other arithmetic  4.69 us (2%)
    all_to_all x3, waiting for transfers between devices, exchange(): lax.all_to_all(x, 'ep', 0, 0, tiled=True, axis_index_groups=SAME_CORE)  61.8 us
    all_to_all x2, blocking collectives, plane_exchange(): lax.all_to_all(x, ('dp', 'ep'), 0, 0, tiled=True, axis_index_groups=PLANES)  53.4 us
    pallas_call x4, Pallas kernels, run_experts(): pl.pallas_call(experts_kernel, grid=(hidden // tile,), in_specs=[whole, w...  39.5 us
    ppermute x12, waiting for transfers between devices, shift(): return lax.ppermute(x, 'ep', pairs)  20.5 us
    ppermute x12, starting transfers between devices, shift(): return lax.ppermute(x, 'ep', pairs)  19 us
    all_to_all x3, starting transfers between devices, exchange(): lax.all_to_all(x, 'ep', 0, 0, tiled=True, axis_index_groups=SAME_CORE)  15.6 us
    pallas_call x4, Pallas kernels, pick(): pl.pallas_call(functools.partial(pick_kernel, sizes), grid=(D // tile,),...  7.01 us
  transfers between devices with their start and end apart: 27, of which 10 were waited for; matrix products, arithmetic and copies ran while one was open for 2% of the time, Pallas kernels for 21%

profile of v5, /device:TPU:0, one launch (start us, length us, event | category | flops | bytes accessed | tf_op | source)
XLA Modules:
  0.0 250.6 jit_solution(18149161964688751926)
XLA Ops:
  6.4 8.1 %all-to-all-start = ((bf16[16,4,16,576]{3,2,1,0:T(8,128)(2,1)}), bf16[16,4,16,576]{3,2,1,0:T(8,128)(2,1)S(1)}, u32[]{:S(2)}, u32[]{:S(2)}) async-start(bf16[16,4,16,576]{3,2,1,0:T(8,128)(2,1)} %pad_maximum_fusion.1), calls=%async_computation | async-start | bytes 2621440 | tf_op jit(solution)/shard_map/all_to_all | solution.py:229
  15.1 20.9 %all-to-all-done.queries = bf16[16,4,16,576]{3,2,1,0:T(8,128)(2,1)S(1)} async-done(((bf16[16,4,16,576]{3,2,1,0:T(8,128)(2,1)}), bf16[16,4,16,576]{3,2,1,0:T(8,128)(2,1)S(1)}, u32[]{:S(2)}, u32[]{:S(2)}) %all-to-all-start) | async-done | bytes 1179680 | tf_op jit(solution)/shard_map/all_to_all | solution.py:229
  36.0 3.4 %shard_map.163 = bf16[16,4,16,512]{3,2,1,0:T(8,128)(2,1)} custom-call(s32[4]{0:T(128)S(1)} %copy-done.3, bf16[16,4,16,576]{3,2,1,0:T(8,128)(2,1)S(1)} %all-to-all-done.queries, bf16[4,128,512]{2,1,0:T(8,128)(2,1)S(1)} %fusion.7.keys, bf16[4,64,128]{2,1,0:T(8,128)(2,1)S(1)} %fusion.18.rotary_keys), custom_call_target="tpu_custom_call" | custom-call | tf_op jit(solution)/shard_map/pallas_call | solution.py:259
  39.4 3.7 %all-to-all-start.1 = ((bf16[16,4,16,512]{3,2,1,0:T(8,128)(2,1)}), bf16[16,4,16,512]{3,2,1,0:T(8,128)(2,1)S(1)}, u32[]{:S(2)}, u32[]{:S(2)}) async-start(bf16[16,4,16,512]{3,2,1,0:T(8,128)(2,1)} %shard_map.163), calls=%async_computation.1 | async-start | bytes 2097152 | tf_op jit(solution)/shard_map/all_to_all | solution.py:229
  43.2 15.9 %all-to-all-done.1 = bf16[16,4,16,512]{3,2,1,0:T(8,128)(2,1)S(1)} async-done(((bf16[16,4,16,512]{3,2,1,0:T(8,128)(2,1)}), bf16[16,4,16,512]{3,2,1,0:T(8,128)(2,1)S(1)}, u32[]{:S(2)}, u32[]{:S(2)}) %all-to-all-start.1) | async-done | bytes 1048608 | tf_op jit(solution)/shard_map/all_to_all | solution.py:229
  60.9 3.8 %convolution_convert_fusion = bf16[256,3584]{1,0:T(8,128)(2,1)} fusion(bf16[256,3584]{1,0:T(8,128)(2,1)} %collective-permute-done.3, bf16[256,3584]{1,0:T(8,128)(2,1)S(1)} %copy-done.12, bf16[32,8,4,128]{3,2,1,0:T(4,128)(2,1)S(1)} %bitcast.77), kind=kOutput, calls=%fused_computation | convolution fusion | flops 947781632 | bytes 5767168 | tf_op jit(solution)/shard_map/dot_general | solution.py:314
  64.8 3.8 %all-to-all-start.2 = ((bf16[16,16,3584]{2,1,0:T(8,128)(2,1)}), bf16[16,16,3584]{2,1,0:T(8,128)(2,1)S(1)}, u32[]{:S(2)}, u32[]{:S(2)}) async-start(bf16[16,16,3584]{2,1,0:T(8,128)(2,1)} %bitcast.70), calls=%async_computation.2 | async-start | bytes 3670016 | tf_op jit(solution)/shard_map/all_to_all | solution.py:229
  68.9 24.9 %all-to-all-done.2 = bf16[16,16,3584]{2,1,0:T(8,128)(2,1)S(1)} async-done(((bf16[16,16,3584]{2,1,0:T(8,128)(2,1)}), bf16[16,16,3584]{2,1,0:T(8,128)(2,1)S(1)}, u32[]{:S(2)}, u32[]{:S(2)}) %all-to-all-start.2) | async-done | bytes 1835040 | tf_op jit(solution)/shard_map/all_to_all | solution.py:229
  94.7 27.6 %all_to_all.25 = bf16[16,16,3712]{2,1,0:T(8,128)(2,1)S(1)} all-to-all(bf16[16,16,3712]{2,1,0:T(8,128)(2,1)S(1)} %broadcast_in_dim.2), channel_id=1, replica_groups={{0,32,64,96,2,34,66,98,4,36,68,100,6,38,70,102},{8,40,72,104,10,42,74,1..., dimensions={0} | all-to-all | bytes 3801088 | tf_op jit(solution)/shard_map/all_to_all | solution.py:59
  130.2 3.1 %copy-done = bf16[1,3584,1024]{2,1,0:T(8,128)(2,1)S(1)} copy-done((bf16[1,3584,1024]{2,1,0:T(8,128)(2,1)S(1)}, bf16[1,3584,1024]{2,1,0:T(8,128)(2,1)}, u32[]{:S(2)}) %copy-start) | copy-done | bytes 7340056
  133.3 6.2 %collective-permute-done.4.refs_0_.refs_2_ = bf16[128,3712]{1,0:T(8,128)(2,1)} collective-permute-done((bf16[128,3712]{1,0:T(8,128)(2,1)}, bf16[128,3712]{1,0:T(8,128)(2,1)}, u32[]{:S(2)}, u32[]{:S(2)}) %collective-permute-start.4) | collective-permute-done | bytes 950304 | tf_op jit(solution)/shard_map/ppermute | solution.py:55
  139.6 2.5 shard_map.165
  143.8 1.9 collective-permute-start.7
  145.7 9.8 %shard_map.166 = (bf16[128,3584]{1,0:T(8,128)(2,1)S(1)}, bf16[128,3584]{1,0:T(8,128)(2,1)S(1)}) custom-call(bf16[128,3584]{1,0:T(8,128)(2,1)S(1)} %get-tuple-element.37.own, bf16[128,3584]{1,0:T(8,128)(2,1)S(1)} %collective-permute-done.10.twin, bf16[1,3584,1024]{2,1,0:T(8,128)(2,1)S(1)} %bitcast.65, bf16[1,3584,1024]{2,1,0:T(8,128)(2,1)} %upward.7, ...), custom_call_target="tpu_custom_call" | custom-call | flops 458752 | bytes 458752 | tf_op jit(solution)/shard_map/pallas_call | solution.py:169
  157.7 2.0 collective-permute-done.11.twin
  159.6 9.8 %shard_map.168 = (bf16[128,3584]{1,0:T(8,128)(2,1)S(1)}, bf16[128,3584]{1,0:T(8,128)(2,1)S(1)}) custom-call(bf16[128,3584]{1,0:T(8,128)(2,1)S(1)} %get-tuple-element.40.own, bf16[128,3584]{1,0:T(8,128)(2,1)S(1)} %collective-permute-done.11.twin, bf16[1,3584,1024]{2,1,0:T(8,128)(2,1)S(1)} %bitcast.65, bf16[1,3584,1024]{2,1,0:T(8,128)(2,1)} %upward.7, ...), custom_call_target="tpu_custom_call" | custom-call | flops 458752 | bytes 458752 | tf_op jit(solution)/shard_map/pallas_call | solution.py:169
  173.3 2.3 collective-permute-start.14
  175.6 10.0 %shard_map.171 = (bf16[128,3584]{1,0:T(8,128)(2,1)S(1)}, bf16[128,3584]{1,0:T(8,128)(2,1)S(1)}) custom-call(bf16[128,3584]{1,0:T(8,128)(2,1)S(1)} %get-tuple-element.47.own, bf16[128,3584]{1,0:T(8,128)(2,1)S(1)} %collective-permute-done.13.twin, bf16[1,3584,1024]{2,1,0:T(8,128)(2,1)S(1)} %bitcast.65, bf16[1,3584,1024]{2,1,0:T(8,128)(2,1)} %upward.7, ...), custom_call_target="tpu_custom_call" | custom-call | flops 458752 | bytes 458752 | tf_op jit(solution)/shard_map/pallas_call | solution.py:169
  190.2 3.3 %collective-permute-start.22 = (bf16[128,3584]{1,0:T(8,128)(2,1)S(1)}, bf16[128,3584]{1,0:T(8,128)(2,1)S(1)}, u32[]{:S(2)}, u32[]{:S(2)}) collective-permute-start(bf16[128,3584]{1,0:T(8,128)(2,1)S(1)} %get-tuple-element.68), channel_id=1, source_target_pairs={{0,24},{1,7},{2,26},{3,1},{4,28},{5,3},{6,30},{7,5},{8,0},{9,15},{... | collective-permute-start | bytes 2752520 | tf_op jit(solution)/shard_map/ppermute | solution.py:55
  193.5 9.8 %shard_map.173 = (bf16[128,3584]{1,0:T(8,128)(2,1)S(1)}, bf16[128,3584]{1,0:T(8,128)(2,1)S(1)}) custom-call(bf16[128,3584]{1,0:T(8,128)(2,1)S(1)} %get-tuple-element.53.own, bf16[128,3584]{1,0:T(8,128)(2,1)S(1)} %collective-permute-done.16.twin, bf16[1,3584,1024]{2,1,0:T(8,128)(2,1)S(1)} %bitcast.65, bf16[1,3584,1024]{2,1,0:T(8,128)(2,1)} %upward.7, ...), custom_call_target="tpu_custom_call" | custom-call | flops 458752 | bytes 458752 | tf_op jit(solution)/shard_map/pallas_call | solution.py:169
  204.8 3.6 %collective-permute-start.23 = (bf16[128,3584]{1,0:T(8,128)(2,1)S(1)}, bf16[128,3584]{1,0:T(8,128)(2,1)S(1)}, u32[]{:S(2)}, u32[]{:S(2)}) collective-permute-start(bf16[128,3584]{1,0:T(8,128)(2,1)S(1)} %add.70), channel_id=1, source_target_pairs={{0,24},{1,7},{2,26},{3,1},{4,28},{5,3},{6,30},{7,5},{8,0},{9,15},{... | collective-permute-start | bytes 2752520 | tf_op jit(solution)/shard_map/ppermute | solution.py:55
  209.8 9.5 %collective-permute-done.23 = bf16[128,3584]{1,0:T(8,128)(2,1)S(1)} collective-permute-done((bf16[128,3584]{1,0:T(8,128)(2,1)S(1)}, bf16[128,3584]{1,0:T(8,128)(2,1)S(1)}, u32[]{:S(2)}, u32[]{:S(2)}) %collective-permute-start.23) | collective-permute-done | bytes 917536 | tf_op jit(solution)/shard_map/ppermute | solution.py:55
  219.6 3.6 %collective-permute-done.21 = bf16[128,3584]{1,0:T(8,128)(2,1)S(1)} collective-permute-done((bf16[128,3584]{1,0:T(8,128)(2,1)S(1)}, bf16[128,3584]{1,0:T(8,128)(2,1)S(1)}, u32[]{:S(2)}, u32[]{:S(2)}) %collective-permute-start.21) | collective-permute-done | bytes 917536 | tf_op jit(solution)/shard_map/ppermute | solution.py:55
  223.7 25.8 %all_to_all.26 = bf16[16,16,3584]{2,1,0:T(8,128)(2,1)S(1)} all-to-all(bf16[16,16,3584]{2,1,0:T(8,128)(2,1)S(1)} %bitcast.69), channel_id=1, replica_groups={{0,32,64,96,2,34,66,98,4,36,68,100,6,38,70,102},{8,40,72,104,10,42,74,1..., dimensions={0} | all-to-all | bytes 3670016 | tf_op jit(solution)/shard_map/all_to_all | solution.py:59
  (135 shorter events, 34.5 us)
Async XLA Ops:
  0.0 4.2 %collective-permute-start.1 = (bf16[2,128,512]{2,1,0:T(8,128)(2,1)}, bf16[2,128,512]{2,1,0:T(8,128)(2,1)S(1)}, u32[]{:S(2)}, u32[]{:S(2)}) collective-permute-start(bf16[2,128,512]{2,1,0:T(8,128)(2,1)} %param.19), channel_id=1, source_target_pairs={{0,1},{1,0},{2,3},{3,2},{4,5},{5,4},{6,7},{7,6},{8,9},{9,8},{10,11... | collective-permute-start | bytes 786440 | tf_op jit(solution)/shard_map/ppermute | solution.py:225
  6.4 29.6 %all-to-all-start = ((bf16[16,4,16,576]{3,2,1,0:T(8,128)(2,1)}), bf16[16,4,16,576]{3,2,1,0:T(8,128)(2,1)S(1)}, u32[]{:S(2)}, u32[]{:S(2)}) async-start(bf16[16,4,16,576]{3,2,1,0:T(8,128)(2,1)} %pad_maximum_fusion.1), calls=%async_computation | async-start | bytes 2621440 | tf_op jit(solution)/shard_map/all_to_all | solution.py:229
  14.6 45.8 %collective-permute-start.3 = (bf16[256,3584]{1,0:T(8,128)(2,1)}, bf16[256,3584]{1,0:T(8,128)(2,1)}, u32[]{:S(2)}, u32[]{:S(2)}) collective-permute-start(bf16[256,3584]{1,0:T(8,128)(2,1)} %param.21), channel_id=1, source_target_pairs={{0,1},{1,0},{2,3},{3,2},{4,5},{5,4},{6,7},{7,6},{8,9},{9,8},{10,11... | collective-permute-start | bytes 5505032 | tf_op jit(solution)/shard_map/ppermute | solution.py:225
  39.4 19.7 %all-to-all-start.1 = ((bf16[16,4,16,512]{3,2,1,0:T(8,128)(2,1)}), bf16[16,4,16,512]{3,2,1,0:T(8,128)(2,1)S(1)}, u32[]{:S(2)}, u32[]{:S(2)}) async-start(bf16[16,4,16,512]{3,2,1,0:T(8,128)(2,1)} %shard_map.163), calls=%async_computation.1 | async-start | bytes 2097152 | tf_op jit(solution)/shard_map/all_to_all | solution.py:229
  43.1 16.3 %collective-permute-start = (bf16[2,512,128]{2,1,0:T(8,128)(2,1)S(1)}, bf16[2,512,128]{2,1,0:T(8,128)(2,1)S(1)}, u32[]{:S(2)}, u32[]{:S(2)}) collective-permute-start(bf16[2,512,128]{2,1,0:T(8,128)(2,1)S(1)} %copy-done.14), channel_id=1, source_target_pairs={{0,1},{1,0},{2,3},{3,2},{4,5},{5,4},{6,7},{7,6},{8,9},{9,8},{10,11... | collective-permute-start | bytes 786440 | tf_op jit(solution)/shard_map/ppermute | solution.py:225
  64.8 29.1 %all-to-all-start.2 = ((bf16[16,16,3584]{2,1,0:T(8,128)(2,1)}), bf16[16,16,3584]{2,1,0:T(8,128)(2,1)S(1)}, u32[]{:S(2)}, u32[]{:S(2)}) async-start(bf16[16,16,3584]{2,1,0:T(8,128)(2,1)} %bitcast.70), calls=%async_computation.2 | async-start | bytes 3670016 | tf_op jit(solution)/shard_map/all_to_all | solution.py:229
  124.2 15.3 %collective-permute-start.4 = (bf16[128,3712]{1,0:T(8,128)(2,1)}, bf16[128,3712]{1,0:T(8,128)(2,1)}, u32[]{:S(2)}, u32[]{:S(2)}) collective-permute-start(bf16[128,3712]{1,0:T(8,128)(2,1)} %bitcast.26), channel_id=1, source_target_pairs={{0,8},{1,3},{2,10},{3,5},{4,12},{5,7},{6,14},{7,1},{8,16},{9,11},{... | collective-permute-start | bytes 2850824 | tf_op jit(solution)/shard_map/ppermute | solution.py:55
  125.5 14.1 %collective-permute-start.6 = (bf16[128,3712]{1,0:T(8,128)(2,1)}, bf16[128,3712]{1,0:T(8,128)(2,1)}, u32[]{:S(2)}, u32[]{:S(2)}) collective-permute-start(bf16[128,3712]{1,0:T(8,128)(2,1)} %bitcast.27), channel_id=1, source_target_pairs={{0,24},{1,7},{2,26},{3,1},{4,28},{5,3},{6,30},{7,5},{8,0},{9,15},{... | collective-permute-start | bytes 2850824 | tf_op jit(solution)/shard_map/ppermute | solution.py:55
  127.4 28.1 %collective-permute-start.8 = (bf16[128,3712]{1,0:T(8,128)(2,1)}, bf16[128,3712]{1,0:T(8,128)(2,1)S(1)}, u32[]{:S(2)}, u32[]{:S(2)}) collective-permute-start(bf16[128,3712]{1,0:T(8,128)(2,1)} %bitcast.26), channel_id=1, source_target_pairs={{0,24},{1,7},{2,26},{3,1},{4,28},{5,3},{6,30},{7,5},{8,0},{9,15},{... | collective-permute-start | bytes 2850824 | tf_op jit(solution)/shard_map/ppermute | solution.py:55
  128.8 26.8 %collective-permute-start.9 = (bf16[128,3712]{1,0:T(8,128)(2,1)}, bf16[128,3712]{1,0:T(8,128)(2,1)S(1)}, u32[]{:S(2)}, u32[]{:S(2)}) collective-permute-start(bf16[128,3712]{1,0:T(8,128)(2,1)} %bitcast.27), channel_id=1, source_target_pairs={{0,8},{1,3},{2,10},{3,5},{4,12},{5,7},{6,14},{7,1},{8,16},{9,11},{... | collective-permute-start | bytes 2850824 | tf_op jit(solution)/shard_map/ppermute | solution.py:55
  142.1 3.6 %collective-permute-start.10 = (bf16[128,3584]{1,0:T(8,128)(2,1)S(1)}, bf16[128,3584]{1,0:T(8,128)(2,1)S(1)}, u32[]{:S(2)}, u32[]{:S(2)}) collective-permute-start(bf16[128,3584]{1,0:T(8,128)(2,1)S(1)} %get-tuple-element.38), channel_id=1, source_target_pairs={{0,1},{1,0},{2,3},{3,2},{4,5},{5,4},{6,7},{7,6},{8,9},{9,8},{10,11... | collective-permute-start | bytes 2752520 | tf_op jit(solution)/shard_map/ppermute | solution.py:225
  142.2 28.4 %collective-permute-start.5 = (bf16[128,3712]{1,0:T(8,128)(2,1)}, bf16[128,3712]{1,0:T(8,128)(2,1)S(1)}, u32[]{:S(2)}, u32[]{:S(2)}) collective-permute-start(bf16[128,3712]{1,0:T(8,128)(2,1)} %collective-permute-done.4.refs_0_.refs_2_), channel_id=1, source_target_pairs={{0,8},{1,3},{2,10},{3,5},{4,12},{5,7},{6,14},{7,1},{8,16},{9,11},{... | collective-permute-start | bytes 2850824 | tf_op jit(solution)/shard_map/ppermute | solution.py:55
  143.8 26.8 %collective-permute-start.7 = (bf16[128,3712]{1,0:T(8,128)(2,1)}, bf16[128,3712]{1,0:T(8,128)(2,1)S(1)}, u32[]{:S(2)}, u32[]{:S(2)}) collective-permute-start(bf16[128,3712]{1,0:T(8,128)(2,1)} %collective-permute-done.6.refs_1_.refs_3_), channel_id=1, source_target_pairs={{0,24},{1,7},{2,26},{3,1},{4,28},{5,3},{6,30},{7,5},{8,0},{9,15},{... | collective-permute-start | bytes 2850824 | tf_op jit(solution)/shard_map/ppermute | solution.py:55
  157.2 12.3 %collective-permute-start.12 = (bf16[128,3584]{1,0:T(8,128)(2,1)S(1)}, bf16[128,3584]{1,0:T(8,128)(2,1)S(1)}, u32[]{:S(2)}, u32[]{:S(2)}) collective-permute-start(bf16[128,3584]{1,0:T(8,128)(2,1)S(1)} %get-tuple-element.45), channel_id=1, source_target_pairs={{0,1},{1,0},{2,3},{3,2},{4,5},{5,4},{6,7},{7,6},{8,9},{9,8},{10,11... | collective-permute-start | bytes 2752520 | tf_op jit(solution)/shard_map/ppermute | solution.py:225
  172.3 14.6 %collective-permute-start.15 = (bf16[128,3584]{1,0:T(8,128)(2,1)S(1)}, bf16[128,3584]{1,0:T(8,128)(2,1)S(1)}, u32[]{:S(2)}, u32[]{:S(2)}) collective-permute-start(bf16[128,3584]{1,0:T(8,128)(2,1)S(1)} %get-tuple-element.50), channel_id=1, source_target_pairs={{0,8},{1,3},{2,10},{3,5},{4,12},{5,7},{6,14},{7,1},{8,16},{9,11},{... | collective-permute-start | bytes 2752520 | tf_op jit(solution)/shard_map/ppermute | solution.py:55
  173.3 13.7 %collective-permute-start.14 = (bf16[128,3584]{1,0:T(8,128)(2,1)S(1)}, bf16[128,3584]{1,0:T(8,128)(2,1)S(1)}, u32[]{:S(2)}, u32[]{:S(2)}) collective-permute-start(bf16[128,3584]{1,0:T(8,128)(2,1)S(1)} %get-tuple-element.46.refs_5_), channel_id=1, source_target_pairs={{0,24},{1,7},{2,26},{3,1},{4,28},{5,3},{6,30},{7,5},{8,0},{9,15},{... | collective-permute-start | bytes 2752520 | tf_op jit(solution)/shard_map/ppermute | solution.py:55
  185.5 3.5 %collective-permute-start.19 = (bf16[128,3584]{1,0:T(8,128)(2,1)S(1)}, bf16[128,3584]{1,0:T(8,128)(2,1)S(1)}, u32[]{:S(2)}, u32[]{:S(2)}) collective-permute-start(bf16[128,3584]{1,0:T(8,128)(2,1)S(1)} %get-tuple-element.64), channel_id=1, source_target_pairs={{0,1},{1,0},{2,3},{3,2},{4,5},{5,4},{6,7},{7,6},{8,9},{9,8},{10,11... | collective-permute-start | bytes 2752520 | tf_op jit(solution)/shard_map/ppermute | solution.py:225
  188.5 5.0 %collective-permute-start.16 = (bf16[128,3584]{1,0:T(8,128)(2,1)S(1)}, bf16[128,3584]{1,0:T(8,128)(2,1)S(1)}, u32[]{:S(2)}, u32[]{:S(2)}) collective-permute-start(bf16[128,3584]{1,0:T(8,128)(2,1)S(1)} %get-tuple-element.54), channel_id=1, source_target_pairs={{0,1},{1,0},{2,3},{3,2},{4,5},{5,4},{6,7},{7,6},{8,9},{9,8},{10,11... | collective-permute-start | bytes 2752520 | tf_op jit(solution)/shard_map/ppermute | solution.py:225
  188.5 14.9 %collective-permute-start.18 = (bf16[128,3584]{1,0:T(8,128)(2,1)S(1)}, bf16[128,3584]{1,0:T(8,128)(2,1)S(1)}, u32[]{:S(2)}, u32[]{:S(2)}) collective-permute-start(bf16[128,3584]{1,0:T(8,128)(2,1)S(1)} %get-tuple-element.60), channel_id=1, source_target_pairs={{0,1},{1,0},{2,3},{3,2},{4,5},{5,4},{6,7},{7,6},{8,9},{9,8},{10,11... | collective-permute-start | bytes 2752520 | tf_op jit(solution)/shard_map/ppermute | solution.py:225
  190.2 14.4 %collective-permute-start.22 = (bf16[128,3584]{1,0:T(8,128)(2,1)S(1)}, bf16[128,3584]{1,0:T(8,128)(2,1)S(1)}, u32[]{:S(2)}, u32[]{:S(2)}) collective-permute-start(bf16[128,3584]{1,0:T(8,128)(2,1)S(1)} %get-tuple-element.68), channel_id=1, source_target_pairs={{0,24},{1,7},{2,26},{3,1},{4,28},{5,3},{6,30},{7,5},{8,0},{9,15},{... | collective-permute-start | bytes 2752520 | tf_op jit(solution)/shard_map/ppermute | solution.py:55
  193.5 14.9 %collective-permute-start.20 = (bf16[128,3584]{1,0:T(8,128)(2,1)S(1)}, bf16[128,3584]{1,0:T(8,128)(2,1)S(1)}, u32[]{:S(2)}, u32[]{:S(2)}) collective-permute-start(bf16[128,3584]{1,0:T(8,128)(2,1)S(1)} %get-tuple-element.65), channel_id=1, source_target_pairs={{0,8},{1,3},{2,10},{3,5},{4,12},{5,7},{6,14},{7,1},{8,16},{9,11},{... | collective-permute-start | bytes 2752520 | tf_op jit(solution)/shard_map/ppermute | solution.py:55
  203.3 5.3 %collective-permute-start.17 = (bf16[128,3584]{1,0:T(8,128)(2,1)S(1)}, bf16[128,3584]{1,0:T(8,128)(2,1)S(1)}, u32[]{:S(2)}, u32[]{:S(2)}) collective-permute-start(bf16[128,3584]{1,0:T(8,128)(2,1)S(1)} %get-tuple-element.56), channel_id=1, source_target_pairs={{0,1},{1,0},{2,3},{3,2},{4,5},{5,4},{6,7},{7,6},{8,9},{9,8},{10,11... | collective-permute-start | bytes 2752520 | tf_op jit(solution)/shard_map/ppermute | solution.py:225
  204.8 14.5 %collective-permute-start.23 = (bf16[128,3584]{1,0:T(8,128)(2,1)S(1)}, bf16[128,3584]{1,0:T(8,128)(2,1)S(1)}, u32[]{:S(2)}, u32[]{:S(2)}) collective-permute-start(bf16[128,3584]{1,0:T(8,128)(2,1)S(1)} %add.70), channel_id=1, source_target_pairs={{0,24},{1,7},{2,26},{3,1},{4,28},{5,3},{6,30},{7,5},{8,0},{9,15},{... | collective-permute-start | bytes 2752520 | tf_op jit(solution)/shard_map/ppermute | solution.py:55
  208.6 14.7 %collective-permute-start.21 = (bf16[128,3584]{1,0:T(8,128)(2,1)S(1)}, bf16[128,3584]{1,0:T(8,128)(2,1)S(1)}, u32[]{:S(2)}, u32[]{:S(2)}) collective-permute-start(bf16[128,3584]{1,0:T(8,128)(2,1)S(1)} %add.67), channel_id=1, source_target_pairs={{0,8},{1,3},{2,10},{3,5},{4,12},{5,7},{6,14},{7,1},{8,16},{9,11},{... | collective-permute-start | bytes 2752520 | tf_op jit(solution)/shard_map/ppermute | solution.py:55
  (20 other events, 219.8 us)
